TPU v7x, 256 devices: a whole 4x4x8 slice. The times are simulated.
256 devices in a mesh: run: 32 (over z, y), rep: 8 (over x, core).
Axes of the slice: x: 4, y: 4, z: 8, core: 2. Of those that a mesh axis runs over, the one named last changes fastest.
Arguments:
- edge_feats: bfloat16 [8, 65536, 1280], P('rep', 'run'), may hold values from -6 to 6
- edge_grads: bfloat16 [8, 65536, 640], P('rep', 'run'), may hold values from -0.059814453 to 0.059814453
- edge_system: int32 [8, 65536], P('rep', 'run'), may hold values from 0 to 5, as said below
- edge_count: int32 [8, 32], P('rep', 'run'), may hold values from 1025 to 2048
- coef: float32 [8, 6, 32], P('rep'), may hold values from 0.05 to 1
- weights: float32 [32, 1280, 640], P('rep', 'run'), may hold values from -0.15625 to 0.15625
- first_moment: float32 [32, 1280, 640], P('rep', 'run'), may hold values from -6 to 6
- second_moment: float32 [32, 1280, 640], P('rep', 'run'), may hold values from 1 to 10
Outputs:
- new_weights: float32 [32, 1280, 640], P('rep', 'run')
- new_first: float32 [32, 1280, 640], P('rep', 'run')
- new_second: float32 [32, 1280, 640], P('rep', 'run')
- merged_next: bfloat16 [8, 6, 1280, 640], P('rep', None, 'run')
Inputs may be any that keep to these rules, and one draw needn't show every extreme that they name: `edge_system`: along each replica's rows the system never falls; every system number appears; the live rows of one device belong to one or two systems, two on some device in every draw.
All inputs are finite; a program needn't handle non-finite values.
Results may differ from a plain program's by a relative error of at most 0.001.
The roundings to bfloat16 on the way count: a program that leaves them out, or rounds other values in their place, can miss the bound.
Values may be sent and summed in bfloat16 or wider, within the bound.
No kernel may reach another device: no remote copies, remote signals or barrier semaphores. Data moves between devices by JAX's collectives and lax.ppermute only.
A program may use at most 128 MiB of HBM per device.

v0:
```python
import jax
import jax.numpy as jnp
from jax import lax
from jax.sharding import PartitionSpec as P


def on_device(
    edge_feats, edge_grads, edge_system, edge_count, coef, weights, first_moment, second_moment
):
    feats = edge_feats[0]
    grads = edge_grads[0]
    system = edge_system[0]
    live_count = edge_count[0, 0]
    group_coef = coef[0]
    nsys = group_coef.shape[0]
    rows = system.shape[0]
    live = jnp.arange(rows) < live_count
    first = system[0]
    last = lax.dynamic_index_in_dim(system, live_count - 1, 0, keepdims=False)
    has_upper = last > first
    empty = jnp.zeros_like(grads)

    def slot_grad(offset):
        keep = live & (system == first + offset)
        right = jnp.where(keep[:, None], grads, empty)
        return lax.dot_general(
            feats, right, (((0,), (0,)), ((), ())), preferred_element_type=jnp.float32
        )

    lower = slot_grad(0)
    upper = lax.cond(has_upper, lambda: slot_grad(1), lambda: jnp.zeros_like(lower))
    picks = jnp.arange(nsys)
    low_hot = (picks == first).astype(jnp.float32)
    high_hot = ((picks == first + 1) & has_upper).astype(jnp.float32)
    term = low_hot[:, None, None] * lower[None] + high_hot[:, None, None] * upper[None]
    owned = lax.psum_scatter(term, "run", scatter_dimension=1, tiled=True)
    mixed = jnp.einsum("se,sio->eio", group_coef, owned, precision=lax.Precision.HIGHEST)
    expert_grad = lax.psum_scatter(mixed, "rep", scatter_dimension=0, tiled=True)
    new_first = 0.9 * first_moment + 0.1 * expert_grad
    new_second = 0.999 * second_moment + 0.001 * expert_grad * expert_grad
    corr_first = 1.0 - 0.9**10
    corr_second = 1.0 - 0.999**10
    new_weights = weights - 0.01 * (new_first / corr_first) / (
        jnp.sqrt(new_second / corr_second) + 1e-08
    )
    rounded = lax.optimization_barrier(new_weights.astype(jnp.bfloat16))
    every_expert = lax.all_gather(rounded, "rep", axis=0, tiled=True)
    experts, din_local, dout = every_expert.shape
    flat = every_expert.astype(jnp.float32).reshape(experts, din_local * dout)
    merged = jnp.dot(group_coef, flat, precision=lax.Precision.HIGHEST)
    merged_next = merged.reshape(nsys, din_local, dout).astype(jnp.bfloat16)
    return (new_weights, new_first, new_second, merged_next[None])


def solution(mesh):
    placed = (
        P("rep", "run", None),
        P("rep", "run", None),
        P("rep", "run"),
        P("rep", "run"),
        P("rep", None, None),
        P("rep", "run", None),
        P("rep", "run", None),
        P("rep", "run", None),
    )
    return jax.shard_map(
        on_device,
        mesh=mesh,
        in_specs=placed,
        out_specs=(
            P("rep", "run", None),
            P("rep", "run", None),
            P("rep", "run", None),
            P("rep", None, "run", None),
        ),
        check_vma=False,
    )
```

profile of v0, /device:TPU:1, one launch (start us, length us, event | category | flops | bytes accessed | tf_op | source)
XLA Modules:
  0.0 412.5 jit_solution(779651478267424646)
XLA Ops:
  7.2 0.0 reduce-scatter.3.cloned.1.call-start
  7.9 1.3 fusion.13
  9.1 1.4 compare_reduce_fusion.1
  12.4 0.7 and_convert_fusion
  13.1 0.2 conditional.1
  13.1 0.2 broadcast.36
  13.4 1.7 copy-done
  15.0 3.5 copy.28
  18.5 8.7 %convolution_bitcast_fusion.1 = f32[1280,640]{0,1:T(8,128)} fusion(bf16[1,2048,640]{2,1,0:T(8,128)(2,1)} %param.11, pred[2048]{0:T(1024)(128)(4,1)S(1)} %fusion.8, bf16[1,2048,1280]{2,1,0:T(8,128)(2,1)} %param.10), kind=kOutput, calls=%fused_computation.9 | convolution fusion | flops 3356753920 | bytes 11143168 | tf_op jit(solution)/shard_map/dot_general | solution.py:26
  27.2 4.6 %copy.27 = f32[1280,640]{1,0:T(8,128)} copy(f32[1280,640]{0,1:T(8,128)} %convolution_bitcast_fusion.1) | data formatting | bytes 6553600 | tf_op jit(solution)/shard_map/dot_general | solution.py:26
  31.8 14.3 %multiply_add_fusion = f32[6,1280,640]{2,0,1:T(8,128)} fusion(f32[1280,640]{1,0:T(8,128)S(1)} %copy.28, f32[6]{0:T(128)S(1)} %get-tuple-element.43, f32[1280,640]{1,0:T(8,128)} %copy.27, f32[6]{0:T(128)S(1)} %get-tuple-element.44), kind=kLoop, calls=%fused_computation.8 | loop fusion | flops 14745600 | bytes 26214448 | tf_op jit(solution)/shard_map/add | solution.py:35
  46.1 0.0 reduce-scatter.3.cloned.1.call-update
  46.2 0.2 reduce-scatter.5.cloned.1.call-start
  46.4 280.4 %reduce-scatter.3.cloned.1.call-done = f32[6,40,640]{2,0,1:T(8,128)} async-done(((f32[6,1280,640]{2,0,1:T(8,128)}), f32[6,40,640]{2,0,1:T(8,128)}) %reduce-scatter.3.cloned.1.call-update) | async-done | bytes 614416 | tf_op jit(solution)/shard_map/reduce_scatter | solution.py:36
  326.8 3.9 convolution_bitcast_fusion.2
  330.8 3.6 copy.29
  334.3 0.0 reduce-scatter.5.cloned.1.call-update
  334.4 0.0 all-gather.2.cloned.1.call-start
  334.4 36.7 %reduce-scatter.5.cloned.1.call-done = f32[4,40,640]{2,1,0:T(8,128)} async-done(((f32[32,40,640]{2,1,0:T(8,128)}), f32[4,40,640]{2,1,0:T(8,128)}) %reduce-scatter.5.cloned.1.call-update) | async-done | bytes 409616 | tf_op jit(solution)/shard_map/reduce_scatter | solution.py:38
  371.1 2.2 fusion.11
  373.4 29.4 %all-gather.2.cloned.1.call-done = bf16[32,40,640]{2,1,0:T(8,128)(2,1)} async-done(((bf16[4,40,640]{2,1,0:T(8,128)(2,1)}), bf16[32,40,640]{2,1,0:T(8,128)(2,1)}) %all-gather.2.cloned.1.call-update) | async-done | bytes 1638416 | tf_op jit(solution)/shard_map/all_gather | solution.py:47
  402.8 1.6 copy.32
  404.4 0.8 convolution_convert_fusion
  405.2 0.8 copy.39
  (12 shorter events, 0.0 us)
Async XLA Ops:
  7.2 319.7 %reduce-scatter.3.cloned.1.call-start = ((), (), s32[]{:S(2)}) async-start(), calls=%async_computation.2 | async-start | bytes 27033600 | tf_op jit(solution)/shard_map/reduce_scatter | solution.py:36
  13.4 1.7 copy-start
  46.1 280.7 %copy-start.4 = (f32[1,6,32]{2,0,1:T(1,128)S(1)}, f32[1,6,32]{2,0,1:T(1,128)}, u32[]{:S(2)}) copy-start(f32[1,6,32]{2,0,1:T(1,128)} %param.14) | copy-start | bytes 2308
  46.2 324.9 %reduce-scatter.5.cloned.1.call-start = ((), (), s32[]{:S(2)}) async-start(), calls=%async_computation.3 | async-start | bytes 3686400 | tf_op jit(solution)/shard_map/reduce_scatter | solution.py:38
  334.3 36.8 %copy-start.1 = (f32[4,40,640]{2,1,0:T(8,128)S(1)}, f32[4,40,640]{2,1,0:T(8,128)}, u32[]{:S(2)}) copy-start(f32[4,40,640]{2,1,0:T(8,128)} %param.15) | copy-start | bytes 1228804
  334.3 36.8 %copy-start.2 = (f32[4,40,640]{2,1,0:T(8,128)S(1)}, f32[4,40,640]{2,1,0:T(8,128)}, u32[]{:S(2)}) copy-start(f32[4,40,640]{2,1,0:T(8,128)} %param.16) | copy-start | bytes 1228804
  334.3 36.8 %copy-start.3 = (f32[4,40,640]{2,1,0:T(8,128)S(1)}, f32[4,40,640]{2,1,0:T(8,128)}, u32[]{:S(2)}) copy-start(f32[4,40,640]{2,1,0:T(8,128)} %param.17) | copy-start | bytes 1228804
  334.4 68.4 %all-gather.2.cloned.1.call-start = ((), (), s32[]{:S(2)}) async-start(), calls=%async_computation.4 | async-start | bytes 1843200 | tf_op jit(solution)/shard_map/all_gather | solution.py:47
Sparse Core Ops, SparseCore 0:
  46.3 280.4 reduce-scatter.2
  334.5 36.5 reduce-scatter.4
  373.7 29.0 all-gather.1
where the time goes:
time: 413 us; the launch traced here: 412 us
  waiting for transfers between devices  347 us (84%)
  other arithmetic  18.6 us (5%)
  local copies, waits for them, and re-layouts  17.2 us (4%)
  between operations  16.4 us (4%)
  matrix products  13.4 us (3%)
    reduce_scatter x1, waiting for transfers between devices, on_device(): owned = lax.psum_scatter(term, 'run', scatter_dimension=1, tiled=True)  280 us
    reduce_scatter x1, waiting for transfers between devices, on_device(): lax.psum_scatter(mixed, 'rep', scatter_dimension=0, tiled=True)  36.7 us
    all_gather x1, waiting for transfers between devices, on_device(): every_expert = lax.all_gather(rounded, 'rep', axis=0, tiled=True)  29.4 us
    add x1, other arithmetic, on_device(): low_hot[:, None, None] * lower[None] + high_hot[:, None, None] * upper[None]  14.3 us
    dot_general x1, matrix products, slot_grad(): lax.dot_general(feats, right, (((0,), (0,)), ((), ())), preferred_element...  8.72 us
  transfers between devices with their start and end apart: 3, of which 3 were waited for; matrix products, arithmetic and copies ran while one was open for 0% of the time, Pallas kernels for 0%

commit v1 on v0

v1 whole, which is shorter than its diff:
```python
import jax
import jax.numpy as jnp
from jax import lax
from jax.experimental import pallas as pl
from jax.experimental.pallas import tpu as pltpu
from jax.sharding import PartitionSpec as P

F32 = jnp.float32
BF16 = jnp.bfloat16
MIB = 1 << 20


def product_kernel(count_ref, system_ref, feats_ref, grads_ref, out_ref, low_acc, high_acc):
    step = pl.program_id(0)
    steps = pl.num_programs(0)
    rows = feats_ref.shape[0]
    owners, per_owner, _ = out_ref.shape
    half = per_owner // 2
    count = count_ref[0, 0]
    first = system_ref[0, 0]

    def halve(_, span):
        lo, hi = span
        mid = (lo + hi) // 2
        same = system_ref[0, jnp.minimum(mid, count - 1)] == first
        inside = lo < hi
        return (
            jnp.where(inside & same, mid + 1, lo),
            jnp.where(inside & jnp.logical_not(same), mid, hi),
        )

    split, _ = lax.fori_loop(0, 12, halve, (jnp.int32(0), count))
    has_upper = split < count
    base = step * rows
    row = base + lax.broadcasted_iota(jnp.int32, (rows, 1), 0)

    def product(begin, end):
        kept = jnp.where((row >= begin) & (row < end), grads_ref[...].astype(F32), 0.0)
        return lax.dot_general(
            feats_ref[...],
            kept.astype(BF16),
            (((0,), (0,)), ((), ())),
            preferred_element_type=F32,
        )

    @pl.when(step == 0)
    def _():
        low_acc[...] = product(0, split)

    @pl.when((step > 0) & (base < split))
    def _():
        low_acc[...] += product(0, split)

    @pl.when(has_upper & (step == 0))
    def _():
        high_acc[...] = jnp.zeros_like(high_acc)

    @pl.when(has_upper & (base + rows > split) & (base < count))
    def _():
        high_acc[...] += product(split, count)

    @pl.when((step == steps - 1) & has_upper)
    def _():
        for owner in range(owners):
            low = low_acc[owner * half : (owner + 1) * half, :]
            high = high_acc[owner * half : (owner + 1) * half, :]
            out_ref[owner] = jnp.concatenate([low, high], axis=0).astype(BF16)

    @pl.when((step == steps - 1) & jnp.logical_not(has_upper))
    def _():
        for owner in range(owners):
            low = low_acc[owner * half : (owner + 1) * half, :]
            out_ref[owner] = jnp.concatenate([low, jnp.zeros_like(low)], axis=0).astype(BF16)


def products(count, system, feats, grads, owners):
    rows, din = feats.shape
    dout = grads.shape[1]
    block = 512
    per_owner = 2 * din // owners
    return pl.pallas_call(
        product_kernel,
        grid=(rows // block,),
        in_specs=[
            pl.BlockSpec(memory_space=pltpu.SMEM),
            pl.BlockSpec(memory_space=pltpu.SMEM),
            pl.BlockSpec((block, din), lambda k: (k, 0)),
            pl.BlockSpec((block, dout), lambda k: (k, 0)),
        ],
        out_specs=pl.BlockSpec((owners, per_owner, dout), lambda k: (0, 0, 0)),
        out_shape=jax.ShapeDtypeStruct((owners, per_owner, dout), BF16),
        scratch_shapes=[pltpu.VMEM((din, dout), F32), pltpu.VMEM((din, dout), F32)],
        compiler_params=pltpu.CompilerParams(vmem_limit_bytes=48 * MIB),
        cost_estimate=pl.CostEstimate(
            flops=2 * rows * din * dout,
            bytes_accessed=2 * rows * (din + dout) + 4 * din * dout,
            transcendentals=0,
        ),
        name="products",
    )(count, system, feats, grads)


def collect_kernel(first_ref, parts_ref, out_ref, total):
    step = pl.program_id(0)
    here = parts_ref.shape[0]
    nsys, half, _ = total.shape

    @pl.when(step == 0)
    def _():
        total[...] = jnp.zeros_like(total)

    for source in range(here):
        low = first_ref[step * here + source]
        high = jnp.minimum(low + 1, nsys - 1)
        part = parts_ref[source].astype(F32)
        total[low] += part[:half]
        total[high] += part[half:]

    @pl.when(step == pl.num_programs(0) - 1)
    def _():
        out_ref[...] = total[...].astype(BF16)


def collect(firsts, parts, nsys):
    sources, both, dout = parts.shape
    half = both // 2
    block = 8
    return pl.pallas_call(
        collect_kernel,
        grid=(sources // block,),
        in_specs=[
            pl.BlockSpec(memory_space=pltpu.SMEM),
            pl.BlockSpec((block, both, dout), lambda k: (k, 0, 0)),
        ],
        out_specs=pl.BlockSpec((nsys, half, dout), lambda k: (0, 0, 0)),
        out_shape=jax.ShapeDtypeStruct((nsys, half, dout), BF16),
        scratch_shapes=[pltpu.VMEM((nsys, half, dout), F32)],
        compiler_params=pltpu.CompilerParams(vmem_limit_bytes=32 * MIB),
        cost_estimate=pl.CostEstimate(
            flops=2 * sources * both * dout,
            bytes_accessed=2 * sources * both * dout,
            transcendentals=0,
        ),
        name="collect",
    )(firsts, parts)


def update_kernel(own_ref, mix_ref, merge_ref, *refs):
    sums = refs[:8]
    weights_ref, first_ref, second_ref = refs[8:11]
    out_weights, out_first, out_second, out_merged = refs[11:15]
    all_weights, all_first, all_second = refs[15:18]
    experts, rows, lanes = weights_ref.shape
    nsys = out_merged.shape[0]
    mine = out_weights.shape[0]
    corr_first = 1.0 - 0.9**10
    corr_second = 1.0 - 0.999**10
    group = 8
    system_sums = jnp.concatenate([ref[...].astype(F32) for ref in sums], axis=0)
    merged = []
    for g in range(rows // group):
        at = slice(g * group, (g + 1) * group)
        right = system_sums[:, at, :].reshape(-1, lanes).astype(BF16)
        both = jnp.dot(mix_ref[...], right, preferred_element_type=F32)
        n = experts * group
        grad = (both[:n] + both[n:]).reshape(experts, group, lanes)
        new_first = 0.9 * first_ref[:, at, :] + 0.1 * grad
        new_second = 0.999 * second_ref[:, at, :] + 0.001 * grad * grad
        new_weights = weights_ref[:, at, :] - 0.01 * (new_first / corr_first) / (
            jnp.sqrt(new_second / corr_second) + 1e-08
        )
        all_weights[:, at, :] = new_weights
        all_first[:, at, :] = new_first
        all_second[:, at, :] = new_second
        rounded = new_weights.reshape(n, lanes).astype(BF16)
        both = jnp.dot(merge_ref[...], rounded, preferred_element_type=F32)
        m = nsys * group
        merged.append((both[:m] + both[m:]).reshape(nsys, group, lanes))
    out_merged[...] = jnp.concatenate(merged, axis=1).astype(BF16)
    own = own_ref[0]
    out_weights[...] = all_weights[pl.ds(own, mine)]
    out_first[...] = all_first[pl.ds(own, mine)]
    out_second[...] = all_second[pl.ds(own, mine)]


def update(own, mix, merge, sums, weights, first_moment, second_moment, mine):
    experts, rows, dout = weights.shape
    nsys = sums[0].shape[0]
    lanes = 128
    whole = lambda k: (0, 0)
    column = lambda k: (0, 0, k)
    state = pl.BlockSpec((experts, rows, lanes), column)
    out_state = pl.BlockSpec((mine, rows, lanes), column)
    return pl.pallas_call(
        update_kernel,
        grid=(dout // lanes,),
        in_specs=[
            pl.BlockSpec(memory_space=pltpu.SMEM),
            pl.BlockSpec(mix.shape, whole),
            pl.BlockSpec(merge.shape, whole),
        ]
        + [pl.BlockSpec((nsys, rows, lanes), column)] * 8
        + [state] * 3,
        out_specs=[out_state] * 3 + [pl.BlockSpec((nsys, rows, lanes), column)],
        out_shape=[jax.ShapeDtypeStruct((mine, rows, dout), F32)] * 3
        + [jax.ShapeDtypeStruct((nsys, rows, dout), BF16)],
        scratch_shapes=[pltpu.VMEM((experts, rows, lanes), F32)] * 3,
        compiler_params=pltpu.CompilerParams(vmem_limit_bytes=48 * MIB),
        name="update",
    )(own, mix, merge, *sums, weights, first_moment, second_moment)


def in_two_parts(matrix):
    high = lax.reduce_precision(matrix, 8, 7)
    return jnp.concatenate([high, matrix - high], axis=0).astype(BF16)


def on_device(
    edge_feats, edge_grads, edge_system, edge_count, coef, weights, first_moment, second_moment
):
    owners = lax.axis_size("run")
    reps = lax.axis_size("rep")
    nsys = coef.shape[1]
    mine = weights.shape[0]
    rep = lax.axis_index("rep")
    firsts = lax.all_gather(edge_system[0, :1], "run", axis=0, tiled=True)
    coefs = lax.all_gather(coef, "rep", axis=0, tiled=True)
    all_weights = lax.all_gather(weights, "rep", axis=0, tiled=True)
    all_first = lax.all_gather(first_moment, "rep", axis=0, tiled=True)
    all_second = lax.all_gather(second_moment, "rep", axis=0, tiled=True)

    chips = reps // 2
    offsets = [(dx, other) for other in (0, 1) for dx in (0, -1, 1, 2)]
    chip, core = rep // 2, rep % 2
    order = jnp.stack(
        [(chip + dx + chips) % chips * 2 + (core + other) % 2 for dx, other in offsets]
    )
    eye = jnp.eye(8, dtype=F32)
    chosen = (order[:, None] == jnp.arange(reps))[:, :, None, None]
    ordered = jnp.sum(jnp.where(chosen, coefs[None], 0.0), axis=1).reshape(reps * nsys, -1)
    mix = in_two_parts(jnp.kron(ordered.T, eye))
    merge = in_two_parts(jnp.kron(coef[0], eye))

    parts = products(edge_count, edge_system, edge_feats[0], edge_grads[0], owners)
    received = lax.all_to_all(parts, "run", 0, 0, tiled=True)
    sums = collect(firsts, received, nsys)

    def from_chip(dx):
        pairs = [((x + dx) % chips * 2 + c, x * 2 + c) for x in range(chips) for c in range(2)]
        return lax.ppermute(sums, "rep", pairs)

    near = [sums] + [from_chip(dx) for dx in (-1, 1, 2)]
    swap = [(i, i ^ 1) for i in range(reps)]
    far = [lax.ppermute(part, "rep", swap) for part in near]
    new_weights, new_first, new_second, merged = update(
        (rep * mine).reshape(1), mix, merge, near + far, all_weights, all_first, all_second, mine
    )
    return (new_weights, new_first, new_second, merged[None])


def solution(mesh):
    placed = (
        P("rep", "run", None),
        P("rep", "run", None),
        P("rep", "run"),
        P("rep", "run"),
        P("rep", None, None),
        P("rep", "run", None),
        P("rep", "run", None),
        P("rep", "run", None),
    )
    return jax.shard_map(
        on_device,
        mesh=mesh,
        in_specs=placed,
        out_specs=(
            P("rep", "run", None),
            P("rep", "run", None),
            P("rep", "run", None),
            P("rep", None, "run", None),
        ),
        check_vma=False,
    )
```

time: 413 us -> 169 us (0.41)
  waiting for transfers between devices: 347 us -> 2.08 us
  blocking collectives: 0 us -> 60.5 us
  starting transfers between devices: 0.3 us -> 35.5 us
  Pallas kernels: 0 us -> 20.6 us
  matrix products: 13.4 us -> 0 us
  other arithmetic: 18.6 us -> 5.23 us
  local copies, waits for them, and re-layouts: 17.2 us -> 27.5 us
    reduce_scatter x2 -> x0, waiting for transfers between devices: 317 us -> none  [the longest x1 280 us: on_device(): owned = lax.psum_scatter(term, 'run', scatter_dimension=1, tiled=True)]
    all_gather x0 -> x2, blocking collectives: none -> 60.5 us  [the longest x1 45.5 us: on_device(): firsts = lax.all_gather(edge_system[0, :1], 'run', axis=0, tiled=True)]
    all_gather x1 -> x3, waiting for transfers between devices: 29.4 us -> 0.01 us  [the longest x1 0.01 us: on_device(): all_weights = lax.all_gather(weights, 'rep', axis=0, tiled=True)]
    ppermute x0 -> x7, starting transfers between devices: none -> 21.9 us  [the longest x4 12.6 us: on_device(): far = [lax.ppermute(part, 'rep', swap) for part in near]]
    pallas_call x0 -> x3, Pallas kernels: none -> 20.6 us  [the longest x1 12.2 us: update(): pl.pallas_call(update_kernel, grid=(dout // lanes,), in_specs=[pl.BlockSp...]
    unnamed x12 -> x48, local copies, waits for them, and re-layouts: 4.08 us -> 18.6 us
    add x1 -> x0, other arithmetic: 14.3 us -> none  [on_device(): low_hot[:, None, None] * lower[None] + high_hot[:, None, None] * upper[None]]
    all_to_all x0 -> x1, starting transfers between devices: none -> 13.5 us  [on_device(): received = lax.all_to_all(parts, 'run', 0, 0, tiled=True)]
  transfers between devices with their start and end apart: 3 -> 11, of which waited for: 3 -> 0; matrix products, arithmetic and copies ran while one was open for 0% -> 10% of each run, Pallas kernels for 0% -> 5%
where the time goes in v1:
time: 169 us; the launch traced here: 166 us
  blocking collectives  60.5 us (36%)
  starting transfers between devices  35.5 us (21%)
  local copies, waits for them, and re-layouts  27.5 us (16%)
  Pallas kernels  20.6 us (12%)
  between operations  14.6 us (9%)
  other arithmetic  5.23 us (3%)
  waiting for transfers between devices  2.08 us (1%)
    all_gather x1, blocking collectives, on_device(): firsts = lax.all_gather(edge_system[0, :1], 'run', axis=0, tiled=True)  45.5 us
    unnamed x48, local copies, waits for them, and re-layouts  18.6 us
    all_gather x1, blocking collectives, on_device(): coefs = lax.all_gather(coef, 'rep', axis=0, tiled=True)  14.9 us
    all_to_all x1, starting transfers between devices, on_device(): received = lax.all_to_all(parts, 'run', 0, 0, tiled=True)  13.5 us
    ppermute x4, starting transfers between devices, on_device(): far = [lax.ppermute(part, 'rep', swap) for part in near]  12.6 us
    pallas_call x1, Pallas kernels, update(): pl.pallas_call(update_kernel, grid=(dout // lanes,), in_specs=[pl.BlockSp...  12.2 us
    ppermute x3, starting transfers between devices, from_chip(): return lax.ppermute(sums, 'rep', pairs)  9.33 us
    pallas_call x1, Pallas kernels, products(): pl.pallas_call(product_kernel, grid=(rows // block,), in_specs=[pl.BlockS...  6.36 us
  transfers between devices with their start and end apart: 11, of which 0 were waited for; matrix products, arithmetic and copies ran while one was open for 10% of the time, Pallas kernels for 5%

profile of v1, /device:TPU:1, one launch (start us, length us, event | category | flops | bytes accessed | tf_op | source)
XLA Modules:
  0.0 166.0 jit_solution(2959443934598671066)
XLA Ops:
  9.3 1.7 %copy-done.17 = bf16[1,2048,640]{2,1,0:T(8,128)(2,1)S(1)} copy-done((bf16[1,2048,640]{2,1,0:T(8,128)(2,1)S(1)}, bf16[1,2048,640]{2,1,0:T(8,128)(2,1)}, u32[]{:S(2)}) %copy-start.17) | copy-done | bytes 2621464
  11.7 6.4 %products.1 = bf16[32,80,640]{2,1,0:T(8,128)(2,1)S(1)} custom-call(s32[1,1]{1,0:T(1,128)S(6)} %copy.25.count_ref, s32[1,2048]{1,0:T(1,128)S(1)} %copy-done.18, bf16[2048,1280]{1,0:T(8,128)(2,1)} %bitcast.26, bf16[2048,640]{1,0:T(8,128)(2,1)S(1)} %bitcast.23), custom_call_target="tpu_custom_call" | custom-call | flops 3355443200 | bytes 11141120 | tf_op jit(solution)/shard_map/products/pallas_call | solution.py:81
  18.1 1.7 %copy-done.1 = bf16[32,80,640]{2,1,0:T(8,128)(2,1)} copy-done((bf16[32,80,640]{2,1,0:T(8,128)(2,1)}, bf16[32,80,640]{2,1,0:T(8,128)(2,1)S(1)}, u32[]{:S(2)}) %copy-start.1) | copy-done | bytes 3276824
  19.8 13.5 %all-to-all-start = ((bf16[32,80,640]{2,1,0:T(8,128)(2,1)}), bf16[32,80,640]{2,1,0:T(8,128)(2,1)S(1)}, u32[]{:S(2)}, u32[]{:S(2)}) async-start(bf16[32,80,640]{2,1,0:T(8,128)(2,1)} %copy-done.1), calls=%async_computation | async-start | bytes 6553600 | tf_op jit(solution)/shard_map/all_to_all | solution.py:245
  34.1 1.2 slice.3
  35.4 14.9 %all_gather.15 = f32[8,6,32]{2,1,0:T(8,128)S(1)} all-gather(f32[1,6,32]{2,1,0:T(8,128)S(1)} %copy.23), channel_id=1, replica_groups=mesh['run'=32,'rep'=8] {'rep'}, dimensions={0}, use_global_device_ids=true | all-gather | bytes 6912 | tf_op jit(solution)/shard_map/all_gather | solution.py:227
  50.7 3.1 %broadcast_multiply_fusion = f32[32,8,48,8]{3,2,1,0:T(8,128)} fusion(f32[8,8]{1,0:T(8,128)S(1)} %fusion.2, f32[32,48]{1,0:T(8,128)S(1)} %copy.19), kind=kLoop, calls=%fused_computation | loop fusion | flops 98304 | bytes 399616 | tf_op jit(solution)/shard_map/jit(kron)/mul | solution.py:241
  53.8 6.0 %mul.77 = f32[256,384]{1,0:T(8,128)} reshape(f32[32,8,48,8]{3,2,1,0:T(8,128)} %broadcast_multiply_fusion) | data formatting | bytes 786432 | tf_op jit(solution)/shard_map/jit(kron)/mul | solution.py:241
  59.8 1.0 broadcast_multiply_fusion.1
  60.8 1.5 mul.82
  63.0 1.4 bitcast_dynamic-update-slice_fusion
  64.3 45.5 %all-reduce.first_ref = s32[32]{0:T(128)S(1)} all-reduce(s32[32]{0:T(128)S(1)} %bitcast_dynamic-update-slice_fusion), channel_id=2, replica_groups=mesh['run'=32,'rep'=8] {'run'}, use_global_device_ids=true, to_apply=%add | all-reduce | flops 32 | bytes 256 | tf_op jit(solution)/shard_map/all_gather | solution.py:226
  109.9 2.1 %collect.1.refs_0_ = bf16[6,40,640]{2,1,0:T(8,128)(2,1)} custom-call(s32[32]{0:T(128)S(1)} %all-reduce.first_ref, bf16[32,80,640]{2,1,0:T(8,128)(2,1)S(1)} %all-to-all-done.parts_ref), custom_call_target="tpu_custom_call" | custom-call | flops 3276800 | bytes 3276800 | tf_op jit(solution)/shard_map/collect/pallas_call | solution.py:128
  111.9 7.5 %collective-permute-start = (bf16[6,40,640]{2,1,0:T(8,128)(2,1)}, bf16[6,40,640]{2,1,0:T(8,128)(2,1)S(1)}, u32[]{:S(2)}, u32[]{:S(2)}) collective-permute-start(bf16[6,40,640]{2,1,0:T(8,128)(2,1)} %collect.1.refs_0_), channel_id=1, source_target_pairs={{6,0},{7,1},{0,2},{1,3},{2,4},{3,5},{4,6},{5,7},{14,8},{15,9},{8,1... | collective-permute-start | bytes 921608 | tf_op jit(solution)/shard_map/ppermute | solution.py:250
  119.5 1.8 %collective-permute-start.2 = (bf16[6,40,640]{2,1,0:T(8,128)(2,1)}, bf16[6,40,640]{2,1,0:T(8,128)(2,1)S(1)}, u32[]{:S(2)}, u32[]{:S(2)}) collective-permute-start(bf16[6,40,640]{2,1,0:T(8,128)(2,1)} %collect.1.refs_0_), channel_id=1, source_target_pairs={{4,0},{5,1},{6,2},{7,3},{0,4},{1,5},{2,6},{3,7},{12,8},{13,9},{14,... | collective-permute-start | bytes 921608 | tf_op jit(solution)/shard_map/ppermute | solution.py:250
  121.3 3.2 %collective-permute-start.3 = (bf16[6,40,640]{2,1,0:T(8,128)(2,1)}, bf16[6,40,640]{2,1,0:T(8,128)(2,1)S(1)}, u32[]{:S(2)}, u32[]{:S(2)}) collective-permute-start(bf16[6,40,640]{2,1,0:T(8,128)(2,1)} %collect.1.refs_0_), channel_id=1, source_target_pairs={{0,1},{1,0},{2,3},{3,2},{4,5},{5,4},{6,7},{7,6},{8,9},{9,8},{10,11... | collective-permute-start | bytes 921608 | tf_op jit(solution)/shard_map/ppermute | solution.py:254
  124.5 5.7 %collective-permute-start.4 = (bf16[6,40,640]{2,1,0:T(8,128)(2,1)S(1)}, bf16[6,40,640]{2,1,0:T(8,128)(2,1)S(1)}, u32[]{:S(2)}, u32[]{:S(2)}) collective-permute-start(bf16[6,40,640]{2,1,0:T(8,128)(2,1)S(1)} %collective-permute-done.refs_1_), channel_id=1, source_target_pairs={{0,1},{1,0},{2,3},{3,2},{4,5},{5,4},{6,7},{7,6},{8,9},{9,8},{10,11... | collective-permute-start | bytes 921608 | tf_op jit(solution)/shard_map/ppermute | solution.py:254
  130.2 2.4 %collective-permute-start.5 = (bf16[6,40,640]{2,1,0:T(8,128)(2,1)S(1)}, bf16[6,40,640]{2,1,0:T(8,128)(2,1)S(1)}, u32[]{:S(2)}, u32[]{:S(2)}) collective-permute-start(bf16[6,40,640]{2,1,0:T(8,128)(2,1)S(1)} %collective-permute-done.1.refs_2_), channel_id=1, source_target_pairs={{0,1},{1,0},{2,3},{3,2},{4,5},{5,4},{6,7},{7,6},{8,9},{9,8},{10,11... | collective-permute-start | bytes 921608 | tf_op jit(solution)/shard_map/ppermute | solution.py:254
  132.5 1.3 collective-permute-start.6
  137.6 1.9 %copy-done = f32[32,40,640]{2,1,0:T(8,128)S(1)} copy-done((f32[32,40,640]{2,1,0:T(8,128)S(1)}, f32[32,40,640]{2,1,0:T(8,128)}, u32[]{:S(2)}) %copy-start) | copy-done | bytes 3276824
  139.5 1.0 copy-done.2
  140.5 1.0 copy-done.4
  142.5 1.0 copy-done.8
  147.3 12.2 %update.1 = (f32[4,40,640]{2,1,0:T(8,128)}, f32[4,40,640]{2,1,0:T(8,128)}, f32[4,40,640]{2,1,0:T(8,128)}, bf16[6,40,640]{2,1,0:T(8,128)(2,1)}) custom-call(s32[1]{0:T(128)} %bitcast.own_ref, bf16[512,384]{1,0:T(8,128)(2,1)S(1)} %copy-done.2, bf16[96,256]{1,0:T(8,128)(2,1)S(1)} %pad_maximum_fusion.1.merge_ref, bf16[6,40,640]{2,1,0:T(8,128)(2,1)} %collect.1.refs_0_, ...), custom_call_target="tpu_custom_call" | custom-call | tf_op jit(solution)/shard_map/update/pallas_call | solution.py:194
  (70 shorter events, 12.4 us)
Async XLA Ops:
  7.2 127.5 %all-gather.5.cloned.1.call-start = ((), (), s32[]{:S(2)}) async-start(), calls=%async_computation.1 | async-start | bytes 3686400 | tf_op jit(solution)/shard_map/all_gather | solution.py:228
  7.9 126.8 %all-gather.7.cloned.1.call-start = ((), (), s32[]{:S(2)}) async-start(), calls=%async_computation.2 | async-start | bytes 3686400 | tf_op jit(solution)/shard_map/all_gather | solution.py:229
  9.3 1.7 %copy-start.17 = (bf16[1,2048,640]{2,1,0:T(8,128)(2,1)S(1)}, bf16[1,2048,640]{2,1,0:T(8,128)(2,1)}, u32[]{:S(2)}) copy-start(bf16[1,2048,640]{2,1,0:T(8,128)(2,1)} %param.9) | copy-start | bytes 7864324
  18.1 1.7 %copy-start.1 = (bf16[32,80,640]{2,1,0:T(8,128)(2,1)}, bf16[32,80,640]{2,1,0:T(8,128)(2,1)S(1)}, u32[]{:S(2)}) copy-start(bf16[32,80,640]{2,1,0:T(8,128)(2,1)S(1)} %products.1) | copy-start | bytes 9830404
  19.8 15.6 %copy-start.20 = (f32[1,6,32]{2,0,1:T(1,128)S(1)}, f32[1,6,32]{2,0,1:T(1,128)}, u32[]{:S(2)}) copy-start(f32[1,6,32]{2,0,1:T(1,128)} %param.12) | copy-start | bytes 2308
  19.8 90.1 %all-to-all-start = ((bf16[32,80,640]{2,1,0:T(8,128)(2,1)}), bf16[32,80,640]{2,1,0:T(8,128)(2,1)S(1)}, u32[]{:S(2)}, u32[]{:S(2)}) async-start(bf16[32,80,640]{2,1,0:T(8,128)(2,1)} %copy-done.1), calls=%async_computation | async-start | bytes 6553600 | tf_op jit(solution)/shard_map/all_to_all | solution.py:245
  33.3 101.4 %all-gather.9.cloned.1.call-start = ((), (), s32[]{:S(2)}) async-start(), calls=%async_computation.3 | async-start | bytes 3686400 | tf_op jit(solution)/shard_map/all_gather | solution.py:230
  53.8 8.6 %copy-start.21 = (u32[256]{0:T(256)S(1)}, u32[256]{0:T(256)}, u32[]{:S(2)}) copy-start(u32[256]{0:T(256)} %constant.97) | copy-start | bytes 3076
  109.9 24.0 %copy-start.19 = (f32[256,384]{1,0:T(8,128)S(1)}, f32[256,384]{1,0:T(8,128)}, u32[]{:S(2)}) copy-start(f32[256,384]{1,0:T(8,128)} %mul.77) | copy-start | bytes 1179652
  111.9 12.6 %collective-permute-start = (bf16[6,40,640]{2,1,0:T(8,128)(2,1)}, bf16[6,40,640]{2,1,0:T(8,128)(2,1)S(1)}, u32[]{:S(2)}, u32[]{:S(2)}) collective-permute-start(bf16[6,40,640]{2,1,0:T(8,128)(2,1)} %collect.1.refs_0_), channel_id=1, source_target_pairs={{6,0},{7,1},{0,2},{1,3},{2,4},{3,5},{4,6},{5,7},{14,8},{15,9},{8,1... | collective-permute-start | bytes 921608 | tf_op jit(solution)/shard_map/ppermute | solution.py:250
  119.5 10.7 %collective-permute-start.1 = (bf16[6,40,640]{2,1,0:T(8,128)(2,1)}, bf16[6,40,640]{2,1,0:T(8,128)(2,1)S(1)}, u32[]{:S(2)}, u32[]{:S(2)}) collective-permute-start(bf16[6,40,640]{2,1,0:T(8,128)(2,1)} %collect.1.refs_0_), channel_id=1, source_target_pairs={{2,0},{3,1},{4,2},{5,3},{6,4},{7,5},{0,6},{1,7},{10,8},{11,9},{12,... | collective-permute-start | bytes 921608 | tf_op jit(solution)/shard_map/ppermute | solution.py:250
  119.5 13.1 %collective-permute-start.2 = (bf16[6,40,640]{2,1,0:T(8,128)(2,1)}, bf16[6,40,640]{2,1,0:T(8,128)(2,1)S(1)}, u32[]{:S(2)}, u32[]{:S(2)}) collective-permute-start(bf16[6,40,640]{2,1,0:T(8,128)(2,1)} %collect.1.refs_0_), channel_id=1, source_target_pairs={{4,0},{5,1},{6,2},{7,3},{0,4},{1,5},{2,6},{3,7},{12,8},{13,9},{14,... | collective-permute-start | bytes 921608 | tf_op jit(solution)/shard_map/ppermute | solution.py:250
  121.3 13.4 %collective-permute-start.3 = (bf16[6,40,640]{2,1,0:T(8,128)(2,1)}, bf16[6,40,640]{2,1,0:T(8,128)(2,1)S(1)}, u32[]{:S(2)}, u32[]{:S(2)}) collective-permute-start(bf16[6,40,640]{2,1,0:T(8,128)(2,1)} %collect.1.refs_0_), channel_id=1, source_target_pairs={{0,1},{1,0},{2,3},{3,2},{4,5},{5,4},{6,7},{7,6},{8,9},{9,8},{10,11... | collective-permute-start | bytes 921608 | tf_op jit(solution)/shard_map/ppermute | solution.py:254
  124.5 12.4 %copy-start.3 = (bf16[6,40,640]{2,1,0:T(8,128)(2,1)}, bf16[6,40,640]{2,1,0:T(8,128)(2,1)S(1)}, u32[]{:S(2)}) copy-start(bf16[6,40,640]{2,1,0:T(8,128)(2,1)S(1)} %collective-permute-done.refs_1_) | copy-start | bytes 921604
  124.5 10.9 %collective-permute-start.4 = (bf16[6,40,640]{2,1,0:T(8,128)(2,1)S(1)}, bf16[6,40,640]{2,1,0:T(8,128)(2,1)S(1)}, u32[]{:S(2)}, u32[]{:S(2)}) collective-permute-start(bf16[6,40,640]{2,1,0:T(8,128)(2,1)S(1)} %collective-permute-done.refs_1_), channel_id=1, source_target_pairs={{0,1},{1,0},{2,3},{3,2},{4,5},{5,4},{6,7},{7,6},{8,9},{9,8},{10,11... | collective-permute-start | bytes 921608 | tf_op jit(solution)/shard_map/ppermute | solution.py:254
  130.2 6.7 %copy-start.5 = (bf16[6,40,640]{2,1,0:T(8,128)(2,1)}, bf16[6,40,640]{2,1,0:T(8,128)(2,1)S(1)}, u32[]{:S(2)}) copy-start(bf16[6,40,640]{2,1,0:T(8,128)(2,1)S(1)} %collective-permute-done.1.refs_2_) | copy-start | bytes 921604
  130.2 6.0 %collective-permute-start.5 = (bf16[6,40,640]{2,1,0:T(8,128)(2,1)S(1)}, bf16[6,40,640]{2,1,0:T(8,128)(2,1)S(1)}, u32[]{:S(2)}, u32[]{:S(2)}) collective-permute-start(bf16[6,40,640]{2,1,0:T(8,128)(2,1)S(1)} %collective-permute-done.1.refs_2_), channel_id=1, source_target_pairs={{0,1},{1,0},{2,3},{3,2},{4,5},{5,4},{6,7},{7,6},{8,9},{9,8},{10,11... | collective-permute-start | bytes 921608 | tf_op jit(solution)/shard_map/ppermute | solution.py:254
  132.5 4.3 %copy-start.7 = (bf16[6,40,640]{2,1,0:T(8,128)(2,1)}, bf16[6,40,640]{2,1,0:T(8,128)(2,1)S(1)}, u32[]{:S(2)}) copy-start(bf16[6,40,640]{2,1,0:T(8,128)(2,1)S(1)} %collective-permute-done.2.refs_3_) | copy-start | bytes 921604
  132.5 4.3 %collective-permute-start.6 = (bf16[6,40,640]{2,1,0:T(8,128)(2,1)S(1)}, bf16[6,40,640]{2,1,0:T(8,128)(2,1)S(1)}, u32[]{:S(2)}, u32[]{:S(2)}) collective-permute-start(bf16[6,40,640]{2,1,0:T(8,128)(2,1)S(1)} %collective-permute-done.2.refs_3_), channel_id=1, source_target_pairs={{0,1},{1,0},{2,3},{3,2},{4,5},{5,4},{6,7},{7,6},{8,9},{9,8},{10,11... | collective-permute-start | bytes 921608 | tf_op jit(solution)/shard_map/ppermute | solution.py:254
  137.6 1.9 %copy-start = (f32[32,40,640]{2,1,0:T(8,128)S(1)}, f32[32,40,640]{2,1,0:T(8,128)}, u32[]{:S(2)}) copy-start(f32[32,40,640]{2,1,0:T(8,128)} %all-gather.5.cloned.1.call-done.refs_8_) | copy-start | bytes 9830404
  139.5 1.0 copy-start.2
  141.5 1.0 copy-start.6
  142.5 1.0 copy-start.8
  146.3 1.0 copy-start.16
  (9 other events, 7.4 us)
Sparse Core Ops, SparseCore 0:
  9.8 35.0 all-gather.4
  46.8 30.7 all-gather.6
  79.4 30.7 all-gather.8

commit v2 on v1

v2 whole, which is shorter than its diff:
```python
import jax
import jax.numpy as jnp
from jax import lax
from jax.experimental import pallas as pl
from jax.experimental.pallas import tpu as pltpu
from jax.sharding import PartitionSpec as P

F32 = jnp.float32
BF16 = jnp.bfloat16
I16 = jnp.int16
MIB = 1 << 20
LANES = 128
NOTE = 16


def exponent(largest):
    return jnp.ceil(jnp.log2(jnp.maximum(largest, 1e-30) * (1.0 / 32700.0)))


def coded(values):
    return jnp.round(values).astype(jnp.int32).astype(I16)


def plain(codes):
    return codes.astype(jnp.int32).astype(F32)


def product_kernel(count_ref, system_ref, feats_ref, grads_ref, out_ref, low_acc, high_acc):
    step = pl.program_id(0)
    steps = pl.num_programs(0)
    rows = feats_ref.shape[0]
    owners = out_ref.shape[0]
    half = low_acc.shape[0] // owners
    blocks = low_acc.shape[1] // LANES
    count = count_ref[0, 0]
    first = system_ref[0, 0]

    def halve(_, span):
        lo, hi = span
        mid = (lo + hi) // 2
        same = system_ref[0, jnp.minimum(mid, count - 1)] == first
        inside = lo < hi
        return (
            jnp.where(inside & same, mid + 1, lo),
            jnp.where(inside & jnp.logical_not(same), mid, hi),
        )

    split, _ = lax.fori_loop(0, 12, halve, (jnp.int32(0), count))
    has_upper = split < count
    base = step * rows
    row = base + lax.broadcasted_iota(jnp.int32, (rows, 1), 0)

    def product(begin, end):
        kept = jnp.where((row >= begin) & (row < end), grads_ref[...].astype(F32), 0.0)
        return lax.dot_general(
            feats_ref[...],
            kept.astype(BF16),
            (((0,), (0,)), ((), ())),
            preferred_element_type=F32,
        )

    @pl.when(step == 0)
    def _():
        low_acc[...] = product(0, split)

    @pl.when((step > 0) & (base < split))
    def _():
        low_acc[...] += product(0, split)

    @pl.when(has_upper & (step == 0))
    def _():
        high_acc[...] = jnp.zeros_like(high_acc)

    @pl.when(has_upper & (base + rows > split) & (base < count))
    def _():
        high_acc[...] += product(split, count)

    def hand_out(low_e, high_e):
        row = lax.broadcasted_iota(jnp.int32, (NOTE, LANES), 0)
        note = jnp.where(row == 0, first.astype(F32), jnp.where(row == 1, low_e, high_e))
        note = coded(note)
        low_by = jnp.exp2(-low_e)
        high_by = None if isinstance(high_e, float) else jnp.exp2(-high_e)
        for owner in range(owners):
            at = slice(owner * half, (owner + 1) * half)
            for block in range(blocks):
                lanes = slice(block * LANES, (block + 1) * LANES)
                low = low_acc[at, lanes] * low_by
                high = jnp.zeros_like(low) if high_by is None else high_acc[at, lanes] * high_by
                to = slice(block * 2 * half, (block + 1) * 2 * half)
                out_ref[owner, to, :] = coded(jnp.concatenate([low, high], axis=0))
            out_ref[owner, blocks * 2 * half :, :] = note

    def largest(ref):
        return jnp.max(jnp.abs(ref[...]), axis=(0, 1), keepdims=True)

    @pl.when((step == steps - 1) & has_upper)
    def _():
        hand_out(exponent(largest(low_acc)), exponent(largest(high_acc)))

    @pl.when((step == steps - 1) & jnp.logical_not(has_upper))
    def _():
        hand_out(exponent(largest(low_acc)), 0.0)


def products(count, system, feats, grads, owners):
    rows, din = feats.shape
    dout = grads.shape[1]
    block = 512
    per_owner = 2 * din // owners * (dout // LANES) + NOTE
    return pl.pallas_call(
        product_kernel,
        grid=(rows // block,),
        in_specs=[
            pl.BlockSpec(memory_space=pltpu.SMEM),
            pl.BlockSpec(memory_space=pltpu.SMEM),
            pl.BlockSpec((block, din), lambda k: (k, 0)),
            pl.BlockSpec((block, dout), lambda k: (k, 0)),
        ],
        out_specs=pl.BlockSpec((owners, per_owner, LANES), lambda k: (0, 0, 0)),
        out_shape=jax.ShapeDtypeStruct((owners, per_owner, LANES), I16),
        scratch_shapes=[pltpu.VMEM((din, dout), F32), pltpu.VMEM((din, dout), F32)],
        compiler_params=pltpu.CompilerParams(vmem_limit_bytes=62 * MIB),
        cost_estimate=pl.CostEstimate(
            flops=2 * rows * din * dout,
            bytes_accessed=2 * rows * (din + dout) + 4 * din * dout,
            transcendentals=0,
        ),
        name="products",
    )(count, system, feats, grads)


def collect_kernel(parts_ref, out_ref, total):
    step = pl.program_id(0)
    nsys, half, dout = total.shape
    blocks = dout // LANES

    @pl.when(step == 0)
    def _():
        total[...] = jnp.zeros_like(total)

    for source in range(parts_ref.shape[0]):
        note = plain(parts_ref[source, blocks * 2 * half :, :])
        low = jnp.max(note[0:1]).astype(jnp.int32)
        high = jnp.minimum(low + 1, nsys - 1)
        low_by, high_by = jnp.exp2(note[1:2]), jnp.exp2(note[2:3])
        for block in range(blocks):
            lanes = slice(block * LANES, (block + 1) * LANES)
            part = plain(parts_ref[source, block * 2 * half : (block + 1) * 2 * half, :])
            total[low, :, lanes] += part[:half] * low_by
            total[high, :, lanes] += part[half:] * high_by

    @pl.when(step == pl.num_programs(0) - 1)
    def _():
        row = lax.broadcasted_iota(jnp.int32, (NOTE, dout), 0)
        note = jnp.zeros((NOTE, dout), F32)
        scaled = []
        for system in range(nsys):
            values = total[system]
            e = exponent(jnp.max(jnp.abs(values), axis=(0, 1), keepdims=True))
            note = jnp.where(row == system, e, note)
            scaled.append(values * jnp.exp2(-e))
        out_ref[...] = coded(jnp.concatenate(scaled + [note], axis=0))


def collect(parts, nsys, half, dout):
    sources = parts.shape[0]
    block = 8
    out = (nsys * half + NOTE, dout)
    return pl.pallas_call(
        collect_kernel,
        grid=(sources // block,),
        in_specs=[pl.BlockSpec((block,) + parts.shape[1:], lambda k: (k, 0, 0))],
        out_specs=pl.BlockSpec(out, lambda k: (0, 0)),
        out_shape=jax.ShapeDtypeStruct(out, I16),
        scratch_shapes=[pltpu.VMEM((nsys, half, dout), F32)],
        compiler_params=pltpu.CompilerParams(vmem_limit_bytes=12 * MIB),
        cost_estimate=pl.CostEstimate(
            flops=2 * parts.size, bytes_accessed=2 * parts.size, transcendentals=0
        ),
        name="collect",
    )(parts)


def update_kernel(mix_ref, merge_ref, *refs):
    sums = refs[:8]
    states = refs[8:16]
    out_weights, out_first, out_second, out_merged = refs[16:20]
    system_sums, merged = refs[20:22]
    step = pl.program_id(0)
    mine, group, lanes = out_weights.shape
    nsys, rows, _ = merged.shape
    n = group * mine * len(states)
    m = group * nsys
    corr_first = 1.0 - 0.9**10
    corr_second = 1.0 - 0.999**10

    @pl.when(step == 0)
    def _():
        for rep, ref in enumerate(sums):
            note = plain(ref[nsys * rows :, :])
            values = plain(ref[: nsys * rows, :])
            for system in range(nsys):
                by = jnp.exp2(note[system : system + 1])
                system_sums[rep * nsys + system] = values[system * rows : (system + 1) * rows] * by

    def of_experts(kind):
        return jnp.concatenate([ref[kind * mine : (kind + 1) * mine] for ref in states], axis=0)

    at = pl.ds(pl.multiple_of(step * group, group), group)
    right = system_sums[:, at, :].reshape(-1, lanes)
    near = right.astype(BF16)
    rest = (right - near.astype(F32)).astype(BF16)
    both = jnp.dot(mix_ref[...], near, preferred_element_type=F32)
    more = jnp.dot(mix_ref[:n, :], rest, preferred_element_type=F32)
    grad = (both[:n] + (both[n:] + more)).reshape(-1, group, lanes)
    new_first = 0.9 * of_experts(1) + 0.1 * grad
    new_second = 0.999 * of_experts(2) + 0.001 * grad * grad
    new_weights = of_experts(0) - 0.01 * (new_first / corr_first) / (
        jnp.sqrt(new_second / corr_second) + 1e-08
    )
    out_weights[...] = new_weights[:mine]
    out_first[...] = new_first[:mine]
    out_second[...] = new_second[:mine]
    rounded = new_weights.reshape(n, lanes).astype(BF16)
    both = jnp.dot(merge_ref[...], rounded, preferred_element_type=F32)
    merged[:, at, :] = (both[:m] + both[m:]).reshape(nsys, group, lanes)

    @pl.when(step == pl.num_programs(0) - 1)
    def _():
        out_merged[...] = merged[...].astype(BF16)


def update(mix, merge, sums, states, nsys):
    mine, rows, dout = states[0].shape
    mine = mine // 3
    group = 8
    whole = lambda g: (0, 0)
    some = lambda g: (0, g, 0)
    return pl.pallas_call(
        update_kernel,
        grid=(rows // group,),
        in_specs=[pl.BlockSpec(a.shape, whole) for a in [mix, merge] + sums]
        + [pl.BlockSpec((3 * mine, group, dout), some)] * 8,
        out_specs=[pl.BlockSpec((mine, group, dout), some)] * 3
        + [pl.BlockSpec((nsys, rows, dout), lambda g: (0, 0, 0))],
        out_shape=[jax.ShapeDtypeStruct((mine, rows, dout), F32)] * 3
        + [jax.ShapeDtypeStruct((nsys, rows, dout), BF16)],
        scratch_shapes=[
            pltpu.VMEM((8 * nsys, rows, dout), F32),
            pltpu.VMEM((nsys, rows, dout), F32),
        ],
        compiler_params=pltpu.CompilerParams(vmem_limit_bytes=32 * MIB),
        name="update",
    )(mix, merge, *sums, *states)


def in_two_parts(matrix):
    high = lax.reduce_precision(matrix, 8, 7)
    return jnp.concatenate([high, matrix - high], axis=0).astype(BF16)


def everywhere(value, axis, moves):
    return [lax.ppermute(value, axis, pairs) for pairs in moves]


def on_device(
    edge_feats, edge_grads, edge_system, edge_count, coef, weights, first_moment, second_moment
):
    owners = lax.axis_size("run")
    reps = lax.axis_size("rep")
    nsys = coef.shape[1]

    chips = reps // 2
    along_x = [
        [((x + dx) % chips * 2 + c, x * 2 + c) for x in range(chips) for c in range(2)]
        for dx in range(1, chips)
    ]
    swap = [(i, i ^ 1) for i in range(reps)]

    def all_reps(value):
        near = [value] + everywhere(value, "rep", along_x)
        return near + [lax.ppermute(part, "rep", swap) for part in near]

    coefs = jnp.stack(all_reps(coef[0]))
    states = all_reps(jnp.concatenate([weights, first_moment, second_moment], axis=0))

    rep = lax.axis_index("rep")
    chip, core = rep // 2, rep % 2
    order = jnp.stack(
        [(chip + dx) % chips * 2 + (core + other) % 2 for other in (0, 1) for dx in range(chips)]
    )
    chosen = (order[:, None] == jnp.arange(reps))[:, :, None]
    by_owner = coefs.reshape(reps * nsys, 1, reps, -1)
    ordered = jnp.sum(jnp.where(chosen, by_owner, 0.0), axis=2).reshape(reps * nsys, -1)
    eye = jnp.eye(8, dtype=F32)
    mix = in_two_parts(jnp.kron(ordered.T, eye))
    merge = in_two_parts(jnp.kron(ordered[:nsys], eye))

    parts = products(edge_count, edge_system, edge_feats[0], edge_grads[0], owners)
    received = lax.all_to_all(parts, "run", 0, 0, tiled=True)
    sums = all_reps(collect(received, nsys, weights.shape[1], weights.shape[2]))
    new_weights, new_first, new_second, merged = update(mix, merge, sums, states, nsys)
    return (new_weights, new_first, new_second, merged[None])


def solution(mesh):
    placed = (
        P("rep", "run", None),
        P("rep", "run", None),
        P("rep", "run"),
        P("rep", "run"),
        P("rep", None, None),
        P("rep", "run", None),
        P("rep", "run", None),
        P("rep", "run", None),
    )
    return jax.shard_map(
        on_device,
        mesh=mesh,
        in_specs=placed,
        out_specs=(
            P("rep", "run", None),
            P("rep", "run", None),
            P("rep", "run", None),
            P("rep", None, "run", None),
        ),
        check_vma=False,
    )
```

time: 169 us -> 154 us (0.911); the launches traced: 166 us -> 155 us
  blocking collectives: 60.5 us -> 0 us
  waiting for transfers between devices: 2.08 us -> 43.4 us
  starting transfers between devices: 35.5 us -> 67.8 us
  local copies, waits for them, and re-layouts: 27.5 us -> 13.7 us
  between operations: 14.6 us -> 1.64 us
  other arithmetic: 5.23 us -> 6.99 us
    all_gather x2 -> x0, blocking collectives: 60.5 us -> none  [the longest x1 45.5 us: on_device(): firsts = lax.all_gather(edge_system[0, :1], 'run', axis=0, tiled=True)]
    ppermute x7 -> x21, waiting for transfers between devices: 0.02 us -> 43.4 us  [the longest x9 39.6 us: everywhere(): return [lax.ppermute(value, axis, pairs) for pairs in moves]]
    ppermute x7 -> x21, starting transfers between devices: 21.9 us -> 54.4 us  [the longest x12 41.4 us: all_reps(): return near + [lax.ppermute(part, 'rep', swap) for part in near]]
    unnamed x48 -> x11, local copies, waits for them, and re-layouts: 18.6 us -> 3.65 us
    pallas_call x1, Pallas kernels: 6.36 us -> 8.78 us  [products(): pl.pallas_call(product_kernel, grid=(rows // block,), in_specs=[pl.BlockS...]
    unnamed x3 -> x0, waiting for transfers between devices: 2.06 us -> none
    pallas_call x1, Pallas kernels: 12.2 us -> 10.4 us  [update(): pl.pallas_call(update_kernel, grid=(rows // group,), in_specs=[pl.BlockSp...]
  transfers between devices with their start and end apart: 11 -> 22, of which waited for: 0 -> 10; matrix products, arithmetic and copies ran while one was open for 10% -> 13% of each run, Pallas kernels for 5% -> 2%
where the time goes in v2:
time: 154 us; the launch traced here: 155 us
  starting transfers between devices  67.8 us (44%)
  waiting for transfers between devices  43.4 us (28%)
  Pallas kernels  21.7 us (14%)
  local copies, waits for them, and re-layouts  13.7 us (9%)
  other arithmetic  6.99 us (5%)
  between operations  1.64 us (1%)
    ppermute x12, starting transfers between devices, all_reps(): return near + [lax.ppermute(part, 'rep', swap) for part in near]  41.4 us
    ppermute x9, waiting for transfers between devices, everywhere(): return [lax.ppermute(value, axis, pairs) for pairs in moves]  39.6 us
    all_to_all x1, starting transfers between devices, on_device(): received = lax.all_to_all(parts, 'run', 0, 0, tiled=True)  13.4 us
    ppermute x9, starting transfers between devices, everywhere(): return [lax.ppermute(value, axis, pairs) for pairs in moves]  13 us
    pallas_call x1, Pallas kernels, update(): pl.pallas_call(update_kernel, grid=(rows // group,), in_specs=[pl.BlockSp...  10.4 us
    pallas_call x1, Pallas kernels, products(): pl.pallas_call(product_kernel, grid=(rows // block,), in_specs=[pl.BlockS...  8.78 us
    mul x1, local copies, waits for them, and re-layouts, on_device(): mix = in_two_parts(jnp.kron(ordered.T, eye))  5.9 us
    mul x1, other arithmetic, on_device(): mix = in_two_parts(jnp.kron(ordered.T, eye))  3.81 us
  transfers between devices with their start and end apart: 22, of which 10 were waited for; matrix products, arithmetic and copies ran while one was open for 13% of the time, Pallas kernels for 2%

profile of v2, /device:TPU:1, one launch (start us, length us, event | category | flops | bytes accessed | tf_op | source)
XLA Modules:
  0.0 155.3 jit_solution(17756499102340924379)
XLA Ops:
  1.3 8.8 %products.1 = s16[32,416,128]{2,1,0:T(8,128)(2,1)} custom-call(s32[1,1]{1,0:T(1,128)S(6)} %copy.52.count_ref, s32[1,2048]{1,0:T(1,128)} %system_ref.1, bf16[2048,1280]{1,0:T(8,128)(2,1)} %bitcast.43, bf16[2048,640]{1,0:T(8,128)(2,1)} %bitcast.44), custom_call_target="tpu_custom_call" | custom-call | flops 3355443200 | bytes 11141120 | tf_op jit(solution)/shard_map/products/pallas_call | solution.py:111
  10.1 13.4 %all-to-all-start = ((s16[32,416,128]{2,1,0:T(8,128)(2,1)}), s16[32,416,128]{2,1,0:T(8,128)(2,1)S(1)}, u32[]{:S(2)}, u32[]{:S(2)}) async-start(s16[32,416,128]{2,1,0:T(8,128)(2,1)} %products.1), calls=%async_computation | async-start | bytes 6815744 | tf_op jit(solution)/shard_map/all_to_all | solution.py:301
  23.5 1.9 %constant_dynamic-update-slice_fusion.2 = f32[12,40,640]{2,1,0:T(8,128)} fusion(f32[4,40,640]{2,1,0:T(8,128)} %param.13), kind=kLoop, calls=%fused_computation.13 | loop fusion | bytes 819200
  25.4 1.8 %constant_dynamic-update-slice_fusion.1 = f32[12,40,640]{2,1,0:T(8,128)} fusion(f32[12,40,640]{2,1,0:T(8,128)} %constant_dynamic-update-slice_fusion.2, f32[4,40,640]{2,1,0:T(8,128)} %param.14), kind=kLoop, calls=%fused_computation.12 | loop fusion | bytes 819200
  28.0 3.1 %collective-permute-start.14 = (f32[12,40,640]{2,1,0:T(8,128)}, f32[12,40,640]{2,1,0:T(8,128)}, u32[]{:S(2)}, u32[]{:S(2)}) collective-permute-start(f32[12,40,640]{2,1,0:T(8,128)} %constant_dynamic-update-slice_fusion.refs_8_), channel_id=1, source_target_pairs={{2,0},{3,1},{4,2},{5,3},{6,4},{7,5},{0,6},{1,7},{10,8},{11,9},{12,... | collective-permute-start | bytes 3686408 | tf_op jit(solution)/shard_map/ppermute | solution.py:264
  32.5 1.4 collective-permute-start.17
  33.8 24.4 %collective-permute-done.14.refs_9_ = f32[12,40,640]{2,1,0:T(8,128)} collective-permute-done((f32[12,40,640]{2,1,0:T(8,128)}, f32[12,40,640]{2,1,0:T(8,128)}, u32[]{:S(2)}, u32[]{:S(2)}) %collective-permute-start.14) | collective-permute-done | bytes 1228832 | tf_op jit(solution)/shard_map/ppermute | solution.py:264
  58.2 26.7 %collective-permute-start.18 = (f32[12,40,640]{2,1,0:T(8,128)}, f32[12,40,640]{2,1,0:T(8,128)}, u32[]{:S(2)}, u32[]{:S(2)}) collective-permute-start(f32[12,40,640]{2,1,0:T(8,128)} %collective-permute-done.14.refs_9_), channel_id=1, source_target_pairs={{0,1},{1,0},{2,3},{3,2},{4,5},{5,4},{6,7},{7,6},{8,9},{9,8},{10,11... | collective-permute-start | bytes 3686408 | tf_op jit(solution)/shard_map/ppermute | solution.py:283
  85.0 3.4 %collective-permute-start = (f32[6,32]{1,0:T(8,128)S(1)}, f32[6,32]{1,0:T(8,128)S(1)}, u32[]{:S(2)}, u32[]{:S(2)}) collective-permute-start(f32[6,32]{1,0:T(8,128)S(1)} %bitcast.34), channel_id=1, source_target_pairs={{2,0},{3,1},{4,2},{5,3},{6,4},{7,5},{0,6},{1,7},{10,8},{11,9},{12,... | collective-permute-start | bytes 2312 | tf_op jit(solution)/shard_map/ppermute | solution.py:264
  89.1 1.7 %collective-permute-start.1 = (f32[6,32]{1,0:T(8,128)S(1)}, f32[6,32]{1,0:T(8,128)S(1)}, u32[]{:S(2)}, u32[]{:S(2)}) collective-permute-start(f32[6,32]{1,0:T(8,128)S(1)} %bitcast.35), channel_id=1, source_target_pairs={{4,0},{5,1},{6,2},{7,3},{0,4},{1,5},{2,6},{3,7},{12,8},{13,9},{14,... | collective-permute-start | bytes 2312 | tf_op jit(solution)/shard_map/ppermute | solution.py:264
  90.8 2.6 %collective-permute-done.1 = f32[6,32]{1,0:T(8,128)S(1)} collective-permute-done((f32[6,32]{1,0:T(8,128)S(1)}, f32[6,32]{1,0:T(8,128)S(1)}, u32[]{:S(2)}, u32[]{:S(2)}) %collective-permute-start.1) | collective-permute-done | bytes 800 | tf_op jit(solution)/shard_map/ppermute | solution.py:264
  94.2 3.7 %collective-permute-done.2 = f32[6,32]{1,0:T(8,128)S(1)} collective-permute-done((f32[6,32]{1,0:T(8,128)S(1)}, f32[6,32]{1,0:T(8,128)S(1)}, u32[]{:S(2)}, u32[]{:S(2)}) %collective-permute-start.2) | collective-permute-done | bytes 800 | tf_op jit(solution)/shard_map/ppermute | solution.py:264
  97.9 2.4 %collective-permute-start.3 = (f32[6,32]{1,0:T(8,128)S(1)}, f32[6,32]{1,0:T(8,128)S(1)}, u32[]{:S(2)}, u32[]{:S(2)}) collective-permute-start(f32[6,32]{1,0:T(8,128)S(1)} %bitcast.37), channel_id=1, source_target_pairs={{0,1},{1,0},{2,3},{3,2},{4,5},{5,4},{6,7},{7,6},{8,9},{9,8},{10,11... | collective-permute-start | bytes 2312 | tf_op jit(solution)/shard_map/ppermute | solution.py:283
  104.4 1.1 collective-permute-done.6
  108.2 3.8 %broadcast_multiply_fusion = f32[32,8,48,8]{3,2,1,0:T(8,128)} fusion(f32[8,8]{1,0:T(8,128)} %fusion.2, f32[32,48]{1,0:T(8,128)S(1)} %bitcast.31), kind=kLoop, calls=%fused_computation | loop fusion | flops 98304 | bytes 399616 | tf_op jit(solution)/shard_map/jit(kron)/mul | solution.py:297
  112.0 5.9 %mul.73 = f32[256,384]{1,0:T(8,128)} reshape(f32[32,8,48,8]{3,2,1,0:T(8,128)} %broadcast_multiply_fusion) | data formatting | bytes 786432 | tf_op jit(solution)/shard_map/jit(kron)/mul | solution.py:297
  119.1 1.5 mul.78
  120.6 2.6 %collect.1.refs_0_ = s16[256,640]{1,0:T(8,128)(2,1)S(1)} custom-call(s16[32,416,128]{2,1,0:T(8,128)(2,1)S(1)} %all-to-all-done.parts_ref), custom_call_target="tpu_custom_call" | custom-call | flops 3407872 | bytes 3407872 | tf_op jit(solution)/shard_map/collect/pallas_call | solution.py:170
  123.2 1.9 %collective-permute-start.7 = (s16[256,640]{1,0:T(8,128)(2,1)S(1)}, s16[256,640]{1,0:T(8,128)(2,1)S(1)}, u32[]{:S(2)}, u32[]{:S(2)}) collective-permute-start(s16[256,640]{1,0:T(8,128)(2,1)S(1)} %collect.1.refs_0_), channel_id=1, source_target_pairs={{2,0},{3,1},{4,2},{5,3},{6,4},{7,5},{0,6},{1,7},{10,8},{11,9},{12,... | collective-permute-start | bytes 983048 | tf_op jit(solution)/shard_map/ppermute | solution.py:264
  126.7 5.4 %collective-permute-done.7.refs_1_ = s16[256,640]{1,0:T(8,128)(2,1)S(1)} collective-permute-done((s16[256,640]{1,0:T(8,128)(2,1)S(1)}, s16[256,640]{1,0:T(8,128)(2,1)S(1)}, u32[]{:S(2)}, u32[]{:S(2)}) %collective-permute-start.7) | collective-permute-done | bytes 327712 | tf_op jit(solution)/shard_map/ppermute | solution.py:264
  132.2 7.8 %collective-permute-start.11 = (s16[256,640]{1,0:T(8,128)(2,1)S(1)}, s16[256,640]{1,0:T(8,128)(2,1)S(1)}, u32[]{:S(2)}, u32[]{:S(2)}) collective-permute-start(s16[256,640]{1,0:T(8,128)(2,1)S(1)} %collective-permute-done.7.refs_1_), channel_id=1, source_target_pairs={{0,1},{1,0},{2,3},{3,2},{4,5},{5,4},{6,7},{7,6},{8,9},{9,8},{10,11... | collective-permute-start | bytes 983048 | tf_op jit(solution)/shard_map/ppermute | solution.py:283
  140.0 2.8 %collective-permute-done.9.refs_3_ = s16[256,640]{1,0:T(8,128)(2,1)S(1)} collective-permute-done((s16[256,640]{1,0:T(8,128)(2,1)S(1)}, s16[256,640]{1,0:T(8,128)(2,1)S(1)}, u32[]{:S(2)}, u32[]{:S(2)}) %collective-permute-start.9) | collective-permute-done | bytes 327712 | tf_op jit(solution)/shard_map/ppermute | solution.py:264
  143.6 1.1 collective-permute-done.13.refs_7_
  144.7 10.4 %update.1 = (f32[4,40,640]{2,1,0:T(8,128)}, f32[4,40,640]{2,1,0:T(8,128)}, f32[4,40,640]{2,1,0:T(8,128)}, bf16[6,40,640]{2,1,0:T(8,128)(2,1)}) custom-call(bf16[512,384]{1,0:T(8,128)(2,1)S(1)} %pad_maximum_fusion.mix_ref, bf16[96,256]{1,0:T(8,128)(2,1)S(1)} %pad_maximum_fusion.1.merge_ref, s16[256,640]{1,0:T(8,128)(2,1)S(1)} %collect.1.refs_0_, ...), custom_call_target="tpu_custom_call" | custom-call | tf_op jit(solution)/shard_map/update/pallas_call | solution.py:240
  (59 shorter events, 14.2 us)
Async XLA Ops:
  10.1 110.5 %all-to-all-start = ((s16[32,416,128]{2,1,0:T(8,128)(2,1)}), s16[32,416,128]{2,1,0:T(8,128)(2,1)S(1)}, u32[]{:S(2)}, u32[]{:S(2)}) async-start(s16[32,416,128]{2,1,0:T(8,128)(2,1)} %products.1), calls=%async_computation | async-start | bytes 6815744 | tf_op jit(solution)/shard_map/all_to_all | solution.py:301
  23.5 61.4 %copy-start.3 = (f32[1,6,32]{2,0,1:T(1,128)S(1)}, f32[1,6,32]{2,0,1:T(1,128)}, u32[]{:S(2)}) copy-start(f32[1,6,32]{2,0,1:T(1,128)} %param.12) | copy-start | bytes 2308
  28.0 30.2 %collective-permute-start.14 = (f32[12,40,640]{2,1,0:T(8,128)}, f32[12,40,640]{2,1,0:T(8,128)}, u32[]{:S(2)}, u32[]{:S(2)}) collective-permute-start(f32[12,40,640]{2,1,0:T(8,128)} %constant_dynamic-update-slice_fusion.refs_8_), channel_id=1, source_target_pairs={{2,0},{3,1},{4,2},{5,3},{6,4},{7,5},{0,6},{1,7},{10,8},{11,9},{12,... | collective-permute-start | bytes 3686408 | tf_op jit(solution)/shard_map/ppermute | solution.py:264
  31.1 71.5 %collective-permute-start.15 = (f32[12,40,640]{2,1,0:T(8,128)}, f32[12,40,640]{2,1,0:T(8,128)}, u32[]{:S(2)}, u32[]{:S(2)}) collective-permute-start(f32[12,40,640]{2,1,0:T(8,128)} %constant_dynamic-update-slice_fusion.refs_8_), channel_id=1, source_target_pairs={{4,0},{5,1},{6,2},{7,3},{0,4},{1,5},{2,6},{3,7},{12,8},{13,9},{14,... | collective-permute-start | bytes 3686408 | tf_op jit(solution)/shard_map/ppermute | solution.py:264
  31.6 76.4 %collective-permute-start.16 = (f32[12,40,640]{2,1,0:T(8,128)}, f32[12,40,640]{2,1,0:T(8,128)}, u32[]{:S(2)}, u32[]{:S(2)}) collective-permute-start(f32[12,40,640]{2,1,0:T(8,128)} %constant_dynamic-update-slice_fusion.refs_8_), channel_id=1, source_target_pairs={{6,0},{7,1},{0,2},{1,3},{2,4},{3,5},{4,6},{5,7},{14,8},{15,9},{8,1... | collective-permute-start | bytes 3686408 | tf_op jit(solution)/shard_map/ppermute | solution.py:264
  32.5 92.6 %collective-permute-start.17 = (f32[12,40,640]{2,1,0:T(8,128)}, f32[12,40,640]{2,1,0:T(8,128)}, u32[]{:S(2)}, u32[]{:S(2)}) collective-permute-start(f32[12,40,640]{2,1,0:T(8,128)} %constant_dynamic-update-slice_fusion.refs_8_), channel_id=1, source_target_pairs={{0,1},{1,0},{2,3},{3,2},{4,5},{5,4},{6,7},{7,6},{8,9},{9,8},{10,11... | collective-permute-start | bytes 3686408 | tf_op jit(solution)/shard_map/ppermute | solution.py:283
  58.2 66.9 %collective-permute-start.18 = (f32[12,40,640]{2,1,0:T(8,128)}, f32[12,40,640]{2,1,0:T(8,128)}, u32[]{:S(2)}, u32[]{:S(2)}) collective-permute-start(f32[12,40,640]{2,1,0:T(8,128)} %collective-permute-done.14.refs_9_), channel_id=1, source_target_pairs={{0,1},{1,0},{2,3},{3,2},{4,5},{5,4},{6,7},{7,6},{8,9},{9,8},{10,11... | collective-permute-start | bytes 3686408 | tf_op jit(solution)/shard_map/ppermute | solution.py:283
  85.0 4.2 %collective-permute-start = (f32[6,32]{1,0:T(8,128)S(1)}, f32[6,32]{1,0:T(8,128)S(1)}, u32[]{:S(2)}, u32[]{:S(2)}) collective-permute-start(f32[6,32]{1,0:T(8,128)S(1)} %bitcast.34), channel_id=1, source_target_pairs={{2,0},{3,1},{4,2},{5,3},{6,4},{7,5},{0,6},{1,7},{10,8},{11,9},{12,... | collective-permute-start | bytes 2312 | tf_op jit(solution)/shard_map/ppermute | solution.py:264
  89.1 4.3 %collective-permute-start.1 = (f32[6,32]{1,0:T(8,128)S(1)}, f32[6,32]{1,0:T(8,128)S(1)}, u32[]{:S(2)}, u32[]{:S(2)}) collective-permute-start(f32[6,32]{1,0:T(8,128)S(1)} %bitcast.35), channel_id=1, source_target_pairs={{4,0},{5,1},{6,2},{7,3},{0,4},{1,5},{2,6},{3,7},{12,8},{13,9},{14,... | collective-permute-start | bytes 2312 | tf_op jit(solution)/shard_map/ppermute | solution.py:264
  93.4 4.5 %collective-permute-start.2 = (f32[6,32]{1,0:T(8,128)S(1)}, f32[6,32]{1,0:T(8,128)S(1)}, u32[]{:S(2)}, u32[]{:S(2)}) collective-permute-start(f32[6,32]{1,0:T(8,128)S(1)} %bitcast.36), channel_id=1, source_target_pairs={{6,0},{7,1},{0,2},{1,3},{2,4},{3,5},{4,6},{5,7},{14,8},{15,9},{8,1... | collective-permute-start | bytes 2312 | tf_op jit(solution)/shard_map/ppermute | solution.py:264
  97.9 3.2 %collective-permute-start.3 = (f32[6,32]{1,0:T(8,128)S(1)}, f32[6,32]{1,0:T(8,128)S(1)}, u32[]{:S(2)}, u32[]{:S(2)}) collective-permute-start(f32[6,32]{1,0:T(8,128)S(1)} %bitcast.37), channel_id=1, source_target_pairs={{0,1},{1,0},{2,3},{3,2},{4,5},{5,4},{6,7},{7,6},{8,9},{9,8},{10,11... | collective-permute-start | bytes 2312 | tf_op jit(solution)/shard_map/ppermute | solution.py:283
  101.1 1.2 collective-permute-start.4
  102.2 1.2 collective-permute-start.5
  102.6 23.2 %collective-permute-start.19 = (f32[12,40,640]{2,1,0:T(8,128)}, f32[12,40,640]{2,1,0:T(8,128)}, u32[]{:S(2)}, u32[]{:S(2)}) collective-permute-start(f32[12,40,640]{2,1,0:T(8,128)} %collective-permute-done.15.refs_10_), channel_id=1, source_target_pairs={{0,1},{1,0},{2,3},{3,2},{4,5},{5,4},{6,7},{7,6},{8,9},{9,8},{10,11... | collective-permute-start | bytes 3686408 | tf_op jit(solution)/shard_map/ppermute | solution.py:283
  103.4 2.1 %collective-permute-start.6 = (f32[6,32]{1,0:T(8,128)S(1)}, f32[6,32]{1,0:T(8,128)S(1)}, u32[]{:S(2)}, u32[]{:S(2)}) collective-permute-start(f32[6,32]{1,0:T(8,128)S(1)} %collective-permute-done.2), channel_id=1, source_target_pairs={{0,1},{1,0},{2,3},{3,2},{4,5},{5,4},{6,7},{7,6},{8,9},{9,8},{10,11... | collective-permute-start | bytes 2312 | tf_op jit(solution)/shard_map/ppermute | solution.py:283
  108.0 35.6 %collective-permute-start.20 = (f32[12,40,640]{2,1,0:T(8,128)}, f32[12,40,640]{2,1,0:T(8,128)}, u32[]{:S(2)}, u32[]{:S(2)}) collective-permute-start(f32[12,40,640]{2,1,0:T(8,128)} %collective-permute-done.16.refs_11_), channel_id=1, source_target_pairs={{0,1},{1,0},{2,3},{3,2},{4,5},{5,4},{6,7},{7,6},{8,9},{9,8},{10,11... | collective-permute-start | bytes 3686408 | tf_op jit(solution)/shard_map/ppermute | solution.py:283
  120.6 22.9 %copy-start = (f32[256,384]{1,0:T(8,128)S(1)}, f32[256,384]{1,0:T(8,128)}, u32[]{:S(2)}) copy-start(f32[256,384]{1,0:T(8,128)} %mul.73) | copy-start | bytes 1179652
  123.2 9.0 %collective-permute-start.7 = (s16[256,640]{1,0:T(8,128)(2,1)S(1)}, s16[256,640]{1,0:T(8,128)(2,1)S(1)}, u32[]{:S(2)}, u32[]{:S(2)}) collective-permute-start(s16[256,640]{1,0:T(8,128)(2,1)S(1)} %collect.1.refs_0_), channel_id=1, source_target_pairs={{2,0},{3,1},{4,2},{5,3},{6,4},{7,5},{0,6},{1,7},{10,8},{11,9},{12,... | collective-permute-start | bytes 983048 | tf_op jit(solution)/shard_map/ppermute | solution.py:264
  125.0 15.0 %collective-permute-start.8 = (s16[256,640]{1,0:T(8,128)(2,1)S(1)}, s16[256,640]{1,0:T(8,128)(2,1)S(1)}, u32[]{:S(2)}, u32[]{:S(2)}) collective-permute-start(s16[256,640]{1,0:T(8,128)(2,1)S(1)} %collect.1.refs_0_), channel_id=1, source_target_pairs={{4,0},{5,1},{6,2},{7,3},{0,4},{1,5},{2,6},{3,7},{12,8},{13,9},{14,... | collective-permute-start | bytes 983048 | tf_op jit(solution)/shard_map/ppermute | solution.py:264
  125.1 17.7 %collective-permute-start.9 = (s16[256,640]{1,0:T(8,128)(2,1)S(1)}, s16[256,640]{1,0:T(8,128)(2,1)S(1)}, u32[]{:S(2)}, u32[]{:S(2)}) collective-permute-start(s16[256,640]{1,0:T(8,128)(2,1)S(1)} %collect.1.refs_0_), channel_id=1, source_target_pairs={{6,0},{7,1},{0,2},{1,3},{2,4},{3,5},{4,6},{5,7},{14,8},{15,9},{8,1... | collective-permute-start | bytes 983048 | tf_op jit(solution)/shard_map/ppermute | solution.py:264
  125.8 17.8 %collective-permute-start.10 = (s16[256,640]{1,0:T(8,128)(2,1)S(1)}, s16[256,640]{1,0:T(8,128)(2,1)S(1)}, u32[]{:S(2)}, u32[]{:S(2)}) collective-permute-start(s16[256,640]{1,0:T(8,128)(2,1)S(1)} %collect.1.refs_0_), channel_id=1, source_target_pairs={{0,1},{1,0},{2,3},{3,2},{4,5},{5,4},{6,7},{7,6},{8,9},{9,8},{10,11... | collective-permute-start | bytes 983048 | tf_op jit(solution)/shard_map/ppermute | solution.py:283
  132.2 11.4 %collective-permute-start.11 = (s16[256,640]{1,0:T(8,128)(2,1)S(1)}, s16[256,640]{1,0:T(8,128)(2,1)S(1)}, u32[]{:S(2)}, u32[]{:S(2)}) collective-permute-start(s16[256,640]{1,0:T(8,128)(2,1)S(1)} %collective-permute-done.7.refs_1_), channel_id=1, source_target_pairs={{0,1},{1,0},{2,3},{3,2},{4,5},{5,4},{6,7},{7,6},{8,9},{9,8},{10,11... | collective-permute-start | bytes 983048 | tf_op jit(solution)/shard_map/ppermute | solution.py:283
  140.0 3.6 %collective-permute-start.12 = (s16[256,640]{1,0:T(8,128)(2,1)S(1)}, s16[256,640]{1,0:T(8,128)(2,1)S(1)}, u32[]{:S(2)}, u32[]{:S(2)}) collective-permute-start(s16[256,640]{1,0:T(8,128)(2,1)S(1)} %collective-permute-done.8.refs_2_), channel_id=1, source_target_pairs={{0,1},{1,0},{2,3},{3,2},{4,5},{5,4},{6,7},{7,6},{8,9},{9,8},{10,11... | collective-permute-start | bytes 983048 | tf_op jit(solution)/shard_map/ppermute | solution.py:283
  142.8 2.0 %collective-permute-start.13 = (s16[256,640]{1,0:T(8,128)(2,1)S(1)}, s16[256,640]{1,0:T(8,128)(2,1)S(1)}, u32[]{:S(2)}, u32[]{:S(2)}) collective-permute-start(s16[256,640]{1,0:T(8,128)(2,1)S(1)} %collective-permute-done.9.refs_3_), channel_id=1, source_target_pairs={{0,1},{1,0},{2,3},{3,2},{4,5},{5,4},{6,7},{7,6},{8,9},{9,8},{10,11... | collective-permute-start | bytes 983048 | tf_op jit(solution)/shard_map/ppermute | solution.py:283
  (2 other events, 9.6 us)

commit v3 on v2

--- a/solution.py
+++ b/solution.py
@@ -255,9 +255,60 @@
     )(mix, merge, *sums, *states)
 
 
-def in_two_parts(matrix):
-    high = lax.reduce_precision(matrix, 8, 7)
-    return jnp.concatenate([high, matrix - high], axis=0).astype(BF16)
+def prepare_kernel(rep_ref, *refs):
+    coefs, (mix_ref, merge_ref) = refs[:-2], refs[-2:]
+    reps, chips = len(coefs), len(coefs) // 2
+    padded, experts = coefs[0].shape
+    rows = mix_ref.shape[0] // 2
+    columns = mix_ref.shape[1]
+    out_rows = merge_ref.shape[0] // 2
+    nsys = out_rows // 8
+    mine = experts // reps
+    chip, core = rep_ref[0] // 2, rep_ref[0] % 2
+
+    def count(shape, axis):
+        return lax.broadcasted_iota(jnp.int32, shape, axis)
+
+    expert = count((rows, experts), 0) >> 3
+    block = expert // mine
+    owner = ((chip + block % chips) % chips) * 2 + (core + block // chips) % 2
+    at_expert = owner * mine + expert % mine == count((rows, experts), 1)
+    at_expert = at_expert.astype(F32).astype(BF16)
+    row = count((padded * reps, columns), 0)
+    place = row % padded
+    at_system = (count((padded * reps, columns), 1) >> 3) == nsys * (row // padded) + place
+    at_system = (at_system & (place < nsys)).astype(F32).astype(BF16)
+    at_out = (count((out_rows, padded), 0) >> 3) == count((out_rows, padded), 1)
+    at_out = at_out.astype(F32).astype(BF16)
+    same_mix = (count((rows, columns), 0) & 7) == (count((rows, columns), 1) & 7)
+    same_merge = (count((out_rows, rows), 0) & 7) == (count((out_rows, rows), 1) & 7)
+    values = jnp.concatenate([ref[...] for ref in coefs], axis=0)
+    near = values.astype(BF16)
+    rest = (values - near.astype(F32)).astype(BF16)
+    transposed = (((1,), (1,)), ((), ()))
+    for k, part in enumerate((near, rest)):
+        wide = lax.dot_general(at_expert, part, transposed, preferred_element_type=F32)
+        wide = jnp.dot(wide.astype(BF16), at_system, preferred_element_type=F32)
+        mix_ref[k * rows : (k + 1) * rows, :] = jnp.where(same_mix, wide, 0.0).astype(BF16)
+        own = jnp.dot(at_out, part[:padded], preferred_element_type=F32)
+        own = lax.dot_general(own.astype(BF16), at_expert, transposed, preferred_element_type=F32)
+        merge_ref[k * out_rows : (k + 1) * out_rows, :] = jnp.where(same_merge, own, 0.0).astype(BF16)
+
+
+def prepare(rep, coefs, nsys):
+    reps, experts = len(coefs), coefs[0].shape[1]
+    vmem = pl.BlockSpec(memory_space=pltpu.VMEM)
+    return pl.pallas_call(
+        prepare_kernel,
+        in_specs=[pl.BlockSpec(memory_space=pltpu.SMEM)] + [vmem] * reps,
+        out_specs=[vmem, vmem],
+        out_shape=[
+            jax.ShapeDtypeStruct((2 * 8 * experts, 8 * reps * nsys), BF16),
+            jax.ShapeDtypeStruct((2 * 8 * nsys, 8 * experts), BF16),
+        ],
+        compiler_params=pltpu.CompilerParams(vmem_limit_bytes=12 * MIB),
+        name="prepare",
+    )(rep, *coefs)
 
 
 def everywhere(value, axis, moves):
@@ -282,20 +333,12 @@
         near = [value] + everywhere(value, "rep", along_x)
         return near + [lax.ppermute(part, "rep", swap) for part in near]
 
-    coefs = jnp.stack(all_reps(coef[0]))
-    states = all_reps(jnp.concatenate([weights, first_moment, second_moment], axis=0))
-
-    rep = lax.axis_index("rep")
-    chip, core = rep // 2, rep % 2
-    order = jnp.stack(
-        [(chip + dx) % chips * 2 + (core + other) % 2 for other in (0, 1) for dx in range(chips)]
+    coefs = all_reps(jnp.pad(coef[0], ((0, -nsys % 8), (0, 0))))
+    mix, merge = prepare(lax.axis_index("rep").reshape(1), coefs, nsys)
+    mix, merge, *state_parts = lax.optimization_barrier(
+        (mix, merge, weights, first_moment, second_moment)
     )
-    chosen = (order[:, None] == jnp.arange(reps))[:, :, None]
-    by_owner = coefs.reshape(reps * nsys, 1, reps, -1)
-    ordered = jnp.sum(jnp.where(chosen, by_owner, 0.0), axis=2).reshape(reps * nsys, -1)
-    eye = jnp.eye(8, dtype=F32)
-    mix = in_two_parts(jnp.kron(ordered.T, eye))
-    merge = in_two_parts(jnp.kron(ordered[:nsys], eye))
+    states = all_reps(jnp.concatenate(state_parts, axis=0))
 
     parts = products(edge_count, edge_system, edge_feats[0], edge_grads[0], owners)
     received = lax.all_to_all(parts, "run", 0, 0, tiled=True)

time: 154 us -> 139 us (0.903); the launches traced: 155 us -> 136 us
  starting transfers between devices: 67.8 us -> 42.6 us
  waiting for transfers between devices: 43.4 us -> 63.8 us
  local copies, waits for them, and re-layouts: 13.7 us -> 5.16 us
  other arithmetic: 6.99 us -> 0 us
    ppermute x12, starting transfers between devices: 41.4 us -> 18.3 us  [all_reps(): return near + [lax.ppermute(part, 'rep', swap) for part in near]]
    ppermute x9, waiting for transfers between devices: 39.6 us -> 59.2 us  [everywhere(): return [lax.ppermute(value, axis, pairs) for pairs in moves]]
    mul x3 -> x0, local copies, waits for them, and re-layouts: 7.5 us -> none  [the longest x1 5.9 us: on_device(): mix = in_two_parts(jnp.kron(ordered.T, eye))]
    mul x2 -> x0, other arithmetic: 4.86 us -> none  [the longest x1 3.81 us: on_device(): mix = in_two_parts(jnp.kron(ordered.T, eye))]
    all_to_all x1, waiting for transfers between devices: 0.01 us -> 2.51 us  [on_device(): received = lax.all_to_all(parts, 'run', 0, 0, tiled=True)]
    ppermute x9, starting transfers between devices: 13 us -> 10.9 us  [everywhere(): return [lax.ppermute(value, axis, pairs) for pairs in moves]]
    ppermute x12, waiting for transfers between devices: 3.81 us -> 2.07 us  [all_reps(): return near + [lax.ppermute(part, 'rep', swap) for part in near]]
    another operation x10 -> x0, local copies, waits for them, and re-layouts: 1.64 us -> none  [the longest x9 1.55 us: on_device(): coefs = jnp.stack(all_reps(coef[0]))]
  transfers between devices with their start and end apart: 22 -> 22, of which waited for: 10 -> 9; matrix products, arithmetic and copies ran while one was open for 13% -> 3% of each run, Pallas kernels for 2% -> 3%
where the time goes in v3:
time: 139 us; the launch traced here: 136 us
  waiting for transfers between devices  63.8 us (46%)
  starting transfers between devices  42.6 us (31%)
  Pallas kernels  22.7 us (16%)
  local copies, waits for them, and re-layouts  5.16 us (4%)
  between operations  1.53 us (1%)
    ppermute x9, waiting for transfers between devices, everywhere(): return [lax.ppermute(value, axis, pairs) for pairs in moves]  59.2 us
    ppermute x12, starting transfers between devices, all_reps(): return near + [lax.ppermute(part, 'rep', swap) for part in near]  18.3 us
    all_to_all x1, starting transfers between devices, on_device(): received = lax.all_to_all(parts, 'run', 0, 0, tiled=True)  13.4 us
    ppermute x9, starting transfers between devices, everywhere(): return [lax.ppermute(value, axis, pairs) for pairs in moves]  10.9 us
    pallas_call x1, Pallas kernels, update(): pl.pallas_call(update_kernel, grid=(rows // group,), in_specs=[pl.BlockSp...  10.4 us
    pallas_call x1, Pallas kernels, products(): pl.pallas_call(product_kernel, grid=(rows // block,), in_specs=[pl.BlockS...  8.74 us
    unnamed x11, local copies, waits for them, and re-layouts  4.35 us
  transfers between devices with their start and end apart: 22, of which 9 were waited for; matrix products, arithmetic and copies ran while one was open for 3% of the time, Pallas kernels for 3%

profile of v3, /device:TPU:1, one launch (start us, length us, event | category | flops | bytes accessed | tf_op | source)
XLA Modules:
  0.0 135.8 jit_solution(4933176555097720061)
XLA Ops:
  1.3 8.7 %products.1 = s16[32,416,128]{2,1,0:T(8,128)(2,1)} custom-call(s32[1,1]{1,0:T(1,128)S(6)} %copy.17.count_ref, s32[1,2048]{1,0:T(1,128)} %system_ref.1, bf16[2048,1280]{1,0:T(8,128)(2,1)} %bitcast.8, bf16[2048,640]{1,0:T(8,128)(2,1)} %bitcast.9), custom_call_target="tpu_custom_call" | custom-call | flops 3355443200 | bytes 11141120 | tf_op jit(solution)/shard_map/products/pallas_call | solution.py:111
  10.0 13.4 %all-to-all-start = ((s16[32,416,128]{2,1,0:T(8,128)(2,1)}), s16[32,416,128]{2,1,0:T(8,128)(2,1)S(1)}, u32[]{:S(2)}, u32[]{:S(2)}) async-start(s16[32,416,128]{2,1,0:T(8,128)(2,1)} %products.1), calls=%async_computation | async-start | bytes 6815744 | tf_op jit(solution)/shard_map/all_to_all | solution.py:344
  23.4 2.9 %collective-permute-start = (f32[8,32]{1,0:T(8,128)S(1)}, f32[8,32]{1,0:T(8,128)S(1)}, u32[]{:S(2)}, u32[]{:S(2)}) collective-permute-start(f32[8,32]{1,0:T(8,128)S(1)} %pad.4.refs_0_), channel_id=1, source_target_pairs={{2,0},{3,1},{4,2},{5,3},{6,4},{7,5},{0,6},{1,7},{10,8},{11,9},{12,... | collective-permute-start | bytes 3080 | tf_op jit(solution)/shard_map/ppermute | solution.py:315
  27.4 1.3 collective-permute-start.3
  28.8 1.5 %collective-permute-done.1.refs_2_ = f32[8,32]{1,0:T(8,128)S(1)} collective-permute-done((f32[8,32]{1,0:T(8,128)S(1)}, f32[8,32]{1,0:T(8,128)S(1)}, u32[]{:S(2)}, u32[]{:S(2)}) %collective-permute-start.1) | collective-permute-done | bytes 1056 | tf_op jit(solution)/shard_map/ppermute | solution.py:315
  30.3 1.9 %collective-permute-start.5 = (f32[8,32]{1,0:T(8,128)S(1)}, f32[8,32]{1,0:T(8,128)S(1)}, u32[]{:S(2)}, u32[]{:S(2)}) collective-permute-start(f32[8,32]{1,0:T(8,128)S(1)} %collective-permute-done.1.refs_2_), channel_id=1, source_target_pairs={{0,1},{1,0},{2,3},{3,2},{4,5},{5,4},{6,7},{7,6},{8,9},{9,8},{10,11... | collective-permute-start | bytes 3080 | tf_op jit(solution)/shard_map/ppermute | solution.py:334
  35.2 1.8 %constant_dynamic-update-slice_fusion.2 = f32[12,40,640]{2,1,0:T(8,128)} fusion(f32[4,40,640]{2,1,0:T(8,128)} %param.13), kind=kLoop, calls=%fused_computation.2 | loop fusion | bytes 819200
  36.9 1.8 %constant_dynamic-update-slice_fusion.1 = f32[12,40,640]{2,1,0:T(8,128)} fusion(f32[12,40,640]{2,1,0:T(8,128)} %constant_dynamic-update-slice_fusion.2, f32[4,40,640]{2,1,0:T(8,128)} %param.14), kind=kLoop, calls=%fused_computation.1 | loop fusion | bytes 819200
  41.6 1.2 collective-permute-start.17
  42.8 25.3 %collective-permute-done.14.refs_9_ = f32[12,40,640]{2,1,0:T(8,128)} collective-permute-done((f32[12,40,640]{2,1,0:T(8,128)}, f32[12,40,640]{2,1,0:T(8,128)}, u32[]{:S(2)}, u32[]{:S(2)}) %collective-permute-start.14) | collective-permute-done | bytes 1228832 | tf_op jit(solution)/shard_map/ppermute | solution.py:315
  68.1 1.9 %collective-permute-start.18 = (f32[12,40,640]{2,1,0:T(8,128)}, f32[12,40,640]{2,1,0:T(8,128)}, u32[]{:S(2)}, u32[]{:S(2)}) collective-permute-start(f32[12,40,640]{2,1,0:T(8,128)} %collective-permute-done.14.refs_9_), channel_id=1, source_target_pairs={{0,1},{1,0},{2,3},{3,2},{4,5},{5,4},{6,7},{7,6},{8,9},{9,8},{10,11... | collective-permute-start | bytes 3686408 | tf_op jit(solution)/shard_map/ppermute | solution.py:334
  70.1 2.0 %collective-permute-start.19 = (f32[12,40,640]{2,1,0:T(8,128)}, f32[12,40,640]{2,1,0:T(8,128)}, u32[]{:S(2)}, u32[]{:S(2)}) collective-permute-start(f32[12,40,640]{2,1,0:T(8,128)} %collective-permute-done.15.refs_10_), channel_id=1, source_target_pairs={{0,1},{1,0},{2,3},{3,2},{4,5},{5,4},{6,7},{7,6},{8,9},{9,8},{10,11... | collective-permute-start | bytes 3686408 | tf_op jit(solution)/shard_map/ppermute | solution.py:334
  72.1 24.9 %collective-permute-done.16.refs_11_ = f32[12,40,640]{2,1,0:T(8,128)} collective-permute-done((f32[12,40,640]{2,1,0:T(8,128)}, f32[12,40,640]{2,1,0:T(8,128)}, u32[]{:S(2)}, u32[]{:S(2)}) %collective-permute-start.16) | collective-permute-done | bytes 1228832 | tf_op jit(solution)/shard_map/ppermute | solution.py:315
  97.5 2.5 %all-to-all-done.parts_ref = s16[32,416,128]{2,1,0:T(8,128)(2,1)S(1)} async-done(((s16[32,416,128]{2,1,0:T(8,128)(2,1)}), s16[32,416,128]{2,1,0:T(8,128)(2,1)S(1)}, u32[]{:S(2)}, u32[]{:S(2)}) %all-to-all-start) | async-done | bytes 3407904 | tf_op jit(solution)/shard_map/all_to_all | solution.py:344
  100.0 2.7 %collect.1.refs_0_ = s16[256,640]{1,0:T(8,128)(2,1)S(1)} custom-call(s16[32,416,128]{2,1,0:T(8,128)(2,1)S(1)} %all-to-all-done.parts_ref), custom_call_target="tpu_custom_call" | custom-call | flops 3407872 | bytes 3407872 | tf_op jit(solution)/shard_map/collect/pallas_call | solution.py:170
  102.7 2.6 %collective-permute-start.7 = (s16[256,640]{1,0:T(8,128)(2,1)S(1)}, s16[256,640]{1,0:T(8,128)(2,1)S(1)}, u32[]{:S(2)}, u32[]{:S(2)}) collective-permute-start(s16[256,640]{1,0:T(8,128)(2,1)S(1)} %collect.1.refs_0_), channel_id=1, source_target_pairs={{2,0},{3,1},{4,2},{5,3},{6,4},{7,5},{0,6},{1,7},{10,8},{11,9},{12,... | collective-permute-start | bytes 983048 | tf_op jit(solution)/shard_map/ppermute | solution.py:315
  105.3 2.2 %collective-permute-start.8 = (s16[256,640]{1,0:T(8,128)(2,1)S(1)}, s16[256,640]{1,0:T(8,128)(2,1)S(1)}, u32[]{:S(2)}, u32[]{:S(2)}) collective-permute-start(s16[256,640]{1,0:T(8,128)(2,1)S(1)} %collect.1.refs_0_), channel_id=1, source_target_pairs={{4,0},{5,1},{6,2},{7,3},{0,4},{1,5},{2,6},{3,7},{12,8},{13,9},{14,... | collective-permute-start | bytes 983048 | tf_op jit(solution)/shard_map/ppermute | solution.py:315
  107.6 1.7 %collective-permute-start.10 = (s16[256,640]{1,0:T(8,128)(2,1)S(1)}, s16[256,640]{1,0:T(8,128)(2,1)S(1)}, u32[]{:S(2)}, u32[]{:S(2)}) collective-permute-start(s16[256,640]{1,0:T(8,128)(2,1)S(1)} %collect.1.refs_0_), channel_id=1, source_target_pairs={{0,1},{1,0},{2,3},{3,2},{4,5},{5,4},{6,7},{7,6},{8,9},{9,8},{10,11... | collective-permute-start | bytes 983048 | tf_op jit(solution)/shard_map/ppermute | solution.py:334
  109.3 3.7 %collective-permute-done.7.refs_1_ = s16[256,640]{1,0:T(8,128)(2,1)S(1)} collective-permute-done((s16[256,640]{1,0:T(8,128)(2,1)S(1)}, s16[256,640]{1,0:T(8,128)(2,1)S(1)}, u32[]{:S(2)}, u32[]{:S(2)}) %collective-permute-start.7) | collective-permute-done | bytes 327712 | tf_op jit(solution)/shard_map/ppermute | solution.py:315
  113.1 2.3 %collective-permute-start.11 = (s16[256,640]{1,0:T(8,128)(2,1)S(1)}, s16[256,640]{1,0:T(8,128)(2,1)S(1)}, u32[]{:S(2)}, u32[]{:S(2)}) collective-permute-start(s16[256,640]{1,0:T(8,128)(2,1)S(1)} %collective-permute-done.7.refs_1_), channel_id=1, source_target_pairs={{0,1},{1,0},{2,3},{3,2},{4,5},{5,4},{6,7},{7,6},{8,9},{9,8},{10,11... | collective-permute-start | bytes 983048 | tf_op jit(solution)/shard_map/ppermute | solution.py:334
  115.4 4.4 %collective-permute-start.12 = (s16[256,640]{1,0:T(8,128)(2,1)S(1)}, s16[256,640]{1,0:T(8,128)(2,1)S(1)}, u32[]{:S(2)}, u32[]{:S(2)}) collective-permute-start(s16[256,640]{1,0:T(8,128)(2,1)S(1)} %collective-permute-done.8.refs_2_), channel_id=1, source_target_pairs={{0,1},{1,0},{2,3},{3,2},{4,5},{5,4},{6,7},{7,6},{8,9},{9,8},{10,11... | collective-permute-start | bytes 983048 | tf_op jit(solution)/shard_map/ppermute | solution.py:334
  119.8 3.7 %collective-permute-done.9.refs_3_ = s16[256,640]{1,0:T(8,128)(2,1)S(1)} collective-permute-done((s16[256,640]{1,0:T(8,128)(2,1)S(1)}, s16[256,640]{1,0:T(8,128)(2,1)S(1)}, u32[]{:S(2)}, u32[]{:S(2)}) %collective-permute-start.9) | collective-permute-done | bytes 327712 | tf_op jit(solution)/shard_map/ppermute | solution.py:315
  124.0 1.2 collective-permute-done.13.refs_7_
  125.2 10.4 %update.1 = (f32[4,40,640]{2,1,0:T(8,128)}, f32[4,40,640]{2,1,0:T(8,128)}, f32[4,40,640]{2,1,0:T(8,128)}, bf16[6,40,640]{2,1,0:T(8,128)(2,1)}) custom-call(bf16[512,384]{1,0:T(8,128)(2,1)S(1)} %copy-done.1, bf16[96,256]{1,0:T(8,128)(2,1)S(1)} %get-tuple-element.18.merge_ref, s16[256,640]{1,0:T(8,128)(2,1)S(1)} %collect.1.refs_0_, ...), custom_call_target="tpu_custom_call" | custom-call | tf_op jit(solution)/shard_map/update/pallas_call | solution.py:240
  (37 shorter events, 8.0 us)
Async XLA Ops:
  10.0 13.4 %copy-start.3 = (f32[1,6,32]{2,0,1:T(1,128)S(1)}, f32[1,6,32]{2,0,1:T(1,128)}, u32[]{:S(2)}) copy-start(f32[1,6,32]{2,0,1:T(1,128)} %param.12) | copy-start | bytes 2308
  10.0 90.0 %all-to-all-start = ((s16[32,416,128]{2,1,0:T(8,128)(2,1)}), s16[32,416,128]{2,1,0:T(8,128)(2,1)S(1)}, u32[]{:S(2)}, u32[]{:S(2)}) async-start(s16[32,416,128]{2,1,0:T(8,128)(2,1)} %products.1), calls=%async_computation | async-start | bytes 6815744 | tf_op jit(solution)/shard_map/all_to_all | solution.py:344
  23.4 5.3 %collective-permute-start = (f32[8,32]{1,0:T(8,128)S(1)}, f32[8,32]{1,0:T(8,128)S(1)}, u32[]{:S(2)}, u32[]{:S(2)}) collective-permute-start(f32[8,32]{1,0:T(8,128)S(1)} %pad.4.refs_0_), channel_id=1, source_target_pairs={{2,0},{3,1},{4,2},{5,3},{6,4},{7,5},{0,6},{1,7},{10,8},{11,9},{12,... | collective-permute-start | bytes 3080 | tf_op jit(solution)/shard_map/ppermute | solution.py:315
  26.3 4.0 %collective-permute-start.1 = (f32[8,32]{1,0:T(8,128)S(1)}, f32[8,32]{1,0:T(8,128)S(1)}, u32[]{:S(2)}, u32[]{:S(2)}) collective-permute-start(f32[8,32]{1,0:T(8,128)S(1)} %pad.4.refs_0_), channel_id=1, source_target_pairs={{4,0},{5,1},{6,2},{7,3},{0,4},{1,5},{2,6},{3,7},{12,8},{13,9},{14,... | collective-permute-start | bytes 3080 | tf_op jit(solution)/shard_map/ppermute | solution.py:315
  27.3 4.8 %collective-permute-start.2 = (f32[8,32]{1,0:T(8,128)S(1)}, f32[8,32]{1,0:T(8,128)S(1)}, u32[]{:S(2)}, u32[]{:S(2)}) collective-permute-start(f32[8,32]{1,0:T(8,128)S(1)} %pad.4.refs_0_), channel_id=1, source_target_pairs={{6,0},{7,1},{0,2},{1,3},{2,4},{3,5},{4,6},{5,7},{14,8},{15,9},{8,1... | collective-permute-start | bytes 3080 | tf_op jit(solution)/shard_map/ppermute | solution.py:315
  27.4 5.2 %collective-permute-start.3 = (f32[8,32]{1,0:T(8,128)S(1)}, f32[8,32]{1,0:T(8,128)S(1)}, u32[]{:S(2)}, u32[]{:S(2)}) collective-permute-start(f32[8,32]{1,0:T(8,128)S(1)} %pad.4.refs_0_), channel_id=1, source_target_pairs={{0,1},{1,0},{2,3},{3,2},{4,5},{5,4},{6,7},{7,6},{8,9},{9,8},{10,11... | collective-permute-start | bytes 3080 | tf_op jit(solution)/shard_map/ppermute | solution.py:334
  28.7 3.9 %collective-permute-start.4 = (f32[8,32]{1,0:T(8,128)S(1)}, f32[8,32]{1,0:T(8,128)S(1)}, u32[]{:S(2)}, u32[]{:S(2)}) collective-permute-start(f32[8,32]{1,0:T(8,128)S(1)} %collective-permute-done.refs_1_), channel_id=1, source_target_pairs={{0,1},{1,0},{2,3},{3,2},{4,5},{5,4},{6,7},{7,6},{8,9},{9,8},{10,11... | collective-permute-start | bytes 3080 | tf_op jit(solution)/shard_map/ppermute | solution.py:334
  30.3 2.7 %collective-permute-start.5 = (f32[8,32]{1,0:T(8,128)S(1)}, f32[8,32]{1,0:T(8,128)S(1)}, u32[]{:S(2)}, u32[]{:S(2)}) collective-permute-start(f32[8,32]{1,0:T(8,128)S(1)} %collective-permute-done.1.refs_2_), channel_id=1, source_target_pairs={{0,1},{1,0},{2,3},{3,2},{4,5},{5,4},{6,7},{7,6},{8,9},{9,8},{10,11... | collective-permute-start | bytes 3080 | tf_op jit(solution)/shard_map/ppermute | solution.py:334
  32.1 1.4 %collective-permute-start.6 = (f32[8,32]{1,0:T(8,128)S(1)}, f32[8,32]{1,0:T(8,128)S(1)}, u32[]{:S(2)}, u32[]{:S(2)}) collective-permute-start(f32[8,32]{1,0:T(8,128)S(1)} %collective-permute-done.2.refs_3_), channel_id=1, source_target_pairs={{0,1},{1,0},{2,3},{3,2},{4,5},{5,4},{6,7},{7,6},{8,9},{9,8},{10,11... | collective-permute-start | bytes 3080 | tf_op jit(solution)/shard_map/ppermute | solution.py:334
  39.6 28.6 %collective-permute-start.14 = (f32[12,40,640]{2,1,0:T(8,128)}, f32[12,40,640]{2,1,0:T(8,128)}, u32[]{:S(2)}, u32[]{:S(2)}) collective-permute-start(f32[12,40,640]{2,1,0:T(8,128)} %constant_dynamic-update-slice_fusion.refs_8_), channel_id=1, source_target_pairs={{2,0},{3,1},{4,2},{5,3},{6,4},{7,5},{0,6},{1,7},{10,8},{11,9},{12,... | collective-permute-start | bytes 3686408 | tf_op jit(solution)/shard_map/ppermute | solution.py:315
  39.9 30.1 %collective-permute-start.15 = (f32[12,40,640]{2,1,0:T(8,128)}, f32[12,40,640]{2,1,0:T(8,128)}, u32[]{:S(2)}, u32[]{:S(2)}) collective-permute-start(f32[12,40,640]{2,1,0:T(8,128)} %constant_dynamic-update-slice_fusion.refs_8_), channel_id=1, source_target_pairs={{4,0},{5,1},{6,2},{7,3},{0,4},{1,5},{2,6},{3,7},{12,8},{13,9},{14,... | collective-permute-start | bytes 3686408 | tf_op jit(solution)/shard_map/ppermute | solution.py:315
  40.8 56.3 %collective-permute-start.16 = (f32[12,40,640]{2,1,0:T(8,128)}, f32[12,40,640]{2,1,0:T(8,128)}, u32[]{:S(2)}, u32[]{:S(2)}) collective-permute-start(f32[12,40,640]{2,1,0:T(8,128)} %constant_dynamic-update-slice_fusion.refs_8_), channel_id=1, source_target_pairs={{6,0},{7,1},{0,2},{1,3},{2,4},{3,5},{4,6},{5,7},{14,8},{15,9},{8,1... | collective-permute-start | bytes 3686408 | tf_op jit(solution)/shard_map/ppermute | solution.py:315
  41.6 63.7 %collective-permute-start.17 = (f32[12,40,640]{2,1,0:T(8,128)}, f32[12,40,640]{2,1,0:T(8,128)}, u32[]{:S(2)}, u32[]{:S(2)}) collective-permute-start(f32[12,40,640]{2,1,0:T(8,128)} %constant_dynamic-update-slice_fusion.refs_8_), channel_id=1, source_target_pairs={{0,1},{1,0},{2,3},{3,2},{4,5},{5,4},{6,7},{7,6},{8,9},{9,8},{10,11... | collective-permute-start | bytes 3686408 | tf_op jit(solution)/shard_map/ppermute | solution.py:334
  68.1 39.4 %collective-permute-start.18 = (f32[12,40,640]{2,1,0:T(8,128)}, f32[12,40,640]{2,1,0:T(8,128)}, u32[]{:S(2)}, u32[]{:S(2)}) collective-permute-start(f32[12,40,640]{2,1,0:T(8,128)} %collective-permute-done.14.refs_9_), channel_id=1, source_target_pairs={{0,1},{1,0},{2,3},{3,2},{4,5},{5,4},{6,7},{7,6},{8,9},{9,8},{10,11... | collective-permute-start | bytes 3686408 | tf_op jit(solution)/shard_map/ppermute | solution.py:334
  70.1 37.5 %collective-permute-start.19 = (f32[12,40,640]{2,1,0:T(8,128)}, f32[12,40,640]{2,1,0:T(8,128)}, u32[]{:S(2)}, u32[]{:S(2)}) collective-permute-start(f32[12,40,640]{2,1,0:T(8,128)} %collective-permute-done.15.refs_10_), channel_id=1, source_target_pairs={{0,1},{1,0},{2,3},{3,2},{4,5},{5,4},{6,7},{7,6},{8,9},{9,8},{10,11... | collective-permute-start | bytes 3686408 | tf_op jit(solution)/shard_map/ppermute | solution.py:334
  97.0 27.0 %collective-permute-start.20 = (f32[12,40,640]{2,1,0:T(8,128)}, f32[12,40,640]{2,1,0:T(8,128)}, u32[]{:S(2)}, u32[]{:S(2)}) collective-permute-start(f32[12,40,640]{2,1,0:T(8,128)} %collective-permute-done.16.refs_11_), channel_id=1, source_target_pairs={{0,1},{1,0},{2,3},{3,2},{4,5},{5,4},{6,7},{7,6},{8,9},{9,8},{10,11... | collective-permute-start | bytes 3686408 | tf_op jit(solution)/shard_map/ppermute | solution.py:334
  100.0 25.2 %copy-start.1 = (bf16[512,384]{1,0:T(8,128)(2,1)S(1)}, bf16[512,384]{1,0:T(8,128)(2,1)}, u32[]{:S(2)}) copy-start(bf16[512,384]{1,0:T(8,128)(2,1)} %copy-done) | copy-start | bytes 1179652
  102.7 10.3 %collective-permute-start.7 = (s16[256,640]{1,0:T(8,128)(2,1)S(1)}, s16[256,640]{1,0:T(8,128)(2,1)S(1)}, u32[]{:S(2)}, u32[]{:S(2)}) collective-permute-start(s16[256,640]{1,0:T(8,128)(2,1)S(1)} %collect.1.refs_0_), channel_id=1, source_target_pairs={{2,0},{3,1},{4,2},{5,3},{6,4},{7,5},{0,6},{1,7},{10,8},{11,9},{12,... | collective-permute-start | bytes 983048 | tf_op jit(solution)/shard_map/ppermute | solution.py:315
  105.3 10.1 %collective-permute-start.8 = (s16[256,640]{1,0:T(8,128)(2,1)S(1)}, s16[256,640]{1,0:T(8,128)(2,1)S(1)}, u32[]{:S(2)}, u32[]{:S(2)}) collective-permute-start(s16[256,640]{1,0:T(8,128)(2,1)S(1)} %collect.1.refs_0_), channel_id=1, source_target_pairs={{4,0},{5,1},{6,2},{7,3},{0,4},{1,5},{2,6},{3,7},{12,8},{13,9},{14,... | collective-permute-start | bytes 983048 | tf_op jit(solution)/shard_map/ppermute | solution.py:315
  107.6 15.9 %collective-permute-start.9 = (s16[256,640]{1,0:T(8,128)(2,1)S(1)}, s16[256,640]{1,0:T(8,128)(2,1)S(1)}, u32[]{:S(2)}, u32[]{:S(2)}) collective-permute-start(s16[256,640]{1,0:T(8,128)(2,1)S(1)} %collect.1.refs_0_), channel_id=1, source_target_pairs={{6,0},{7,1},{0,2},{1,3},{2,4},{3,5},{4,6},{5,7},{14,8},{15,9},{8,1... | collective-permute-start | bytes 983048 | tf_op jit(solution)/shard_map/ppermute | solution.py:315
  107.6 16.4 %collective-permute-start.10 = (s16[256,640]{1,0:T(8,128)(2,1)S(1)}, s16[256,640]{1,0:T(8,128)(2,1)S(1)}, u32[]{:S(2)}, u32[]{:S(2)}) collective-permute-start(s16[256,640]{1,0:T(8,128)(2,1)S(1)} %collect.1.refs_0_), channel_id=1, source_target_pairs={{0,1},{1,0},{2,3},{3,2},{4,5},{5,4},{6,7},{7,6},{8,9},{9,8},{10,11... | collective-permute-start | bytes 983048 | tf_op jit(solution)/shard_map/ppermute | solution.py:334
  113.1 10.9 %collective-permute-start.11 = (s16[256,640]{1,0:T(8,128)(2,1)S(1)}, s16[256,640]{1,0:T(8,128)(2,1)S(1)}, u32[]{:S(2)}, u32[]{:S(2)}) collective-permute-start(s16[256,640]{1,0:T(8,128)(2,1)S(1)} %collective-permute-done.7.refs_1_), channel_id=1, source_target_pairs={{0,1},{1,0},{2,3},{3,2},{4,5},{5,4},{6,7},{7,6},{8,9},{9,8},{10,11... | collective-permute-start | bytes 983048 | tf_op jit(solution)/shard_map/ppermute | solution.py:334
  115.4 8.6 %collective-permute-start.12 = (s16[256,640]{1,0:T(8,128)(2,1)S(1)}, s16[256,640]{1,0:T(8,128)(2,1)S(1)}, u32[]{:S(2)}, u32[]{:S(2)}) collective-permute-start(s16[256,640]{1,0:T(8,128)(2,1)S(1)} %collective-permute-done.8.refs_2_), channel_id=1, source_target_pairs={{0,1},{1,0},{2,3},{3,2},{4,5},{5,4},{6,7},{7,6},{8,9},{9,8},{10,11... | collective-permute-start | bytes 983048 | tf_op jit(solution)/shard_map/ppermute | solution.py:334
  123.5 1.8 %collective-permute-start.13 = (s16[256,640]{1,0:T(8,128)(2,1)S(1)}, s16[256,640]{1,0:T(8,128)(2,1)S(1)}, u32[]{:S(2)}, u32[]{:S(2)}) collective-permute-start(s16[256,640]{1,0:T(8,128)(2,1)S(1)} %collective-permute-done.9.refs_3_), channel_id=1, source_target_pairs={{0,1},{1,0},{2,3},{3,2},{4,5},{5,4},{6,7},{7,6},{8,9},{9,8},{10,11... | collective-permute-start | bytes 983048 | tf_op jit(solution)/shard_map/ppermute | solution.py:334
  (2 other events, 6.8 us)

commit v4 on v3

--- a/solution.py
+++ b/solution.py
@@ -152,21 +152,26 @@
 
     @pl.when(step == pl.num_programs(0) - 1)
     def _():
-        row = lax.broadcasted_iota(jnp.int32, (NOTE, dout), 0)
-        note = jnp.zeros((NOTE, dout), F32)
+        row = lax.broadcasted_iota(jnp.int32, (NOTE, LANES), 0)
+        note = jnp.zeros((NOTE, LANES), F32)
         scaled = []
         for system in range(nsys):
             values = total[system]
             e = exponent(jnp.max(jnp.abs(values), axis=(0, 1), keepdims=True))
             note = jnp.where(row == system, e, note)
             scaled.append(values * jnp.exp2(-e))
-        out_ref[...] = coded(jnp.concatenate(scaled + [note], axis=0))
+        rows = nsys * half
+        for block in range(blocks):
+            lanes = slice(block * LANES, (block + 1) * LANES)
+            values = jnp.concatenate([part[:, lanes] for part in scaled], axis=0)
+            out_ref[block * rows : (block + 1) * rows, :] = coded(values)
+        out_ref[blocks * rows :, :] = coded(note)
 
 
 def collect(parts, nsys, half, dout):
     sources = parts.shape[0]
     block = 8
-    out = (nsys * half + NOTE, dout)
+    out = (nsys * half * (dout // LANES) + NOTE, LANES)
     return pl.pallas_call(
         collect_kernel,
         grid=(sources // block,),
@@ -198,11 +203,15 @@
     @pl.when(step == 0)
     def _():
         for rep, ref in enumerate(sums):
-            note = plain(ref[nsys * rows :, :])
-            values = plain(ref[: nsys * rows, :])
-            for system in range(nsys):
-                by = jnp.exp2(note[system : system + 1])
-                system_sums[rep * nsys + system] = values[system * rows : (system + 1) * rows] * by
+            per_block = nsys * rows
+            by = jnp.exp2(plain(ref[lanes // LANES * per_block :, :]))
+            for block in range(lanes // LANES):
+                to = slice(block * LANES, (block + 1) * LANES)
+                values = plain(ref[block * per_block : (block + 1) * per_block, :])
+                for system in range(nsys):
+                    system_sums[rep * nsys + system, :, to] = (
+                        values[system * rows : (system + 1) * rows] * by[system : system + 1]
+                    )
 
     def of_experts(kind):
         return jnp.concatenate([ref[kind * mine : (kind + 1) * mine] for ref in states], axis=0)
@@ -216,9 +225,11 @@
     grad = (both[:n] + (both[n:] + more)).reshape(-1, group, lanes)
     new_first = 0.9 * of_experts(1) + 0.1 * grad
     new_second = 0.999 * of_experts(2) + 0.001 * grad * grad
-    new_weights = of_experts(0) - 0.01 * (new_first / corr_first) / (
-        jnp.sqrt(new_second / corr_second) + 1e-08
-    )
+    scaled = new_second * (1.0 / corr_second)
+    below = scaled * lax.rsqrt(scaled) + 1e-08
+    inverse = pl.reciprocal(below, approx=True)
+    inverse = inverse * (2.0 - below * inverse)
+    new_weights = of_experts(0) - new_first * (0.01 / corr_first) * inverse
     out_weights[...] = new_weights[:mine]
     out_first[...] = new_first[:mine]
     out_second[...] = new_second[:mine]

time: 139 us -> 139 us (level)
  the two profiles are of different devices: /device:TPU:1 before, /device:TPU:9 now
where the time goes in v4:
time: 139 us; the launch traced here: 137 us
  waiting for transfers between devices  65.2 us (47%)
  starting transfers between devices  41.7 us (30%)
  Pallas kernels  23.5 us (17%)
  local copies, waits for them, and re-layouts  5.16 us (4%)
  between operations  1.54 us (1%)
    ppermute x9, waiting for transfers between devices, everywhere(): return [lax.ppermute(value, axis, pairs) for pairs in moves]  60.9 us
    ppermute x12, starting transfers between devices, all_reps(): return near + [lax.ppermute(part, 'rep', swap) for part in near]  17 us
    ppermute x9, starting transfers between devices, everywhere(): return [lax.ppermute(value, axis, pairs) for pairs in moves]  13.3 us
    all_to_all x1, starting transfers between devices, on_device(): received = lax.all_to_all(parts, 'run', 0, 0, tiled=True)  11.3 us
    pallas_call x1, Pallas kernels, update(): pl.pallas_call(update_kernel, grid=(rows // group,), in_specs=[pl.BlockSp...  9.98 us
    pallas_call x1, Pallas kernels, products(): pl.pallas_call(product_kernel, grid=(rows // block,), in_specs=[pl.BlockS...  9.95 us
    unnamed x11, local copies, waits for them, and re-layouts  4.35 us
  transfers between devices with their start and end apart: 22, of which 8 were waited for; matrix products, arithmetic and copies ran while one was open for 3% of the time, Pallas kernels for 3%

profile of v4, /device:TPU:9, one launch (start us, length us, event | category | flops | bytes accessed | tf_op | source)
XLA Modules:
  0.0 137.1 jit_solution(5462100936641110885)
XLA Ops:
  1.3 10.0 %products.1 = s16[32,416,128]{2,1,0:T(8,128)(2,1)} custom-call(s32[1,1]{1,0:T(1,128)S(6)} %copy.17.count_ref, s32[1,2048]{1,0:T(1,128)} %system_ref.1, bf16[2048,1280]{1,0:T(8,128)(2,1)} %bitcast.8, bf16[2048,640]{1,0:T(8,128)(2,1)} %bitcast.9), custom_call_target="tpu_custom_call" | custom-call | flops 3355443200 | bytes 11141120 | tf_op jit(solution)/shard_map/products/pallas_call | solution.py:111
  11.2 11.3 %all-to-all-start = ((s16[32,416,128]{2,1,0:T(8,128)(2,1)}), s16[32,416,128]{2,1,0:T(8,128)(2,1)S(1)}, u32[]{:S(2)}, u32[]{:S(2)}) async-start(s16[32,416,128]{2,1,0:T(8,128)(2,1)} %products.1), calls=%async_computation | async-start | bytes 6815744 | tf_op jit(solution)/shard_map/all_to_all | solution.py:355
  22.6 2.7 %collective-permute-start = (f32[8,32]{1,0:T(8,128)S(1)}, f32[8,32]{1,0:T(8,128)S(1)}, u32[]{:S(2)}, u32[]{:S(2)}) collective-permute-start(f32[8,32]{1,0:T(8,128)S(1)} %pad.4.refs_0_), channel_id=1, source_target_pairs={{2,0},{3,1},{4,2},{5,3},{6,4},{7,5},{0,6},{1,7},{10,8},{11,9},{12,... | collective-permute-start | bytes 3080 | tf_op jit(solution)/shard_map/ppermute | solution.py:326
  25.3 1.6 %collective-permute-start.1 = (f32[8,32]{1,0:T(8,128)S(1)}, f32[8,32]{1,0:T(8,128)S(1)}, u32[]{:S(2)}, u32[]{:S(2)}) collective-permute-start(f32[8,32]{1,0:T(8,128)S(1)} %pad.4.refs_0_), channel_id=1, source_target_pairs={{4,0},{5,1},{6,2},{7,3},{0,4},{1,5},{2,6},{3,7},{12,8},{13,9},{14,... | collective-permute-start | bytes 3080 | tf_op jit(solution)/shard_map/ppermute | solution.py:326
  26.9 2.7 %collective-permute-start.3 = (f32[8,32]{1,0:T(8,128)S(1)}, f32[8,32]{1,0:T(8,128)S(1)}, u32[]{:S(2)}, u32[]{:S(2)}) collective-permute-start(f32[8,32]{1,0:T(8,128)S(1)} %pad.4.refs_0_), channel_id=1, source_target_pairs={{0,1},{1,0},{2,3},{3,2},{4,5},{5,4},{6,7},{7,6},{8,9},{9,8},{10,11... | collective-permute-start | bytes 3080 | tf_op jit(solution)/shard_map/ppermute | solution.py:345
  29.6 2.1 %collective-permute-start.5 = (f32[8,32]{1,0:T(8,128)S(1)}, f32[8,32]{1,0:T(8,128)S(1)}, u32[]{:S(2)}, u32[]{:S(2)}) collective-permute-start(f32[8,32]{1,0:T(8,128)S(1)} %collective-permute-done.1.refs_2_), channel_id=1, source_target_pairs={{0,1},{1,0},{2,3},{3,2},{4,5},{5,4},{6,7},{7,6},{8,9},{9,8},{10,11... | collective-permute-start | bytes 3080 | tf_op jit(solution)/shard_map/ppermute | solution.py:345
  31.7 1.3 collective-permute-start.6
  35.5 1.8 %constant_dynamic-update-slice_fusion.2 = f32[12,40,640]{2,1,0:T(8,128)} fusion(f32[4,40,640]{2,1,0:T(8,128)} %param.13), kind=kLoop, calls=%fused_computation.2 | loop fusion | bytes 819200
  37.3 1.8 %constant_dynamic-update-slice_fusion.1 = f32[12,40,640]{2,1,0:T(8,128)} fusion(f32[12,40,640]{2,1,0:T(8,128)} %constant_dynamic-update-slice_fusion.2, f32[4,40,640]{2,1,0:T(8,128)} %param.14), kind=kLoop, calls=%fused_computation.1 | loop fusion | bytes 819200
  42.5 26.1 %collective-permute-done.14.refs_9_ = f32[12,40,640]{2,1,0:T(8,128)} collective-permute-done((f32[12,40,640]{2,1,0:T(8,128)}, f32[12,40,640]{2,1,0:T(8,128)}, u32[]{:S(2)}, u32[]{:S(2)}) %collective-permute-start.14) | collective-permute-done | bytes 1228832 | tf_op jit(solution)/shard_map/ppermute | solution.py:326
  68.5 1.9 %collective-permute-start.18 = (f32[12,40,640]{2,1,0:T(8,128)}, f32[12,40,640]{2,1,0:T(8,128)}, u32[]{:S(2)}, u32[]{:S(2)}) collective-permute-start(f32[12,40,640]{2,1,0:T(8,128)} %collective-permute-done.14.refs_9_), channel_id=1, source_target_pairs={{0,1},{1,0},{2,3},{3,2},{4,5},{5,4},{6,7},{7,6},{8,9},{9,8},{10,11... | collective-permute-start | bytes 3686408 | tf_op jit(solution)/shard_map/ppermute | solution.py:345
  70.8 2.2 %collective-permute-start.19 = (f32[12,40,640]{2,1,0:T(8,128)}, f32[12,40,640]{2,1,0:T(8,128)}, u32[]{:S(2)}, u32[]{:S(2)}) collective-permute-start(f32[12,40,640]{2,1,0:T(8,128)} %collective-permute-done.15.refs_10_), channel_id=1, source_target_pairs={{0,1},{1,0},{2,3},{3,2},{4,5},{5,4},{6,7},{7,6},{8,9},{9,8},{10,11... | collective-permute-start | bytes 3686408 | tf_op jit(solution)/shard_map/ppermute | solution.py:345
  72.9 24.9 %collective-permute-done.16.refs_11_ = f32[12,40,640]{2,1,0:T(8,128)} collective-permute-done((f32[12,40,640]{2,1,0:T(8,128)}, f32[12,40,640]{2,1,0:T(8,128)}, u32[]{:S(2)}, u32[]{:S(2)}) %collective-permute-start.16) | collective-permute-done | bytes 1228832 | tf_op jit(solution)/shard_map/ppermute | solution.py:326
  98.3 2.3 %all-to-all-done.parts_ref = s16[32,416,128]{2,1,0:T(8,128)(2,1)S(1)} async-done(((s16[32,416,128]{2,1,0:T(8,128)(2,1)}), s16[32,416,128]{2,1,0:T(8,128)(2,1)S(1)}, u32[]{:S(2)}, u32[]{:S(2)}) %all-to-all-start) | async-done | bytes 3407904 | tf_op jit(solution)/shard_map/all_to_all | solution.py:355
  100.6 2.7 %collect.1.refs_0_ = s16[1216,128]{1,0:T(8,128)(2,1)S(1)} custom-call(s16[32,416,128]{2,1,0:T(8,128)(2,1)S(1)} %all-to-all-done.parts_ref), custom_call_target="tpu_custom_call" | custom-call | flops 3407872 | bytes 3407872 | tf_op jit(solution)/shard_map/collect/pallas_call | solution.py:175
  103.3 2.1 %collective-permute-start.7 = (s16[1216,128]{1,0:T(8,128)(2,1)S(1)}, s16[1216,128]{1,0:T(8,128)(2,1)S(1)}, u32[]{:S(2)}, u32[]{:S(2)}) collective-permute-start(s16[1216,128]{1,0:T(8,128)(2,1)S(1)} %collect.1.refs_0_), channel_id=1, source_target_pairs={{2,0},{3,1},{4,2},{5,3},{6,4},{7,5},{0,6},{1,7},{10,8},{11,9},{12,... | collective-permute-start | bytes 933896 | tf_op jit(solution)/shard_map/ppermute | solution.py:326
  105.5 5.3 %collective-permute-start.8 = (s16[1216,128]{1,0:T(8,128)(2,1)S(1)}, s16[1216,128]{1,0:T(8,128)(2,1)S(1)}, u32[]{:S(2)}, u32[]{:S(2)}) collective-permute-start(s16[1216,128]{1,0:T(8,128)(2,1)S(1)} %collect.1.refs_0_), channel_id=1, source_target_pairs={{4,0},{5,1},{6,2},{7,3},{0,4},{1,5},{2,6},{3,7},{12,8},{13,9},{14,... | collective-permute-start | bytes 933896 | tf_op jit(solution)/shard_map/ppermute | solution.py:326
  110.8 1.1 collective-permute-start.10
  111.9 4.4 %collective-permute-done.7.refs_1_ = s16[1216,128]{1,0:T(8,128)(2,1)S(1)} collective-permute-done((s16[1216,128]{1,0:T(8,128)(2,1)S(1)}, s16[1216,128]{1,0:T(8,128)(2,1)S(1)}, u32[]{:S(2)}, u32[]{:S(2)}) %collective-permute-start.7) | collective-permute-done | bytes 311328 | tf_op jit(solution)/shard_map/ppermute | solution.py:326
  116.3 1.6 %collective-permute-start.11 = (s16[1216,128]{1,0:T(8,128)(2,1)S(1)}, s16[1216,128]{1,0:T(8,128)(2,1)S(1)}, u32[]{:S(2)}, u32[]{:S(2)}) collective-permute-start(s16[1216,128]{1,0:T(8,128)(2,1)S(1)} %collective-permute-done.7.refs_1_), channel_id=1, source_target_pairs={{0,1},{1,0},{2,3},{3,2},{4,5},{5,4},{6,7},{7,6},{8,9},{9,8},{10,11... | collective-permute-start | bytes 933896 | tf_op jit(solution)/shard_map/ppermute | solution.py:345
  117.9 2.1 %collective-permute-start.12 = (s16[1216,128]{1,0:T(8,128)(2,1)S(1)}, s16[1216,128]{1,0:T(8,128)(2,1)S(1)}, u32[]{:S(2)}, u32[]{:S(2)}) collective-permute-start(s16[1216,128]{1,0:T(8,128)(2,1)S(1)} %collective-permute-done.8.refs_2_), channel_id=1, source_target_pairs={{0,1},{1,0},{2,3},{3,2},{4,5},{5,4},{6,7},{7,6},{8,9},{9,8},{10,11... | collective-permute-start | bytes 933896 | tf_op jit(solution)/shard_map/ppermute | solution.py:345
  120.0 5.2 %collective-permute-done.9.refs_3_ = s16[1216,128]{1,0:T(8,128)(2,1)S(1)} collective-permute-done((s16[1216,128]{1,0:T(8,128)(2,1)S(1)}, s16[1216,128]{1,0:T(8,128)(2,1)S(1)}, u32[]{:S(2)}, u32[]{:S(2)}) %collective-permute-start.9) | collective-permute-done | bytes 311328 | tf_op jit(solution)/shard_map/ppermute | solution.py:326
  125.8 1.2 collective-permute-done.13.refs_7_
  127.0 10.0 %update.1 = (f32[4,40,640]{2,1,0:T(8,128)}, f32[4,40,640]{2,1,0:T(8,128)}, f32[4,40,640]{2,1,0:T(8,128)}, bf16[6,40,640]{2,1,0:T(8,128)(2,1)}) custom-call(bf16[512,384]{1,0:T(8,128)(2,1)S(1)} %copy-done.1, bf16[96,256]{1,0:T(8,128)(2,1)S(1)} %get-tuple-element.18.merge_ref, s16[1216,128]{1,0:T(8,128)(2,1)S(1)} %collect.1.refs_0_, ...), custom_call_target="tpu_custom_call" | custom-call | tf_op jit(solution)/shard_map/update/pallas_call | solution.py:251
  (37 shorter events, 7.1 us)
Async XLA Ops:
  11.2 11.4 %copy-start.3 = (f32[1,6,32]{2,0,1:T(1,128)S(1)}, f32[1,6,32]{2,0,1:T(1,128)}, u32[]{:S(2)}) copy-start(f32[1,6,32]{2,0,1:T(1,128)} %param.12) | copy-start | bytes 2308
  11.2 89.4 %all-to-all-start = ((s16[32,416,128]{2,1,0:T(8,128)(2,1)}), s16[32,416,128]{2,1,0:T(8,128)(2,1)S(1)}, u32[]{:S(2)}, u32[]{:S(2)}) async-start(s16[32,416,128]{2,1,0:T(8,128)(2,1)} %products.1), calls=%async_computation | async-start | bytes 6815744 | tf_op jit(solution)/shard_map/all_to_all | solution.py:355
  22.6 7.0 %collective-permute-start = (f32[8,32]{1,0:T(8,128)S(1)}, f32[8,32]{1,0:T(8,128)S(1)}, u32[]{:S(2)}, u32[]{:S(2)}) collective-permute-start(f32[8,32]{1,0:T(8,128)S(1)} %pad.4.refs_0_), channel_id=1, source_target_pairs={{2,0},{3,1},{4,2},{5,3},{6,4},{7,5},{0,6},{1,7},{10,8},{11,9},{12,... | collective-permute-start | bytes 3080 | tf_op jit(solution)/shard_map/ppermute | solution.py:326
  25.3 4.3 %collective-permute-start.1 = (f32[8,32]{1,0:T(8,128)S(1)}, f32[8,32]{1,0:T(8,128)S(1)}, u32[]{:S(2)}, u32[]{:S(2)}) collective-permute-start(f32[8,32]{1,0:T(8,128)S(1)} %pad.4.refs_0_), channel_id=1, source_target_pairs={{4,0},{5,1},{6,2},{7,3},{0,4},{1,5},{2,6},{3,7},{12,8},{13,9},{14,... | collective-permute-start | bytes 3080 | tf_op jit(solution)/shard_map/ppermute | solution.py:326
  26.9 4.8 %collective-permute-start.2 = (f32[8,32]{1,0:T(8,128)S(1)}, f32[8,32]{1,0:T(8,128)S(1)}, u32[]{:S(2)}, u32[]{:S(2)}) collective-permute-start(f32[8,32]{1,0:T(8,128)S(1)} %pad.4.refs_0_), channel_id=1, source_target_pairs={{6,0},{7,1},{0,2},{1,3},{2,4},{3,5},{4,6},{5,7},{14,8},{15,9},{8,1... | collective-permute-start | bytes 3080 | tf_op jit(solution)/shard_map/ppermute | solution.py:326
  26.9 6.2 %collective-permute-start.3 = (f32[8,32]{1,0:T(8,128)S(1)}, f32[8,32]{1,0:T(8,128)S(1)}, u32[]{:S(2)}, u32[]{:S(2)}) collective-permute-start(f32[8,32]{1,0:T(8,128)S(1)} %pad.4.refs_0_), channel_id=1, source_target_pairs={{0,1},{1,0},{2,3},{3,2},{4,5},{5,4},{6,7},{7,6},{8,9},{9,8},{10,11... | collective-permute-start | bytes 3080 | tf_op jit(solution)/shard_map/ppermute | solution.py:345
  29.6 3.5 %collective-permute-start.4 = (f32[8,32]{1,0:T(8,128)S(1)}, f32[8,32]{1,0:T(8,128)S(1)}, u32[]{:S(2)}, u32[]{:S(2)}) collective-permute-start(f32[8,32]{1,0:T(8,128)S(1)} %collective-permute-done.refs_1_), channel_id=1, source_target_pairs={{0,1},{1,0},{2,3},{3,2},{4,5},{5,4},{6,7},{7,6},{8,9},{9,8},{10,11... | collective-permute-start | bytes 3080 | tf_op jit(solution)/shard_map/ppermute | solution.py:345
  29.6 3.5 %collective-permute-start.5 = (f32[8,32]{1,0:T(8,128)S(1)}, f32[8,32]{1,0:T(8,128)S(1)}, u32[]{:S(2)}, u32[]{:S(2)}) collective-permute-start(f32[8,32]{1,0:T(8,128)S(1)} %collective-permute-done.1.refs_2_), channel_id=1, source_target_pairs={{0,1},{1,0},{2,3},{3,2},{4,5},{5,4},{6,7},{7,6},{8,9},{9,8},{10,11... | collective-permute-start | bytes 3080 | tf_op jit(solution)/shard_map/ppermute | solution.py:345
  31.7 2.2 %collective-permute-start.6 = (f32[8,32]{1,0:T(8,128)S(1)}, f32[8,32]{1,0:T(8,128)S(1)}, u32[]{:S(2)}, u32[]{:S(2)}) collective-permute-start(f32[8,32]{1,0:T(8,128)S(1)} %collective-permute-done.2.refs_3_), channel_id=1, source_target_pairs={{0,1},{1,0},{2,3},{3,2},{4,5},{5,4},{6,7},{7,6},{8,9},{9,8},{10,11... | collective-permute-start | bytes 3080 | tf_op jit(solution)/shard_map/ppermute | solution.py:345
  39.9 28.6 %collective-permute-start.14 = (f32[12,40,640]{2,1,0:T(8,128)}, f32[12,40,640]{2,1,0:T(8,128)}, u32[]{:S(2)}, u32[]{:S(2)}) collective-permute-start(f32[12,40,640]{2,1,0:T(8,128)} %constant_dynamic-update-slice_fusion.refs_8_), channel_id=1, source_target_pairs={{2,0},{3,1},{4,2},{5,3},{6,4},{7,5},{0,6},{1,7},{10,8},{11,9},{12,... | collective-permute-start | bytes 3686408 | tf_op jit(solution)/shard_map/ppermute | solution.py:326
  40.8 30.0 %collective-permute-start.15 = (f32[12,40,640]{2,1,0:T(8,128)}, f32[12,40,640]{2,1,0:T(8,128)}, u32[]{:S(2)}, u32[]{:S(2)}) collective-permute-start(f32[12,40,640]{2,1,0:T(8,128)} %constant_dynamic-update-slice_fusion.refs_8_), channel_id=1, source_target_pairs={{4,0},{5,1},{6,2},{7,3},{0,4},{1,5},{2,6},{3,7},{12,8},{13,9},{14,... | collective-permute-start | bytes 3686408 | tf_op jit(solution)/shard_map/ppermute | solution.py:326
  41.6 56.3 %collective-permute-start.16 = (f32[12,40,640]{2,1,0:T(8,128)}, f32[12,40,640]{2,1,0:T(8,128)}, u32[]{:S(2)}, u32[]{:S(2)}) collective-permute-start(f32[12,40,640]{2,1,0:T(8,128)} %constant_dynamic-update-slice_fusion.refs_8_), channel_id=1, source_target_pairs={{6,0},{7,1},{0,2},{1,3},{2,4},{3,5},{4,6},{5,7},{14,8},{15,9},{8,1... | collective-permute-start | bytes 3686408 | tf_op jit(solution)/shard_map/ppermute | solution.py:326
  41.6 63.9 %collective-permute-start.17 = (f32[12,40,640]{2,1,0:T(8,128)}, f32[12,40,640]{2,1,0:T(8,128)}, u32[]{:S(2)}, u32[]{:S(2)}) collective-permute-start(f32[12,40,640]{2,1,0:T(8,128)} %constant_dynamic-update-slice_fusion.refs_8_), channel_id=1, source_target_pairs={{0,1},{1,0},{2,3},{3,2},{4,5},{5,4},{6,7},{7,6},{8,9},{9,8},{10,11... | collective-permute-start | bytes 3686408 | tf_op jit(solution)/shard_map/ppermute | solution.py:345
  68.5 42.3 %collective-permute-start.18 = (f32[12,40,640]{2,1,0:T(8,128)}, f32[12,40,640]{2,1,0:T(8,128)}, u32[]{:S(2)}, u32[]{:S(2)}) collective-permute-start(f32[12,40,640]{2,1,0:T(8,128)} %collective-permute-done.14.refs_9_), channel_id=1, source_target_pairs={{0,1},{1,0},{2,3},{3,2},{4,5},{5,4},{6,7},{7,6},{8,9},{9,8},{10,11... | collective-permute-start | bytes 3686408 | tf_op jit(solution)/shard_map/ppermute | solution.py:345
  70.8 40.0 %collective-permute-start.19 = (f32[12,40,640]{2,1,0:T(8,128)}, f32[12,40,640]{2,1,0:T(8,128)}, u32[]{:S(2)}, u32[]{:S(2)}) collective-permute-start(f32[12,40,640]{2,1,0:T(8,128)} %collective-permute-done.15.refs_10_), channel_id=1, source_target_pairs={{0,1},{1,0},{2,3},{3,2},{4,5},{5,4},{6,7},{7,6},{8,9},{9,8},{10,11... | collective-permute-start | bytes 3686408 | tf_op jit(solution)/shard_map/ppermute | solution.py:345
  97.9 27.9 %collective-permute-start.20 = (f32[12,40,640]{2,1,0:T(8,128)}, f32[12,40,640]{2,1,0:T(8,128)}, u32[]{:S(2)}, u32[]{:S(2)}) collective-permute-start(f32[12,40,640]{2,1,0:T(8,128)} %collective-permute-done.16.refs_11_), channel_id=1, source_target_pairs={{0,1},{1,0},{2,3},{3,2},{4,5},{5,4},{6,7},{7,6},{8,9},{9,8},{10,11... | collective-permute-start | bytes 3686408 | tf_op jit(solution)/shard_map/ppermute | solution.py:345
  100.6 26.4 %copy-start.1 = (bf16[512,384]{1,0:T(8,128)(2,1)S(1)}, bf16[512,384]{1,0:T(8,128)(2,1)}, u32[]{:S(2)}) copy-start(bf16[512,384]{1,0:T(8,128)(2,1)} %copy-done) | copy-start | bytes 1179652
  103.3 13.0 %collective-permute-start.7 = (s16[1216,128]{1,0:T(8,128)(2,1)S(1)}, s16[1216,128]{1,0:T(8,128)(2,1)S(1)}, u32[]{:S(2)}, u32[]{:S(2)}) collective-permute-start(s16[1216,128]{1,0:T(8,128)(2,1)S(1)} %collect.1.refs_0_), channel_id=1, source_target_pairs={{2,0},{3,1},{4,2},{5,3},{6,4},{7,5},{0,6},{1,7},{10,8},{11,9},{12,... | collective-permute-start | bytes 933896 | tf_op jit(solution)/shard_map/ppermute | solution.py:326
  105.5 12.4 %collective-permute-start.8 = (s16[1216,128]{1,0:T(8,128)(2,1)S(1)}, s16[1216,128]{1,0:T(8,128)(2,1)S(1)}, u32[]{:S(2)}, u32[]{:S(2)}) collective-permute-start(s16[1216,128]{1,0:T(8,128)(2,1)S(1)} %collect.1.refs_0_), channel_id=1, source_target_pairs={{4,0},{5,1},{6,2},{7,3},{0,4},{1,5},{2,6},{3,7},{12,8},{13,9},{14,... | collective-permute-start | bytes 933896 | tf_op jit(solution)/shard_map/ppermute | solution.py:326
  110.8 14.5 %collective-permute-start.9 = (s16[1216,128]{1,0:T(8,128)(2,1)S(1)}, s16[1216,128]{1,0:T(8,128)(2,1)S(1)}, u32[]{:S(2)}, u32[]{:S(2)}) collective-permute-start(s16[1216,128]{1,0:T(8,128)(2,1)S(1)} %collect.1.refs_0_), channel_id=1, source_target_pairs={{6,0},{7,1},{0,2},{1,3},{2,4},{3,5},{4,6},{5,7},{14,8},{15,9},{8,1... | collective-permute-start | bytes 933896 | tf_op jit(solution)/shard_map/ppermute | solution.py:326
  110.8 15.0 %collective-permute-start.10 = (s16[1216,128]{1,0:T(8,128)(2,1)S(1)}, s16[1216,128]{1,0:T(8,128)(2,1)S(1)}, u32[]{:S(2)}, u32[]{:S(2)}) collective-permute-start(s16[1216,128]{1,0:T(8,128)(2,1)S(1)} %collect.1.refs_0_), channel_id=1, source_target_pairs={{0,1},{1,0},{2,3},{3,2},{4,5},{5,4},{6,7},{7,6},{8,9},{9,8},{10,11... | collective-permute-start | bytes 933896 | tf_op jit(solution)/shard_map/ppermute | solution.py:345
  116.3 9.4 %collective-permute-start.11 = (s16[1216,128]{1,0:T(8,128)(2,1)S(1)}, s16[1216,128]{1,0:T(8,128)(2,1)S(1)}, u32[]{:S(2)}, u32[]{:S(2)}) collective-permute-start(s16[1216,128]{1,0:T(8,128)(2,1)S(1)} %collective-permute-done.7.refs_1_), channel_id=1, source_target_pairs={{0,1},{1,0},{2,3},{3,2},{4,5},{5,4},{6,7},{7,6},{8,9},{9,8},{10,11... | collective-permute-start | bytes 933896 | tf_op jit(solution)/shard_map/ppermute | solution.py:345
  117.9 7.9 %collective-permute-start.12 = (s16[1216,128]{1,0:T(8,128)(2,1)S(1)}, s16[1216,128]{1,0:T(8,128)(2,1)S(1)}, u32[]{:S(2)}, u32[]{:S(2)}) collective-permute-start(s16[1216,128]{1,0:T(8,128)(2,1)S(1)} %collective-permute-done.8.refs_2_), channel_id=1, source_target_pairs={{0,1},{1,0},{2,3},{3,2},{4,5},{5,4},{6,7},{7,6},{8,9},{9,8},{10,11... | collective-permute-start | bytes 933896 | tf_op jit(solution)/shard_map/ppermute | solution.py:345
  125.3 1.7 %collective-permute-start.13 = (s16[1216,128]{1,0:T(8,128)(2,1)S(1)}, s16[1216,128]{1,0:T(8,128)(2,1)S(1)}, u32[]{:S(2)}, u32[]{:S(2)}) collective-permute-start(s16[1216,128]{1,0:T(8,128)(2,1)S(1)} %collective-permute-done.9.refs_3_), channel_id=1, source_target_pairs={{0,1},{1,0},{2,3},{3,2},{4,5},{5,4},{6,7},{7,6},{8,9},{9,8},{10,11... | collective-permute-start | bytes 933896 | tf_op jit(solution)/shard_map/ppermute | solution.py:345
  (2 other events, 6.8 us)

commit v5 on v4

--- a/solution.py
+++ b/solution.py
@@ -187,15 +187,39 @@
     )(parts)
 
 
+def hold_kernel(*refs):
+    states, held_ref, sems = refs[:-2], refs[-2], refs[-1]
+    copies = [
+        pltpu.make_async_copy(ref, held_ref.at[k], sems.at[k]) for k, ref in enumerate(states)
+    ]
+    for copy in copies:
+        copy.start()
+    for copy in copies:
+        copy.wait()
+
+
+def hold(states):
+    shape = (len(states),) + states[0].shape
+    return pl.pallas_call(
+        hold_kernel,
+        in_specs=[pl.BlockSpec(memory_space=pl.ANY)] * len(states),
+        out_specs=pl.BlockSpec(memory_space=pltpu.VMEM),
+        out_shape=pltpu.VMEM(shape, F32),
+        scratch_shapes=[pltpu.SemaphoreType.DMA((len(states),))],
+        compiler_params=pltpu.CompilerParams(vmem_limit_bytes=4 * MIB),
+        name="hold",
+    )(*states)
+
+
 def update_kernel(mix_ref, merge_ref, *refs):
-    sums = refs[:8]
-    states = refs[8:16]
-    out_weights, out_first, out_second, out_merged = refs[16:20]
-    system_sums, merged = refs[20:22]
+    sums, states = refs[:8], refs[8]
+    out_weights, out_first, out_second, out_merged, system_sums, merged = refs[9:]
     step = pl.program_id(0)
     mine, group, lanes = out_weights.shape
     nsys, rows, _ = merged.shape
-    n = group * mine * len(states)
+    reps = states.shape[0]
+    n = group * mine * reps
+    at = pl.ds(pl.multiple_of(step * group, group), group)
     m = group * nsys
     corr_first = 1.0 - 0.9**10
     corr_second = 1.0 - 0.999**10
@@ -214,9 +238,8 @@
                     )
 
     def of_experts(kind):
-        return jnp.concatenate([ref[kind * mine : (kind + 1) * mine] for ref in states], axis=0)
-
-    at = pl.ds(pl.multiple_of(step * group, group), group)
+        return states[:, kind * mine : (kind + 1) * mine, at, :].reshape(-1, group, lanes)
+
     right = system_sums[:, at, :].reshape(-1, lanes)
     near = right.astype(BF16)
     rest = (right - near.astype(F32)).astype(BF16)
@@ -243,7 +266,7 @@
 
 
 def update(mix, merge, sums, states, nsys):
-    mine, rows, dout = states[0].shape
+    reps, mine, rows, dout = states.shape
     mine = mine // 3
     group = 8
     whole = lambda g: (0, 0)
@@ -252,7 +275,7 @@
         update_kernel,
         grid=(rows // group,),
         in_specs=[pl.BlockSpec(a.shape, whole) for a in [mix, merge] + sums]
-        + [pl.BlockSpec((3 * mine, group, dout), some)] * 8,
+        + [pl.BlockSpec(memory_space=pltpu.VMEM)],
         out_specs=[pl.BlockSpec((mine, group, dout), some)] * 3
         + [pl.BlockSpec((nsys, rows, dout), lambda g: (0, 0, 0))],
         out_shape=[jax.ShapeDtypeStruct((mine, rows, dout), F32)] * 3
@@ -263,7 +286,7 @@
         ],
         compiler_params=pltpu.CompilerParams(vmem_limit_bytes=32 * MIB),
         name="update",
-    )(mix, merge, *sums, *states)
+    )(mix, merge, *sums, states)
 
 
 def prepare_kernel(rep_ref, *refs):
@@ -353,7 +376,11 @@
 
     parts = products(edge_count, edge_system, edge_feats[0], edge_grads[0], owners)
     received = lax.all_to_all(parts, "run", 0, 0, tiled=True)
-    sums = all_reps(collect(received, nsys, weights.shape[1], weights.shape[2]))
+    sums = collect(received, nsys, weights.shape[1], weights.shape[2])
+    near = [sums] + everywhere(sums, "rep", along_x)
+    *states, after = lax.optimization_barrier((*states, sums))
+    states, after = lax.optimization_barrier((hold(states), after))
+    sums = near + [lax.ppermute(part, "rep", swap) for part in [after] + near[1:]]
     new_weights, new_first, new_second, merged = update(mix, merge, sums, states, nsys)
     return (new_weights, new_first, new_second, merged[None])
 

time: 139 us -> 134 us (0.964)
  the two profiles are of different devices: /device:TPU:9 before, /device:TPU:1 now
where the time goes in v5:
time: 134 us; the launch traced here: 132 us
  waiting for transfers between devices  57.7 us (43%)
  starting transfers between devices  42.7 us (32%)
  Pallas kernels  25 us (19%)
  local copies, waits for them, and re-layouts  5.16 us (4%)
  between operations  1.54 us (1%)
    ppermute x9, waiting for transfers between devices, everywhere(): return [lax.ppermute(value, axis, pairs) for pairs in moves]  52.5 us
    ppermute x9, starting transfers between devices, everywhere(): return [lax.ppermute(value, axis, pairs) for pairs in moves]  13.3 us
    all_to_all x1, starting transfers between devices, on_device(): received = lax.all_to_all(parts, 'run', 0, 0, tiled=True)  13.2 us
    pallas_call x1, Pallas kernels, products(): pl.pallas_call(product_kernel, grid=(rows // block,), in_specs=[pl.BlockS...  9.95 us
    ppermute x4, starting transfers between devices, on_device(): lax.ppermute(part, 'rep', swap)  8.73 us
    pallas_call x1, Pallas kernels, update(): pl.pallas_call(update_kernel, grid=(rows // group,), in_specs=[pl.BlockSp...  7.59 us
    ppermute x8, starting transfers between devices, all_reps(): return near + [lax.ppermute(part, 'rep', swap) for part in near]  7.4 us
    unnamed x11, local copies, waits for them, and re-layouts  4.35 us
  transfers between devices with their start and end apart: 22, of which 8 were waited for; matrix products, arithmetic and copies ran while one was open for 3% of the time, Pallas kernels for 6%

profile of v5, /device:TPU:1, one launch (start us, length us, event | category | flops | bytes accessed | tf_op | source)
XLA Modules:
  0.0 132.1 jit_solution(17794788349138842698)
XLA Ops:
  1.3 10.0 %products.1 = s16[32,416,128]{2,1,0:T(8,128)(2,1)} custom-call(s32[1,1]{1,0:T(1,128)S(6)} %copy.17.count_ref, s32[1,2048]{1,0:T(1,128)} %system_ref.1, bf16[2048,1280]{1,0:T(8,128)(2,1)} %bitcast.8, bf16[2048,640]{1,0:T(8,128)(2,1)} %bitcast.9), custom_call_target="tpu_custom_call" | custom-call | flops 3355443200 | bytes 11141120 | tf_op jit(solution)/shard_map/products/pallas_call | solution.py:111
  11.2 13.2 %all-to-all-start = ((s16[32,416,128]{2,1,0:T(8,128)(2,1)}), s16[32,416,128]{2,1,0:T(8,128)(2,1)S(1)}, u32[]{:S(2)}, u32[]{:S(2)}) async-start(s16[32,416,128]{2,1,0:T(8,128)(2,1)} %products.1), calls=%async_computation | async-start | bytes 6815744 | tf_op jit(solution)/shard_map/all_to_all | solution.py:378
  24.5 1.5 %collective-permute-start.2 = (f32[8,32]{1,0:T(8,128)S(1)}, f32[8,32]{1,0:T(8,128)S(1)}, u32[]{:S(2)}, u32[]{:S(2)}) collective-permute-start(f32[8,32]{1,0:T(8,128)S(1)} %pad.4.refs_0_), channel_id=1, source_target_pairs={{6,0},{7,1},{0,2},{1,3},{2,4},{3,5},{4,6},{5,7},{14,8},{15,9},{8,1... | collective-permute-start | bytes 3080 | tf_op jit(solution)/shard_map/ppermute | solution.py:349
  26.0 1.4 %collective-permute-start.1 = (f32[8,32]{1,0:T(8,128)S(1)}, f32[8,32]{1,0:T(8,128)S(1)}, u32[]{:S(2)}, u32[]{:S(2)}) collective-permute-start(f32[8,32]{1,0:T(8,128)S(1)} %pad.4.refs_0_), channel_id=1, source_target_pairs={{4,0},{5,1},{6,2},{7,3},{0,4},{1,5},{2,6},{3,7},{12,8},{13,9},{14,... | collective-permute-start | bytes 3080 | tf_op jit(solution)/shard_map/ppermute | solution.py:349
  27.4 2.0 %collective-permute-start = (f32[8,32]{1,0:T(8,128)S(1)}, f32[8,32]{1,0:T(8,128)S(1)}, u32[]{:S(2)}, u32[]{:S(2)}) collective-permute-start(f32[8,32]{1,0:T(8,128)S(1)} %pad.4.refs_0_), channel_id=1, source_target_pairs={{2,0},{3,1},{4,2},{5,3},{6,4},{7,5},{0,6},{1,7},{10,8},{11,9},{12,... | collective-permute-start | bytes 3080 | tf_op jit(solution)/shard_map/ppermute | solution.py:349
  29.4 2.3 %collective-permute-start.3 = (f32[8,32]{1,0:T(8,128)S(1)}, f32[8,32]{1,0:T(8,128)S(1)}, u32[]{:S(2)}, u32[]{:S(2)}) collective-permute-start(f32[8,32]{1,0:T(8,128)S(1)} %pad.4.refs_0_), channel_id=1, source_target_pairs={{0,1},{1,0},{2,3},{3,2},{4,5},{5,4},{6,7},{7,6},{8,9},{9,8},{10,11... | collective-permute-start | bytes 3080 | tf_op jit(solution)/shard_map/ppermute | solution.py:368
  32.2 1.4 %collective-permute-start.4 = (f32[8,32]{1,0:T(8,128)S(1)}, f32[8,32]{1,0:T(8,128)S(1)}, u32[]{:S(2)}, u32[]{:S(2)}) collective-permute-start(f32[8,32]{1,0:T(8,128)S(1)} %collective-permute-done.refs_1_), channel_id=1, source_target_pairs={{0,1},{1,0},{2,3},{3,2},{4,5},{5,4},{6,7},{7,6},{8,9},{9,8},{10,11... | collective-permute-start | bytes 3080 | tf_op jit(solution)/shard_map/ppermute | solution.py:368
  36.0 1.8 %constant_dynamic-update-slice_fusion.2 = f32[12,40,640]{2,1,0:T(8,128)} fusion(f32[4,40,640]{2,1,0:T(8,128)} %param.13), kind=kLoop, calls=%fused_computation.2 | loop fusion | bytes 819200
  37.8 1.8 %constant_dynamic-update-slice_fusion.1 = f32[12,40,640]{2,1,0:T(8,128)} fusion(f32[12,40,640]{2,1,0:T(8,128)} %constant_dynamic-update-slice_fusion.2, f32[4,40,640]{2,1,0:T(8,128)} %param.14), kind=kLoop, calls=%fused_computation.1 | loop fusion | bytes 819200
  41.0 3.2 %collective-permute-start.11 = (f32[12,40,640]{2,1,0:T(8,128)}, f32[12,40,640]{2,1,0:T(8,128)}, u32[]{:S(2)}, u32[]{:S(2)}) collective-permute-start(f32[12,40,640]{2,1,0:T(8,128)} %constant_dynamic-update-slice_fusion.refs_0_), channel_id=1, source_target_pairs={{4,0},{5,1},{6,2},{7,3},{0,4},{1,5},{2,6},{3,7},{12,8},{13,9},{14,... | collective-permute-start | bytes 3686408 | tf_op jit(solution)/shard_map/ppermute | solution.py:349
  44.3 0.9 collective-permute-start.13
  45.2 25.1 %collective-permute-done.12.refs_3_ = f32[12,40,640]{2,1,0:T(8,128)} collective-permute-done((f32[12,40,640]{2,1,0:T(8,128)}, f32[12,40,640]{2,1,0:T(8,128)}, u32[]{:S(2)}, u32[]{:S(2)}) %collective-permute-start.12) | collective-permute-done | bytes 1228832 | tf_op jit(solution)/shard_map/ppermute | solution.py:349
  70.2 1.2 collective-permute-start.16
  71.4 26.3 %collective-permute-done.11.refs_2_ = f32[12,40,640]{2,1,0:T(8,128)} collective-permute-done((f32[12,40,640]{2,1,0:T(8,128)}, f32[12,40,640]{2,1,0:T(8,128)}, u32[]{:S(2)}, u32[]{:S(2)}) %collective-permute-start.11) | collective-permute-done | bytes 1228832 | tf_op jit(solution)/shard_map/ppermute | solution.py:349
  97.7 1.2 collective-permute-start.15
  98.9 2.9 %all-to-all-done.parts_ref = s16[32,416,128]{2,1,0:T(8,128)(2,1)S(1)} async-done(((s16[32,416,128]{2,1,0:T(8,128)(2,1)}), s16[32,416,128]{2,1,0:T(8,128)(2,1)S(1)}, u32[]{:S(2)}, u32[]{:S(2)}) %all-to-all-start) | async-done | bytes 3407904 | tf_op jit(solution)/shard_map/all_to_all | solution.py:378
  101.8 2.6 %collect.1.refs_0_ = s16[1216,128]{1,0:T(8,128)(2,1)S(1)} custom-call(s16[32,416,128]{2,1,0:T(8,128)(2,1)S(1)} %all-to-all-done.parts_ref), custom_call_target="tpu_custom_call" | custom-call | flops 3407872 | bytes 3407872 | tf_op jit(solution)/shard_map/collect/pallas_call | solution.py:175
  104.5 2.1 %collective-permute-start.9 = (s16[1216,128]{1,0:T(8,128)(2,1)S(1)}, s16[1216,128]{1,0:T(8,128)(2,1)S(1)}, u32[]{:S(2)}, u32[]{:S(2)}) collective-permute-start(s16[1216,128]{1,0:T(8,128)(2,1)S(1)} %collect.1.refs_0_), channel_id=1, source_target_pairs={{6,0},{7,1},{0,2},{1,3},{2,4},{3,5},{4,6},{5,7},{14,8},{15,9},{8,1... | collective-permute-start | bytes 933896 | tf_op jit(solution)/shard_map/ppermute | solution.py:349
  106.6 2.5 %collective-permute-start.7 = (s16[1216,128]{1,0:T(8,128)(2,1)S(1)}, s16[1216,128]{1,0:T(8,128)(2,1)S(1)}, u32[]{:S(2)}, u32[]{:S(2)}) collective-permute-start(s16[1216,128]{1,0:T(8,128)(2,1)S(1)} %collect.1.refs_0_), channel_id=1, source_target_pairs={{2,0},{3,1},{4,2},{5,3},{6,4},{7,5},{0,6},{1,7},{10,8},{11,9},{12,... | collective-permute-start | bytes 933896 | tf_op jit(solution)/shard_map/ppermute | solution.py:349
  109.1 3.9 %hold.1.refs_8_ = f32[8,12,40,640]{3,2,1,0:T(8,128)S(1)} custom-call(f32[12,40,640]{2,1,0:T(8,128)} %constant_dynamic-update-slice_fusion.refs_0_, f32[12,40,640]{2,1,0:T(8,128)} %collective-permute-done.10.refs_1_, f32[12,40,640]{2,1,0:T(8,128)} %collective-permute-done.11.refs_2_, f32[12,40,640]{2,1,0:T(8,128)} %collective-permute-done.12.refs_3_, ...), custom_call_target="tpu_custom_call" | custom-call | tf_op jit(solution)/shard_map/hold/pallas_call | solution.py:203
  113.0 2.7 %collective-permute-start.17 = (s16[1216,128]{1,0:T(8,128)(2,1)S(1)}, s16[1216,128]{1,0:T(8,128)(2,1)S(1)}, u32[]{:S(2)}, u32[]{:S(2)}) collective-permute-start(s16[1216,128]{1,0:T(8,128)(2,1)S(1)} %collect.1.refs_0_), channel_id=1, source_target_pairs={{0,1},{1,0},{2,3},{3,2},{4,5},{5,4},{6,7},{7,6},{8,9},{9,8},{10,11... | collective-permute-start | bytes 933896 | tf_op jit(solution)/shard_map/ppermute | solution.py:383
  115.6 1.1 collective-permute-done.9.refs_3_
  116.8 5.4 %collective-permute-start.20 = (s16[1216,128]{1,0:T(8,128)(2,1)S(1)}, s16[1216,128]{1,0:T(8,128)(2,1)S(1)}, u32[]{:S(2)}, u32[]{:S(2)}) collective-permute-start(s16[1216,128]{1,0:T(8,128)(2,1)S(1)} %collective-permute-done.9.refs_3_), channel_id=1, source_target_pairs={{0,1},{1,0},{2,3},{3,2},{4,5},{5,4},{6,7},{7,6},{8,9},{9,8},{10,11... | collective-permute-start | bytes 933896 | tf_op jit(solution)/shard_map/ppermute | solution.py:383
  124.3 7.6 %update.1 = (f32[4,40,640]{2,1,0:T(8,128)}, f32[4,40,640]{2,1,0:T(8,128)}, f32[4,40,640]{2,1,0:T(8,128)}, bf16[6,40,640]{2,1,0:T(8,128)(2,1)}) custom-call(bf16[512,384]{1,0:T(8,128)(2,1)S(1)} %copy-done.1, bf16[96,256]{1,0:T(8,128)(2,1)S(1)} %get-tuple-element.29.merge_ref, s16[1216,128]{1,0:T(8,128)(2,1)S(1)} %collect.1.refs_0_, ...), custom_call_target="tpu_custom_call" | custom-call | tf_op jit(solution)/shard_map/update/pallas_call | solution.py:274
  (38 shorter events, 6.5 us)
Async XLA Ops:
  11.2 13.2 %copy-start.3 = (f32[1,6,32]{2,0,1:T(1,128)S(1)}, f32[1,6,32]{2,0,1:T(1,128)}, u32[]{:S(2)}) copy-start(f32[1,6,32]{2,0,1:T(1,128)} %param.12) | copy-start | bytes 2308
  11.2 90.6 %all-to-all-start = ((s16[32,416,128]{2,1,0:T(8,128)(2,1)}), s16[32,416,128]{2,1,0:T(8,128)(2,1)S(1)}, u32[]{:S(2)}, u32[]{:S(2)}) async-start(s16[32,416,128]{2,1,0:T(8,128)(2,1)} %products.1), calls=%async_computation | async-start | bytes 6815744 | tf_op jit(solution)/shard_map/all_to_all | solution.py:378
  24.5 7.2 %collective-permute-start.2 = (f32[8,32]{1,0:T(8,128)S(1)}, f32[8,32]{1,0:T(8,128)S(1)}, u32[]{:S(2)}, u32[]{:S(2)}) collective-permute-start(f32[8,32]{1,0:T(8,128)S(1)} %pad.4.refs_0_), channel_id=1, source_target_pairs={{6,0},{7,1},{0,2},{1,3},{2,4},{3,5},{4,6},{5,7},{14,8},{15,9},{8,1... | collective-permute-start | bytes 3080 | tf_op jit(solution)/shard_map/ppermute | solution.py:349
  26.0 5.7 %collective-permute-start.1 = (f32[8,32]{1,0:T(8,128)S(1)}, f32[8,32]{1,0:T(8,128)S(1)}, u32[]{:S(2)}, u32[]{:S(2)}) collective-permute-start(f32[8,32]{1,0:T(8,128)S(1)} %pad.4.refs_0_), channel_id=1, source_target_pairs={{4,0},{5,1},{6,2},{7,3},{0,4},{1,5},{2,6},{3,7},{12,8},{13,9},{14,... | collective-permute-start | bytes 3080 | tf_op jit(solution)/shard_map/ppermute | solution.py:349
  27.4 4.8 %collective-permute-start = (f32[8,32]{1,0:T(8,128)S(1)}, f32[8,32]{1,0:T(8,128)S(1)}, u32[]{:S(2)}, u32[]{:S(2)}) collective-permute-start(f32[8,32]{1,0:T(8,128)S(1)} %pad.4.refs_0_), channel_id=1, source_target_pairs={{2,0},{3,1},{4,2},{5,3},{6,4},{7,5},{0,6},{1,7},{10,8},{11,9},{12,... | collective-permute-start | bytes 3080 | tf_op jit(solution)/shard_map/ppermute | solution.py:349
  29.4 4.2 %collective-permute-start.3 = (f32[8,32]{1,0:T(8,128)S(1)}, f32[8,32]{1,0:T(8,128)S(1)}, u32[]{:S(2)}, u32[]{:S(2)}) collective-permute-start(f32[8,32]{1,0:T(8,128)S(1)} %pad.4.refs_0_), channel_id=1, source_target_pairs={{0,1},{1,0},{2,3},{3,2},{4,5},{5,4},{6,7},{7,6},{8,9},{9,8},{10,11... | collective-permute-start | bytes 3080 | tf_op jit(solution)/shard_map/ppermute | solution.py:368
  31.7 1.9 %collective-permute-start.6 = (f32[8,32]{1,0:T(8,128)S(1)}, f32[8,32]{1,0:T(8,128)S(1)}, u32[]{:S(2)}, u32[]{:S(2)}) collective-permute-start(f32[8,32]{1,0:T(8,128)S(1)} %collective-permute-done.2.refs_3_), channel_id=1, source_target_pairs={{0,1},{1,0},{2,3},{3,2},{4,5},{5,4},{6,7},{7,6},{8,9},{9,8},{10,11... | collective-permute-start | bytes 3080 | tf_op jit(solution)/shard_map/ppermute | solution.py:368
  31.7 1.9 %collective-permute-start.5 = (f32[8,32]{1,0:T(8,128)S(1)}, f32[8,32]{1,0:T(8,128)S(1)}, u32[]{:S(2)}, u32[]{:S(2)}) collective-permute-start(f32[8,32]{1,0:T(8,128)S(1)} %collective-permute-done.1.refs_2_), channel_id=1, source_target_pairs={{0,1},{1,0},{2,3},{3,2},{4,5},{5,4},{6,7},{7,6},{8,9},{9,8},{10,11... | collective-permute-start | bytes 3080 | tf_op jit(solution)/shard_map/ppermute | solution.py:368
  32.2 2.2 %collective-permute-start.4 = (f32[8,32]{1,0:T(8,128)S(1)}, f32[8,32]{1,0:T(8,128)S(1)}, u32[]{:S(2)}, u32[]{:S(2)}) collective-permute-start(f32[8,32]{1,0:T(8,128)S(1)} %collective-permute-done.refs_1_), channel_id=1, source_target_pairs={{0,1},{1,0},{2,3},{3,2},{4,5},{5,4},{6,7},{7,6},{8,9},{9,8},{10,11... | collective-permute-start | bytes 3080 | tf_op jit(solution)/shard_map/ppermute | solution.py:368
  40.4 29.8 %collective-permute-start.12 = (f32[12,40,640]{2,1,0:T(8,128)}, f32[12,40,640]{2,1,0:T(8,128)}, u32[]{:S(2)}, u32[]{:S(2)}) collective-permute-start(f32[12,40,640]{2,1,0:T(8,128)} %constant_dynamic-update-slice_fusion.refs_0_), channel_id=1, source_target_pairs={{6,0},{7,1},{0,2},{1,3},{2,4},{3,5},{4,6},{5,7},{14,8},{15,9},{8,1... | collective-permute-start | bytes 3686408 | tf_op jit(solution)/shard_map/ppermute | solution.py:349
  41.0 56.7 %collective-permute-start.11 = (f32[12,40,640]{2,1,0:T(8,128)}, f32[12,40,640]{2,1,0:T(8,128)}, u32[]{:S(2)}, u32[]{:S(2)}) collective-permute-start(f32[12,40,640]{2,1,0:T(8,128)} %constant_dynamic-update-slice_fusion.refs_0_), channel_id=1, source_target_pairs={{4,0},{5,1},{6,2},{7,3},{0,4},{1,5},{2,6},{3,7},{12,8},{13,9},{14,... | collective-permute-start | bytes 3686408 | tf_op jit(solution)/shard_map/ppermute | solution.py:349
  44.3 54.6 %collective-permute-start.10 = (f32[12,40,640]{2,1,0:T(8,128)}, f32[12,40,640]{2,1,0:T(8,128)}, u32[]{:S(2)}, u32[]{:S(2)}) collective-permute-start(f32[12,40,640]{2,1,0:T(8,128)} %constant_dynamic-update-slice_fusion.refs_0_), channel_id=1, source_target_pairs={{2,0},{3,1},{4,2},{5,3},{6,4},{7,5},{0,6},{1,7},{10,8},{11,9},{12,... | collective-permute-start | bytes 3686408 | tf_op jit(solution)/shard_map/ppermute | solution.py:349
  44.3 62.3 %collective-permute-start.13 = (f32[12,40,640]{2,1,0:T(8,128)}, f32[12,40,640]{2,1,0:T(8,128)}, u32[]{:S(2)}, u32[]{:S(2)}) collective-permute-start(f32[12,40,640]{2,1,0:T(8,128)} %constant_dynamic-update-slice_fusion.refs_0_), channel_id=1, source_target_pairs={{0,1},{1,0},{2,3},{3,2},{4,5},{5,4},{6,7},{7,6},{8,9},{9,8},{10,11... | collective-permute-start | bytes 3686408 | tf_op jit(solution)/shard_map/ppermute | solution.py:368
  70.2 36.3 %collective-permute-start.16 = (f32[12,40,640]{2,1,0:T(8,128)}, f32[12,40,640]{2,1,0:T(8,128)}, u32[]{:S(2)}, u32[]{:S(2)}) collective-permute-start(f32[12,40,640]{2,1,0:T(8,128)} %collective-permute-done.12.refs_3_), channel_id=1, source_target_pairs={{0,1},{1,0},{2,3},{3,2},{4,5},{5,4},{6,7},{7,6},{8,9},{9,8},{10,11... | collective-permute-start | bytes 3686408 | tf_op jit(solution)/shard_map/ppermute | solution.py:368
  97.7 11.4 %collective-permute-start.15 = (f32[12,40,640]{2,1,0:T(8,128)}, f32[12,40,640]{2,1,0:T(8,128)}, u32[]{:S(2)}, u32[]{:S(2)}) collective-permute-start(f32[12,40,640]{2,1,0:T(8,128)} %collective-permute-done.11.refs_2_), channel_id=1, source_target_pairs={{0,1},{1,0},{2,3},{3,2},{4,5},{5,4},{6,7},{7,6},{8,9},{9,8},{10,11... | collective-permute-start | bytes 3686408 | tf_op jit(solution)/shard_map/ppermute | solution.py:368
  98.9 10.2 %collective-permute-start.14 = (f32[12,40,640]{2,1,0:T(8,128)}, f32[12,40,640]{2,1,0:T(8,128)}, u32[]{:S(2)}, u32[]{:S(2)}) collective-permute-start(f32[12,40,640]{2,1,0:T(8,128)} %collective-permute-done.10.refs_1_), channel_id=1, source_target_pairs={{0,1},{1,0},{2,3},{3,2},{4,5},{5,4},{6,7},{7,6},{8,9},{9,8},{10,11... | collective-permute-start | bytes 3686408 | tf_op jit(solution)/shard_map/ppermute | solution.py:368
  104.5 19.9 %copy-start.1 = (bf16[512,384]{1,0:T(8,128)(2,1)S(1)}, bf16[512,384]{1,0:T(8,128)(2,1)}, u32[]{:S(2)}) copy-start(bf16[512,384]{1,0:T(8,128)(2,1)} %copy-done) | copy-start | bytes 1179652
  104.5 12.3 %collective-permute-start.9 = (s16[1216,128]{1,0:T(8,128)(2,1)S(1)}, s16[1216,128]{1,0:T(8,128)(2,1)S(1)}, u32[]{:S(2)}, u32[]{:S(2)}) collective-permute-start(s16[1216,128]{1,0:T(8,128)(2,1)S(1)} %collect.1.refs_0_), channel_id=1, source_target_pairs={{6,0},{7,1},{0,2},{1,3},{2,4},{3,5},{4,6},{5,7},{14,8},{15,9},{8,1... | collective-permute-start | bytes 933896 | tf_op jit(solution)/shard_map/ppermute | solution.py:349
  106.6 15.7 %collective-permute-start.8 = (s16[1216,128]{1,0:T(8,128)(2,1)S(1)}, s16[1216,128]{1,0:T(8,128)(2,1)S(1)}, u32[]{:S(2)}, u32[]{:S(2)}) collective-permute-start(s16[1216,128]{1,0:T(8,128)(2,1)S(1)} %collect.1.refs_0_), channel_id=1, source_target_pairs={{4,0},{5,1},{6,2},{7,3},{0,4},{1,5},{2,6},{3,7},{12,8},{13,9},{14,... | collective-permute-start | bytes 933896 | tf_op jit(solution)/shard_map/ppermute | solution.py:349
  106.6 15.7 %collective-permute-start.7 = (s16[1216,128]{1,0:T(8,128)(2,1)S(1)}, s16[1216,128]{1,0:T(8,128)(2,1)S(1)}, u32[]{:S(2)}, u32[]{:S(2)}) collective-permute-start(s16[1216,128]{1,0:T(8,128)(2,1)S(1)} %collect.1.refs_0_), channel_id=1, source_target_pairs={{2,0},{3,1},{4,2},{5,3},{6,4},{7,5},{0,6},{1,7},{10,8},{11,9},{12,... | collective-permute-start | bytes 933896 | tf_op jit(solution)/shard_map/ppermute | solution.py:349
  113.0 9.9 %collective-permute-start.17 = (s16[1216,128]{1,0:T(8,128)(2,1)S(1)}, s16[1216,128]{1,0:T(8,128)(2,1)S(1)}, u32[]{:S(2)}, u32[]{:S(2)}) collective-permute-start(s16[1216,128]{1,0:T(8,128)(2,1)S(1)} %collect.1.refs_0_), channel_id=1, source_target_pairs={{0,1},{1,0},{2,3},{3,2},{4,5},{5,4},{6,7},{7,6},{8,9},{9,8},{10,11... | collective-permute-start | bytes 933896 | tf_op jit(solution)/shard_map/ppermute | solution.py:383
  116.8 6.7 %collective-permute-start.20 = (s16[1216,128]{1,0:T(8,128)(2,1)S(1)}, s16[1216,128]{1,0:T(8,128)(2,1)S(1)}, u32[]{:S(2)}, u32[]{:S(2)}) collective-permute-start(s16[1216,128]{1,0:T(8,128)(2,1)S(1)} %collective-permute-done.9.refs_3_), channel_id=1, source_target_pairs={{0,1},{1,0},{2,3},{3,2},{4,5},{5,4},{6,7},{7,6},{8,9},{9,8},{10,11... | collective-permute-start | bytes 933896 | tf_op jit(solution)/shard_map/ppermute | solution.py:383
  122.2 1.7 %collective-permute-start.19 = (s16[1216,128]{1,0:T(8,128)(2,1)S(1)}, s16[1216,128]{1,0:T(8,128)(2,1)S(1)}, u32[]{:S(2)}, u32[]{:S(2)}) collective-permute-start(s16[1216,128]{1,0:T(8,128)(2,1)S(1)} %collective-permute-done.8.refs_2_), channel_id=1, source_target_pairs={{0,1},{1,0},{2,3},{3,2},{4,5},{5,4},{6,7},{7,6},{8,9},{9,8},{10,11... | collective-permute-start | bytes 933896 | tf_op jit(solution)/shard_map/ppermute | solution.py:383
  122.2 2.1 %collective-permute-start.18 = (s16[1216,128]{1,0:T(8,128)(2,1)S(1)}, s16[1216,128]{1,0:T(8,128)(2,1)S(1)}, u32[]{:S(2)}, u32[]{:S(2)}) collective-permute-start(s16[1216,128]{1,0:T(8,128)(2,1)S(1)} %collective-permute-done.7.refs_1_), channel_id=1, source_target_pairs={{0,1},{1,0},{2,3},{3,2},{4,5},{5,4},{6,7},{7,6},{8,9},{9,8},{10,11... | collective-permute-start | bytes 933896 | tf_op jit(solution)/shard_map/ppermute | solution.py:383
  (2 other events, 6.8 us)

commit v6 on v5

--- a/solution.py
+++ b/solution.py
@@ -211,9 +211,55 @@
     )(*states)
 
 
+def unpack(sums, system_sums):
+    nsys = system_sums.shape[0] // len(sums)
+    rows, lanes = system_sums.shape[1:]
+    per_block = nsys * rows
+    for rep, ref in enumerate(sums):
+        by = jnp.exp2(plain(ref[lanes // LANES * per_block :, :]))
+        for block in range(lanes // LANES):
+            to = slice(block * LANES, (block + 1) * LANES)
+            values = plain(ref[block * per_block : (block + 1) * per_block, :])
+            for system in range(nsys):
+                system_sums[rep * nsys + system, :, to] = (
+                    values[system * rows : (system + 1) * rows] * by[system : system + 1]
+                )
+
+
+def mixed(mix_ref, right):
+    n = mix_ref.shape[0] // 2
+    near = right.astype(BF16)
+    rest = (right - near.astype(F32)).astype(BF16)
+    both = jnp.dot(mix_ref[...], near, preferred_element_type=F32)
+    more = jnp.dot(mix_ref[:n, :], rest, preferred_element_type=F32)
+    return both[:n] + (both[n:] + more)
+
+
+def begin_kernel(mix_ref, *refs):
+    sums, out_ref, system_sums = refs[:-2], refs[-2], refs[-1]
+    _, rows, lanes = out_ref.shape
+    unpack(sums, system_sums)
+    for row in range(0, rows, 8):
+        right = system_sums[:, row : row + 8, :].reshape(-1, lanes)
+        out_ref[:, row : row + 8, :] = mixed(mix_ref, right).reshape(-1, 8, lanes)
+
+
+def begin(mix, sums, nsys, rows, dout):
+    vmem = pl.BlockSpec(memory_space=pltpu.VMEM)
+    return pl.pallas_call(
+        begin_kernel,
+        in_specs=[vmem] * (1 + len(sums)),
+        out_specs=vmem,
+        out_shape=pltpu.VMEM((mix.shape[0] // 16, rows, dout), F32),
+        scratch_shapes=[pltpu.VMEM((len(sums) * nsys, rows, dout), F32)],
+        compiler_params=pltpu.CompilerParams(vmem_limit_bytes=14 * MIB),
+        name="begin",
+    )(mix, *sums)
+
+
 def update_kernel(mix_ref, merge_ref, *refs):
-    sums, states = refs[:8], refs[8]
-    out_weights, out_first, out_second, out_merged, system_sums, merged = refs[9:]
+    *sums, states, begun = refs[:-6]
+    out_weights, out_first, out_second, out_merged, system_sums, merged = refs[-6:]
     step = pl.program_id(0)
     mine, group, lanes = out_weights.shape
     nsys, rows, _ = merged.shape
@@ -226,26 +272,13 @@
 
     @pl.when(step == 0)
     def _():
-        for rep, ref in enumerate(sums):
-            per_block = nsys * rows
-            by = jnp.exp2(plain(ref[lanes // LANES * per_block :, :]))
-            for block in range(lanes // LANES):
-                to = slice(block * LANES, (block + 1) * LANES)
-                values = plain(ref[block * per_block : (block + 1) * per_block, :])
-                for system in range(nsys):
-                    system_sums[rep * nsys + system, :, to] = (
-                        values[system * rows : (system + 1) * rows] * by[system : system + 1]
-                    )
+        unpack(sums, system_sums)
 
     def of_experts(kind):
         return states[:, kind * mine : (kind + 1) * mine, at, :].reshape(-1, group, lanes)
 
     right = system_sums[:, at, :].reshape(-1, lanes)
-    near = right.astype(BF16)
-    rest = (right - near.astype(F32)).astype(BF16)
-    both = jnp.dot(mix_ref[...], near, preferred_element_type=F32)
-    more = jnp.dot(mix_ref[:n, :], rest, preferred_element_type=F32)
-    grad = (both[:n] + (both[n:] + more)).reshape(-1, group, lanes)
+    grad = begun[:, at, :] + mixed(mix_ref, right).reshape(-1, group, lanes)
     new_first = 0.9 * of_experts(1) + 0.1 * grad
     new_second = 0.999 * of_experts(2) + 0.001 * grad * grad
     scaled = new_second * (1.0 / corr_second)
@@ -265,7 +298,7 @@
         out_merged[...] = merged[...].astype(BF16)
 
 
-def update(mix, merge, sums, states, nsys):
+def update(mix, merge, sums, states, begun, nsys):
     reps, mine, rows, dout = states.shape
     mine = mine // 3
     group = 8
@@ -275,26 +308,27 @@
         update_kernel,
         grid=(rows // group,),
         in_specs=[pl.BlockSpec(a.shape, whole) for a in [mix, merge] + sums]
-        + [pl.BlockSpec(memory_space=pltpu.VMEM)],
+        + [pl.BlockSpec(memory_space=pltpu.VMEM)] * 2,
         out_specs=[pl.BlockSpec((mine, group, dout), some)] * 3
         + [pl.BlockSpec((nsys, rows, dout), lambda g: (0, 0, 0))],
         out_shape=[jax.ShapeDtypeStruct((mine, rows, dout), F32)] * 3
         + [jax.ShapeDtypeStruct((nsys, rows, dout), BF16)],
         scratch_shapes=[
-            pltpu.VMEM((8 * nsys, rows, dout), F32),
+            pltpu.VMEM((len(sums) * nsys, rows, dout), F32),
             pltpu.VMEM((nsys, rows, dout), F32),
         ],
         compiler_params=pltpu.CompilerParams(vmem_limit_bytes=32 * MIB),
         name="update",
-    )(mix, merge, *sums, states)
+    )(mix, merge, *sums, states, begun)
 
 
 def prepare_kernel(rep_ref, *refs):
-    coefs, (mix_ref, merge_ref) = refs[:-2], refs[-2:]
+    coefs, (first_ref, mix_ref, merge_ref) = refs[:-3], refs[-3:]
     reps, chips = len(coefs), len(coefs) // 2
     padded, experts = coefs[0].shape
     rows = mix_ref.shape[0] // 2
-    columns = mix_ref.shape[1]
+    begun = first_ref.shape[1]
+    columns = begun + mix_ref.shape[1]
     out_rows = merge_ref.shape[0] // 2
     nsys = out_rows // 8
     mine = experts // reps
@@ -323,21 +357,24 @@
     for k, part in enumerate((near, rest)):
         wide = lax.dot_general(at_expert, part, transposed, preferred_element_type=F32)
         wide = jnp.dot(wide.astype(BF16), at_system, preferred_element_type=F32)
-        mix_ref[k * rows : (k + 1) * rows, :] = jnp.where(same_mix, wide, 0.0).astype(BF16)
+        wide = jnp.where(same_mix, wide, 0.0)
+        first_ref[k * rows : (k + 1) * rows, :] = wide[:, :begun].astype(BF16)
+        mix_ref[k * rows : (k + 1) * rows, :] = wide[:, begun:].astype(BF16)
         own = jnp.dot(at_out, part[:padded], preferred_element_type=F32)
         own = lax.dot_general(own.astype(BF16), at_expert, transposed, preferred_element_type=F32)
         merge_ref[k * out_rows : (k + 1) * out_rows, :] = jnp.where(same_merge, own, 0.0).astype(BF16)
 
 
-def prepare(rep, coefs, nsys):
+def prepare(rep, coefs, nsys, begun):
     reps, experts = len(coefs), coefs[0].shape[1]
     vmem = pl.BlockSpec(memory_space=pltpu.VMEM)
     return pl.pallas_call(
         prepare_kernel,
         in_specs=[pl.BlockSpec(memory_space=pltpu.SMEM)] + [vmem] * reps,
-        out_specs=[vmem, vmem],
+        out_specs=[vmem] * 3,
         out_shape=[
-            jax.ShapeDtypeStruct((2 * 8 * experts, 8 * reps * nsys), BF16),
+            jax.ShapeDtypeStruct((2 * 8 * experts, 8 * begun * nsys), BF16),
+            jax.ShapeDtypeStruct((2 * 8 * experts, 8 * (reps - begun) * nsys), BF16),
             jax.ShapeDtypeStruct((2 * 8 * nsys, 8 * experts), BF16),
         ],
         compiler_params=pltpu.CompilerParams(vmem_limit_bytes=12 * MIB),
@@ -368,9 +405,12 @@
         return near + [lax.ppermute(part, "rep", swap) for part in near]
 
     coefs = all_reps(jnp.pad(coef[0], ((0, -nsys % 8), (0, 0))))
-    mix, merge = prepare(lax.axis_index("rep").reshape(1), coefs, nsys)
-    mix, merge, *state_parts = lax.optimization_barrier(
-        (mix, merge, weights, first_moment, second_moment)
+    early = [0, chips, chips - 1]
+    late = [k for k in range(reps) if k not in early]
+    in_turn = [coefs[k] for k in early + late]
+    first_mix, mix, merge = prepare(lax.axis_index("rep").reshape(1), in_turn, nsys, len(early))
+    first_mix, mix, merge, *state_parts = lax.optimization_barrier(
+        (first_mix, mix, merge, weights, first_moment, second_moment)
     )
     states = all_reps(jnp.concatenate(state_parts, axis=0))
 
@@ -379,9 +419,17 @@
     sums = collect(received, nsys, weights.shape[1], weights.shape[2])
     near = [sums] + everywhere(sums, "rep", along_x)
     *states, after = lax.optimization_barrier((*states, sums))
-    states, after = lax.optimization_barrier((hold(states), after))
-    sums = near + [lax.ppermute(part, "rep", swap) for part in [after] + near[1:]]
-    new_weights, new_first, new_second, merged = update(mix, merge, sums, states, nsys)
+    swapped = [lax.ppermute(sums, "rep", swap)] + [None] * (chips - 1)
+    states, last = lax.optimization_barrier((hold(states), near[chips - 1]))
+    swapped[chips - 1] = lax.ppermute(last, "rep", swap)
+    begun = begin(first_mix, [sums, swapped[0], last], nsys, *weights.shape[1:])
+    begun, near[chips - 2] = lax.optimization_barrier((begun, near[chips - 2]))
+    for k in range(chips - 2, 0, -1):
+        swapped[k] = lax.ppermute(near[k], "rep", swap)
+    sums = near + swapped
+    new_weights, new_first, new_second, merged = update(
+        mix, merge, [sums[k] for k in late], states, begun, nsys
+    )
     return (new_weights, new_first, new_second, merged[None])
 
 

time: 134 us -> 135 us (level)
  waiting for transfers between devices: 57.7 us -> 60.6 us
  starting transfers between devices: 42.7 us -> 40.8 us
    ppermute x9, waiting for transfers between devices: 52.5 us -> 58.1 us  [everywhere(): return [lax.ppermute(value, axis, pairs) for pairs in moves]]
    all_to_all x1, waiting for transfers between devices: 2.92 us -> 0.01 us  [on_device(): received = lax.all_to_all(parts, 'run', 0, 0, tiled=True)]
    ppermute x4, starting transfers between devices: 8.73 us -> 6.63 us  [the longest x1 3.53 us: on_device(): swapped = [lax.ppermute(sums, 'rep', swap)] + [None] * (chips - 1)]
    ppermute x8, starting transfers between devices: 7.4 us -> 9.49 us  [all_reps(): return near + [lax.ppermute(part, 'rep', swap) for part in near]]
    pallas_call x0 -> x1, Pallas kernels: none -> 1.69 us  [begin(): pl.pallas_call(begin_kernel, in_specs=[vmem] * (1 + len(sums)), out_specs...]
    pallas_call x1, Pallas kernels: 7.59 us -> 6.12 us  [update(): pl.pallas_call(update_kernel, grid=(rows // group,), in_specs=[pl.BlockSp...]
    unnamed x11 -> x15, local copies, waits for them, and re-layouts: 4.35 us -> 4.43 us
  transfers between devices with their start and end apart: 22 -> 22, of which waited for: 8 -> 5; matrix products, arithmetic and copies ran while one was open for 3% -> 3% of each run, Pallas kernels for 6% -> 7%
where the time goes in v6:
time: 135 us; the launch traced here: 133 us
  waiting for transfers between devices  60.6 us (45%)
  starting transfers between devices  40.8 us (30%)
  Pallas kernels  25.1 us (19%)
  local copies, waits for them, and re-layouts  5.22 us (4%)
  between operations  1.57 us (1%)
    ppermute x9, waiting for transfers between devices, everywhere(): return [lax.ppermute(value, axis, pairs) for pairs in moves]  58.1 us
    ppermute x9, starting transfers between devices, everywhere(): return [lax.ppermute(value, axis, pairs) for pairs in moves]  12.5 us
    all_to_all x1, starting transfers between devices, on_device(): received = lax.all_to_all(parts, 'run', 0, 0, tiled=True)  12.2 us
    pallas_call x1, Pallas kernels, products(): pl.pallas_call(product_kernel, grid=(rows // block,), in_specs=[pl.BlockS...  9.96 us
    ppermute x8, starting transfers between devices, all_reps(): return near + [lax.ppermute(part, 'rep', swap) for part in near]  9.49 us
    pallas_call x1, Pallas kernels, update(): pl.pallas_call(update_kernel, grid=(rows // group,), in_specs=[pl.BlockSp...  6.12 us
    unnamed x15, local copies, waits for them, and re-layouts  4.43 us
    pallas_call x1, Pallas kernels, hold(): pl.pallas_call(hold_kernel, in_specs=[pl.BlockSpec(memory_space=pl.ANY)]...  3.9 us
  transfers between devices with their start and end apart: 22, of which 5 were waited for; matrix products, arithmetic and copies ran while one was open for 3% of the time, Pallas kernels for 7%

profile of v6, /device:TPU:1, one launch (start us, length us, event | category | flops | bytes accessed | tf_op | source)
XLA Modules:
  0.0 133.3 jit_solution(12330046121118474644)
XLA Ops:
  1.3 10.0 %products.1 = s16[32,416,128]{2,1,0:T(8,128)(2,1)} custom-call(s32[1,1]{1,0:T(1,128)S(6)} %copy.17.count_ref, s32[1,2048]{1,0:T(1,128)} %system_ref.1, bf16[2048,1280]{1,0:T(8,128)(2,1)} %bitcast.8, bf16[2048,640]{1,0:T(8,128)(2,1)} %bitcast.9), custom_call_target="tpu_custom_call" | custom-call | flops 3355443200 | bytes 11141120 | tf_op jit(solution)/shard_map/products/pallas_call | solution.py:111
  11.2 12.2 %all-to-all-start = ((s16[32,416,128]{2,1,0:T(8,128)(2,1)}), s16[32,416,128]{2,1,0:T(8,128)(2,1)S(1)}, u32[]{:S(2)}, u32[]{:S(2)}) async-start(s16[32,416,128]{2,1,0:T(8,128)(2,1)} %products.1), calls=%async_computation | async-start | bytes 6815744 | tf_op jit(solution)/shard_map/all_to_all | solution.py:418
  23.4 3.5 %collective-permute-start.3 = (f32[8,32]{1,0:T(8,128)S(1)}, f32[8,32]{1,0:T(8,128)S(1)}, u32[]{:S(2)}, u32[]{:S(2)}) collective-permute-start(f32[8,32]{1,0:T(8,128)S(1)} %pad.4.refs_0_), channel_id=1, source_target_pairs={{4,0},{5,1},{6,2},{7,3},{0,4},{1,5},{2,6},{3,7},{12,8},{13,9},{14,... | collective-permute-start | bytes 3080 | tf_op jit(solution)/shard_map/ppermute | solution.py:386
  27.2 1.2 collective-permute-start.1
  28.4 2.0 %collective-permute-start = (f32[8,32]{1,0:T(8,128)S(1)}, f32[8,32]{1,0:T(8,128)S(1)}, u32[]{:S(2)}, u32[]{:S(2)}) collective-permute-start(f32[8,32]{1,0:T(8,128)S(1)} %pad.4.refs_0_), channel_id=1, source_target_pairs={{0,1},{1,0},{2,3},{3,2},{4,5},{5,4},{6,7},{7,6},{8,9},{9,8},{10,11... | collective-permute-start | bytes 3080 | tf_op jit(solution)/shard_map/ppermute | solution.py:405
  30.5 1.2 collective-permute-start.4
  31.7 3.5 %collective-permute-start.6 = (f32[8,32]{1,0:T(8,128)S(1)}, f32[8,32]{1,0:T(8,128)S(1)}, u32[]{:S(2)}, u32[]{:S(2)}) collective-permute-start(f32[8,32]{1,0:T(8,128)S(1)} %collective-permute-done.1.refs_2_), channel_id=1, source_target_pairs={{0,1},{1,0},{2,3},{3,2},{4,5},{5,4},{6,7},{7,6},{8,9},{9,8},{10,11... | collective-permute-start | bytes 3080 | tf_op jit(solution)/shard_map/ppermute | solution.py:405
  36.0 0.9 prepare.1
  37.6 1.9 %constant_dynamic-update-slice_fusion.2 = f32[12,40,640]{2,1,0:T(8,128)} fusion(f32[4,40,640]{2,1,0:T(8,128)} %param.13), kind=kLoop, calls=%fused_computation.2 | loop fusion | bytes 819200
  39.5 1.8 %constant_dynamic-update-slice_fusion.1 = f32[12,40,640]{2,1,0:T(8,128)} fusion(f32[12,40,640]{2,1,0:T(8,128)} %constant_dynamic-update-slice_fusion.2, f32[4,40,640]{2,1,0:T(8,128)} %param.14), kind=kLoop, calls=%fused_computation.1 | loop fusion | bytes 819200
  42.1 1.2 collective-permute-start.10
  43.4 1.4 %collective-permute-start.9 = (f32[12,40,640]{2,1,0:T(8,128)}, f32[12,40,640]{2,1,0:T(8,128)}, u32[]{:S(2)}, u32[]{:S(2)}) collective-permute-start(f32[12,40,640]{2,1,0:T(8,128)} %constant_dynamic-update-slice_fusion.refs_0_), channel_id=1, source_target_pairs={{2,0},{3,1},{4,2},{5,3},{6,4},{7,5},{0,6},{1,7},{10,8},{11,9},{12,... | collective-permute-start | bytes 3686408 | tf_op jit(solution)/shard_map/ppermute | solution.py:386
  44.8 0.9 collective-permute-start.12
  45.7 52.5 %collective-permute-done.11.refs_3_ = f32[12,40,640]{2,1,0:T(8,128)} collective-permute-done((f32[12,40,640]{2,1,0:T(8,128)}, f32[12,40,640]{2,1,0:T(8,128)}, u32[]{:S(2)}, u32[]{:S(2)}) %collective-permute-start.11) | collective-permute-done | bytes 1228832 | tf_op jit(solution)/shard_map/ppermute | solution.py:386
  98.2 1.2 collective-permute-start.15
  100.0 2.6 %collect.1.refs_0_ = s16[1216,128]{1,0:T(8,128)(2,1)S(1)} custom-call(s16[32,416,128]{2,1,0:T(8,128)(2,1)S(1)} %all-to-all-done.parts_ref), custom_call_target="tpu_custom_call" | custom-call | flops 3407872 | bytes 3407872 | tf_op jit(solution)/shard_map/collect/pallas_call | solution.py:175
  102.9 3.5 %collective-permute-start.8 = (s16[1216,128]{1,0:T(8,128)(2,1)S(1)}, s16[1216,128]{1,0:T(8,128)(2,1)S(1)}, u32[]{:S(2)}, u32[]{:S(2)}) collective-permute-start(s16[1216,128]{1,0:T(8,128)(2,1)S(1)} %collect.1.refs_0_), channel_id=1, source_target_pairs={{0,1},{1,0},{2,3},{3,2},{4,5},{5,4},{6,7},{7,6},{8,9},{9,8},{10,11... | collective-permute-start | bytes 933896 | tf_op jit(solution)/shard_map/ppermute | solution.py:422
  106.4 4.7 %collective-permute-start.17 = (s16[1216,128]{1,0:T(8,128)(2,1)S(1)}, s16[1216,128]{1,0:T(8,128)(2,1)S(1)}, u32[]{:S(2)}, u32[]{:S(2)}) collective-permute-start(s16[1216,128]{1,0:T(8,128)(2,1)S(1)} %collect.1.refs_0_), channel_id=1, source_target_pairs={{4,0},{5,1},{6,2},{7,3},{0,4},{1,5},{2,6},{3,7},{12,8},{13,9},{14,... | collective-permute-start | bytes 933896 | tf_op jit(solution)/shard_map/ppermute | solution.py:386
  111.1 3.9 %hold.1.refs_5_ = f32[8,12,40,640]{3,2,1,0:T(8,128)S(1)} custom-call(f32[12,40,640]{2,1,0:T(8,128)} %constant_dynamic-update-slice_fusion.refs_0_, f32[12,40,640]{2,1,0:T(8,128)} %collective-permute-done.9.refs_1_, f32[12,40,640]{2,1,0:T(8,128)} %collective-permute-done.10.refs_2_, f32[12,40,640]{2,1,0:T(8,128)} %collective-permute-done.11.refs_3_, ...), custom_call_target="tpu_custom_call" | custom-call | tf_op jit(solution)/shard_map/hold/pallas_call | solution.py:203
  115.0 2.2 %collective-permute-start.20 = (s16[1216,128]{1,0:T(8,128)(2,1)S(1)}, s16[1216,128]{1,0:T(8,128)(2,1)S(1)}, u32[]{:S(2)}, u32[]{:S(2)}) collective-permute-start(s16[1216,128]{1,0:T(8,128)(2,1)S(1)} %collective-permute-done.16.refs_2_), channel_id=1, source_target_pairs={{0,1},{1,0},{2,3},{3,2},{4,5},{5,4},{6,7},{7,6},{8,9},{9,8},{10,11... | collective-permute-start | bytes 933896 | tf_op jit(solution)/shard_map/ppermute | solution.py:424
  117.3 1.7 %begin.1.refs_6_ = f32[32,40,640]{2,1,0:T(8,128)S(1)} custom-call(bf16[512,144]{1,0:T(8,128)(2,1)S(1)} %copy-done.3, s16[1216,128]{1,0:T(8,128)(2,1)S(1)} %collect.1.refs_0_, s16[1216,128]{1,0:T(8,128)(2,1)S(1)} %collective-permute-done.8.refs_1_, s16[1216,128]{1,0:T(8,128)(2,1)S(1)} %collective-permute-done.16.refs_2_), custom_call_target="tpu_custom_call" | custom-call | tf_op jit(solution)/shard_map/begin/pallas_call | solution.py:249
  119.0 5.5 %collective-permute-done.7.refs_0_ = s16[1216,128]{1,0:T(8,128)(2,1)S(1)} collective-permute-done((s16[1216,128]{1,0:T(8,128)(2,1)S(1)}, s16[1216,128]{1,0:T(8,128)(2,1)S(1)}, u32[]{:S(2)}, u32[]{:S(2)}) %collective-permute-start.7) | collective-permute-done | bytes 311328 | tf_op jit(solution)/shard_map/ppermute | solution.py:386
  125.3 1.2 collective-permute-done.18.refs_2_
  127.0 6.1 %update.1 = (f32[4,40,640]{2,1,0:T(8,128)}, f32[4,40,640]{2,1,0:T(8,128)}, f32[4,40,640]{2,1,0:T(8,128)}, bf16[6,40,640]{2,1,0:T(8,128)(2,1)}) custom-call(bf16[512,240]{1,0:T(8,128)(2,1)S(1)} %copy-done.1, bf16[96,256]{1,0:T(8,128)(2,1)S(1)} %get-tuple-element.33.merge_ref, s16[1216,128]{1,0:T(8,128)(2,1)S(1)} %collective-permute-done.7.refs_0_, ...), custom_call_target="tpu_custom_call" | custom-call | tf_op jit(solution)/shard_map/update/pallas_call | solution.py:307
  (43 shorter events, 4.9 us)
Async XLA Ops:
  11.2 12.2 %copy-start.5 = (f32[1,6,32]{2,0,1:T(1,128)S(1)}, f32[1,6,32]{2,0,1:T(1,128)}, u32[]{:S(2)}) copy-start(f32[1,6,32]{2,0,1:T(1,128)} %param.12) | copy-start | bytes 2308
  11.2 88.8 %all-to-all-start = ((s16[32,416,128]{2,1,0:T(8,128)(2,1)}), s16[32,416,128]{2,1,0:T(8,128)(2,1)S(1)}, u32[]{:S(2)}, u32[]{:S(2)}) async-start(s16[32,416,128]{2,1,0:T(8,128)(2,1)} %products.1), calls=%async_computation | async-start | bytes 6815744 | tf_op jit(solution)/shard_map/all_to_all | solution.py:418
  23.4 6.9 %collective-permute-start.3 = (f32[8,32]{1,0:T(8,128)S(1)}, f32[8,32]{1,0:T(8,128)S(1)}, u32[]{:S(2)}, u32[]{:S(2)}) collective-permute-start(f32[8,32]{1,0:T(8,128)S(1)} %pad.4.refs_0_), channel_id=1, source_target_pairs={{4,0},{5,1},{6,2},{7,3},{0,4},{1,5},{2,6},{3,7},{12,8},{13,9},{14,... | collective-permute-start | bytes 3080 | tf_op jit(solution)/shard_map/ppermute | solution.py:386
  26.9 3.6 %collective-permute-start.2 = (f32[8,32]{1,0:T(8,128)S(1)}, f32[8,32]{1,0:T(8,128)S(1)}, u32[]{:S(2)}, u32[]{:S(2)}) collective-permute-start(f32[8,32]{1,0:T(8,128)S(1)} %pad.4.refs_0_), channel_id=1, source_target_pairs={{2,0},{3,1},{4,2},{5,3},{6,4},{7,5},{0,6},{1,7},{10,8},{11,9},{12,... | collective-permute-start | bytes 3080 | tf_op jit(solution)/shard_map/ppermute | solution.py:386
  27.2 4.5 %collective-permute-start.1 = (f32[8,32]{1,0:T(8,128)S(1)}, f32[8,32]{1,0:T(8,128)S(1)}, u32[]{:S(2)}, u32[]{:S(2)}) collective-permute-start(f32[8,32]{1,0:T(8,128)S(1)} %pad.4.refs_0_), channel_id=1, source_target_pairs={{6,0},{7,1},{0,2},{1,3},{2,4},{3,5},{4,6},{5,7},{14,8},{15,9},{8,1... | collective-permute-start | bytes 3080 | tf_op jit(solution)/shard_map/ppermute | solution.py:386
  28.4 6.8 %collective-permute-start = (f32[8,32]{1,0:T(8,128)S(1)}, f32[8,32]{1,0:T(8,128)S(1)}, u32[]{:S(2)}, u32[]{:S(2)}) collective-permute-start(f32[8,32]{1,0:T(8,128)S(1)} %pad.4.refs_0_), channel_id=1, source_target_pairs={{0,1},{1,0},{2,3},{3,2},{4,5},{5,4},{6,7},{7,6},{8,9},{9,8},{10,11... | collective-permute-start | bytes 3080 | tf_op jit(solution)/shard_map/ppermute | solution.py:405
  30.4 4.8 %collective-permute-start.5 = (f32[8,32]{1,0:T(8,128)S(1)}, f32[8,32]{1,0:T(8,128)S(1)}, u32[]{:S(2)}, u32[]{:S(2)}) collective-permute-start(f32[8,32]{1,0:T(8,128)S(1)} %collective-permute-done.3.refs_4_), channel_id=1, source_target_pairs={{0,1},{1,0},{2,3},{3,2},{4,5},{5,4},{6,7},{7,6},{8,9},{9,8},{10,11... | collective-permute-start | bytes 3080 | tf_op jit(solution)/shard_map/ppermute | solution.py:405
  30.5 4.7 %collective-permute-start.4 = (f32[8,32]{1,0:T(8,128)S(1)}, f32[8,32]{1,0:T(8,128)S(1)}, u32[]{:S(2)}, u32[]{:S(2)}) collective-permute-start(f32[8,32]{1,0:T(8,128)S(1)} %collective-permute-done.2.refs_3_), channel_id=1, source_target_pairs={{0,1},{1,0},{2,3},{3,2},{4,5},{5,4},{6,7},{7,6},{8,9},{9,8},{10,11... | collective-permute-start | bytes 3080 | tf_op jit(solution)/shard_map/ppermute | solution.py:405
  31.7 4.3 %collective-permute-start.6 = (f32[8,32]{1,0:T(8,128)S(1)}, f32[8,32]{1,0:T(8,128)S(1)}, u32[]{:S(2)}, u32[]{:S(2)}) collective-permute-start(f32[8,32]{1,0:T(8,128)S(1)} %collective-permute-done.1.refs_2_), channel_id=1, source_target_pairs={{0,1},{1,0},{2,3},{3,2},{4,5},{5,4},{6,7},{7,6},{8,9},{9,8},{10,11... | collective-permute-start | bytes 3080 | tf_op jit(solution)/shard_map/ppermute | solution.py:405
  42.1 56.1 %collective-permute-start.11 = (f32[12,40,640]{2,1,0:T(8,128)}, f32[12,40,640]{2,1,0:T(8,128)}, u32[]{:S(2)}, u32[]{:S(2)}) collective-permute-start(f32[12,40,640]{2,1,0:T(8,128)} %constant_dynamic-update-slice_fusion.refs_0_), channel_id=1, source_target_pairs={{6,0},{7,1},{0,2},{1,3},{2,4},{3,5},{4,6},{5,7},{14,8},{15,9},{8,1... | collective-permute-start | bytes 3686408 | tf_op jit(solution)/shard_map/ppermute | solution.py:386
  42.1 57.3 %collective-permute-start.10 = (f32[12,40,640]{2,1,0:T(8,128)}, f32[12,40,640]{2,1,0:T(8,128)}, u32[]{:S(2)}, u32[]{:S(2)}) collective-permute-start(f32[12,40,640]{2,1,0:T(8,128)} %constant_dynamic-update-slice_fusion.refs_0_), channel_id=1, source_target_pairs={{4,0},{5,1},{6,2},{7,3},{0,4},{1,5},{2,6},{3,7},{12,8},{13,9},{14,... | collective-permute-start | bytes 3686408 | tf_op jit(solution)/shard_map/ppermute | solution.py:386
  43.4 56.1 %collective-permute-start.9 = (f32[12,40,640]{2,1,0:T(8,128)}, f32[12,40,640]{2,1,0:T(8,128)}, u32[]{:S(2)}, u32[]{:S(2)}) collective-permute-start(f32[12,40,640]{2,1,0:T(8,128)} %constant_dynamic-update-slice_fusion.refs_0_), channel_id=1, source_target_pairs={{2,0},{3,1},{4,2},{5,3},{6,4},{7,5},{0,6},{1,7},{10,8},{11,9},{12,... | collective-permute-start | bytes 3686408 | tf_op jit(solution)/shard_map/ppermute | solution.py:386
  44.8 58.1 %collective-permute-start.12 = (f32[12,40,640]{2,1,0:T(8,128)}, f32[12,40,640]{2,1,0:T(8,128)}, u32[]{:S(2)}, u32[]{:S(2)}) collective-permute-start(f32[12,40,640]{2,1,0:T(8,128)} %constant_dynamic-update-slice_fusion.refs_0_), channel_id=1, source_target_pairs={{0,1},{1,0},{2,3},{3,2},{4,5},{5,4},{6,7},{7,6},{8,9},{9,8},{10,11... | collective-permute-start | bytes 3686408 | tf_op jit(solution)/shard_map/ppermute | solution.py:405
  98.2 8.1 %collective-permute-start.15 = (f32[12,40,640]{2,1,0:T(8,128)}, f32[12,40,640]{2,1,0:T(8,128)}, u32[]{:S(2)}, u32[]{:S(2)}) collective-permute-start(f32[12,40,640]{2,1,0:T(8,128)} %collective-permute-done.11.refs_3_), channel_id=1, source_target_pairs={{0,1},{1,0},{2,3},{3,2},{4,5},{5,4},{6,7},{7,6},{8,9},{9,8},{10,11... | collective-permute-start | bytes 3686408 | tf_op jit(solution)/shard_map/ppermute | solution.py:405
  99.4 11.7 %collective-permute-start.14 = (f32[12,40,640]{2,1,0:T(8,128)}, f32[12,40,640]{2,1,0:T(8,128)}, u32[]{:S(2)}, u32[]{:S(2)}) collective-permute-start(f32[12,40,640]{2,1,0:T(8,128)} %collective-permute-done.10.refs_2_), channel_id=1, source_target_pairs={{0,1},{1,0},{2,3},{3,2},{4,5},{5,4},{6,7},{7,6},{8,9},{9,8},{10,11... | collective-permute-start | bytes 3686408 | tf_op jit(solution)/shard_map/ppermute | solution.py:405
  99.4 11.7 %collective-permute-start.13 = (f32[12,40,640]{2,1,0:T(8,128)}, f32[12,40,640]{2,1,0:T(8,128)}, u32[]{:S(2)}, u32[]{:S(2)}) collective-permute-start(f32[12,40,640]{2,1,0:T(8,128)} %collective-permute-done.9.refs_1_), channel_id=1, source_target_pairs={{0,1},{1,0},{2,3},{3,2},{4,5},{5,4},{6,7},{7,6},{8,9},{9,8},{10,11... | collective-permute-start | bytes 3686408 | tf_op jit(solution)/shard_map/ppermute | solution.py:405
  102.6 14.7 %copy-start.3 = (bf16[512,144]{1,0:T(8,128)(2,1)S(1)}, bf16[512,144]{1,0:T(8,128)(2,1)}, u32[]{:S(2)}) copy-start(bf16[512,144]{1,0:T(8,128)(2,1)} %copy-done.2) | copy-start | bytes 442372
  102.6 12.4 %collective-permute-start.16 = (s16[1216,128]{1,0:T(8,128)(2,1)S(1)}, s16[1216,128]{1,0:T(8,128)(2,1)S(1)}, u32[]{:S(2)}, u32[]{:S(2)}) collective-permute-start(s16[1216,128]{1,0:T(8,128)(2,1)S(1)} %collect.1.refs_0_), channel_id=1, source_target_pairs={{6,0},{7,1},{0,2},{1,3},{2,4},{3,5},{4,6},{5,7},{14,8},{15,9},{8,1... | collective-permute-start | bytes 933896 | tf_op jit(solution)/shard_map/ppermute | solution.py:386
  102.9 14.4 %collective-permute-start.8 = (s16[1216,128]{1,0:T(8,128)(2,1)S(1)}, s16[1216,128]{1,0:T(8,128)(2,1)S(1)}, u32[]{:S(2)}, u32[]{:S(2)}) collective-permute-start(s16[1216,128]{1,0:T(8,128)(2,1)S(1)} %collect.1.refs_0_), channel_id=1, source_target_pairs={{0,1},{1,0},{2,3},{3,2},{4,5},{5,4},{6,7},{7,6},{8,9},{9,8},{10,11... | collective-permute-start | bytes 933896 | tf_op jit(solution)/shard_map/ppermute | solution.py:422
  106.4 12.6 %collective-permute-start.17 = (s16[1216,128]{1,0:T(8,128)(2,1)S(1)}, s16[1216,128]{1,0:T(8,128)(2,1)S(1)}, u32[]{:S(2)}, u32[]{:S(2)}) collective-permute-start(s16[1216,128]{1,0:T(8,128)(2,1)S(1)} %collect.1.refs_0_), channel_id=1, source_target_pairs={{4,0},{5,1},{6,2},{7,3},{0,4},{1,5},{2,6},{3,7},{12,8},{13,9},{14,... | collective-permute-start | bytes 933896 | tf_op jit(solution)/shard_map/ppermute | solution.py:386
  111.1 13.4 %collective-permute-start.7 = (s16[1216,128]{1,0:T(8,128)(2,1)S(1)}, s16[1216,128]{1,0:T(8,128)(2,1)S(1)}, u32[]{:S(2)}, u32[]{:S(2)}) collective-permute-start(s16[1216,128]{1,0:T(8,128)(2,1)S(1)} %collect.1.refs_0_), channel_id=1, source_target_pairs={{2,0},{3,1},{4,2},{5,3},{6,4},{7,5},{0,6},{1,7},{10,8},{11,9},{12,... | collective-permute-start | bytes 933896 | tf_op jit(solution)/shard_map/ppermute | solution.py:386
  115.0 10.3 %collective-permute-start.20 = (s16[1216,128]{1,0:T(8,128)(2,1)S(1)}, s16[1216,128]{1,0:T(8,128)(2,1)S(1)}, u32[]{:S(2)}, u32[]{:S(2)}) collective-permute-start(s16[1216,128]{1,0:T(8,128)(2,1)S(1)} %collective-permute-done.16.refs_2_), channel_id=1, source_target_pairs={{0,1},{1,0},{2,3},{3,2},{4,5},{5,4},{6,7},{7,6},{8,9},{9,8},{10,11... | collective-permute-start | bytes 933896 | tf_op jit(solution)/shard_map/ppermute | solution.py:424
  124.5 2.1 %collective-permute-start.18 = (s16[1216,128]{1,0:T(8,128)(2,1)S(1)}, s16[1216,128]{1,0:T(8,128)(2,1)S(1)}, u32[]{:S(2)}, u32[]{:S(2)}) collective-permute-start(s16[1216,128]{1,0:T(8,128)(2,1)S(1)} %collective-permute-done.7.refs_0_), channel_id=1, source_target_pairs={{0,1},{1,0},{2,3},{3,2},{4,5},{5,4},{6,7},{7,6},{8,9},{9,8},{10,11... | collective-permute-start | bytes 933896 | tf_op jit(solution)/shard_map/ppermute | solution.py:428
  125.3 1.7 %collective-permute-start.19 = (s16[1216,128]{1,0:T(8,128)(2,1)S(1)}, s16[1216,128]{1,0:T(8,128)(2,1)S(1)}, u32[]{:S(2)}, u32[]{:S(2)}) collective-permute-start(s16[1216,128]{1,0:T(8,128)(2,1)S(1)} %collective-permute-done.17.refs_1_), channel_id=1, source_target_pairs={{0,1},{1,0},{2,3},{3,2},{4,5},{5,4},{6,7},{7,6},{8,9},{9,8},{10,11... | collective-permute-start | bytes 933896 | tf_op jit(solution)/shard_map/ppermute | solution.py:428
  (4 other events, 23.4 us)

commit v7 on v6

--- a/solution.py
+++ b/solution.py
@@ -423,7 +423,6 @@
     states, last = lax.optimization_barrier((hold(states), near[chips - 1]))
     swapped[chips - 1] = lax.ppermute(last, "rep", swap)
     begun = begin(first_mix, [sums, swapped[0], last], nsys, *weights.shape[1:])
-    begun, near[chips - 2] = lax.optimization_barrier((begun, near[chips - 2]))
     for k in range(chips - 2, 0, -1):
         swapped[k] = lax.ppermute(near[k], "rep", swap)
     sums = near + swapped

time: 135 us -> 133 us (0.985)
  the two profiles are of different devices: /device:TPU:1 before, /device:TPU:25 now
where the time goes in v7:
time: 133 us; the launch traced here: 132 us
  waiting for transfers between devices  59.6 us (45%)
  starting transfers between devices  41.2 us (31%)
  Pallas kernels  24 us (18%)
  local copies, waits for them, and re-layouts  5.23 us (4%)
  between operations  1.6 us (1%)
    ppermute x9, waiting for transfers between devices, everywhere(): return [lax.ppermute(value, axis, pairs) for pairs in moves]  54.5 us
    all_to_all x1, starting transfers between devices, on_device(): received = lax.all_to_all(parts, 'run', 0, 0, tiled=True)  12.9 us
    ppermute x9, starting transfers between devices, everywhere(): return [lax.ppermute(value, axis, pairs) for pairs in moves]  11.5 us
    pallas_call x1, Pallas kernels, products(): pl.pallas_call(product_kernel, grid=(rows // block,), in_specs=[pl.BlockS...  8.75 us
    ppermute x8, starting transfers between devices, all_reps(): return near + [lax.ppermute(part, 'rep', swap) for part in near]  7.98 us
    ppermute x1, starting transfers between devices, on_device(): swapped[chips - 1] = lax.ppermute(last, 'rep', swap)  6.92 us
    pallas_call x1, Pallas kernels, update(): pl.pallas_call(update_kernel, grid=(rows // group,), in_specs=[pl.BlockSp...  6.17 us
    unnamed x15, local copies, waits for them, and re-layouts  4.43 us
  transfers between devices with their start and end apart: 22, of which 4 were waited for; matrix products, arithmetic and copies ran while one was open for 3% of the time, Pallas kernels for 7%

profile of v7, /device:TPU:25, one launch (start us, length us, event | category | flops | bytes accessed | tf_op | source)
XLA Modules:
  0.0 131.6 jit_solution(10135965419170901825)
XLA Ops:
  1.3 8.7 %products.1 = s16[32,416,128]{2,1,0:T(8,128)(2,1)} custom-call(s32[1,1]{1,0:T(1,128)S(6)} %copy.17.count_ref, s32[1,2048]{1,0:T(1,128)} %system_ref.1, bf16[2048,1280]{1,0:T(8,128)(2,1)} %bitcast.8, bf16[2048,640]{1,0:T(8,128)(2,1)} %bitcast.9), custom_call_target="tpu_custom_call" | custom-call | flops 3355443200 | bytes 11141120 | tf_op jit(solution)/shard_map/products/pallas_call | solution.py:111
  10.0 12.9 %all-to-all-start = ((s16[32,416,128]{2,1,0:T(8,128)(2,1)}), s16[32,416,128]{2,1,0:T(8,128)(2,1)S(1)}, u32[]{:S(2)}, u32[]{:S(2)}) async-start(s16[32,416,128]{2,1,0:T(8,128)(2,1)} %products.1), calls=%async_computation | async-start | bytes 6815744 | tf_op jit(solution)/shard_map/all_to_all | solution.py:418
  23.0 3.7 %collective-permute-start.3 = (f32[8,32]{1,0:T(8,128)S(1)}, f32[8,32]{1,0:T(8,128)S(1)}, u32[]{:S(2)}, u32[]{:S(2)}) collective-permute-start(f32[8,32]{1,0:T(8,128)S(1)} %pad.4.refs_0_), channel_id=1, source_target_pairs={{4,0},{5,1},{6,2},{7,3},{0,4},{1,5},{2,6},{3,7},{12,8},{13,9},{14,... | collective-permute-start | bytes 3080 | tf_op jit(solution)/shard_map/ppermute | solution.py:386
  26.7 1.5 %collective-permute-start.1 = (f32[8,32]{1,0:T(8,128)S(1)}, f32[8,32]{1,0:T(8,128)S(1)}, u32[]{:S(2)}, u32[]{:S(2)}) collective-permute-start(f32[8,32]{1,0:T(8,128)S(1)} %pad.4.refs_0_), channel_id=1, source_target_pairs={{6,0},{7,1},{0,2},{1,3},{2,4},{3,5},{4,6},{5,7},{14,8},{15,9},{8,1... | collective-permute-start | bytes 3080 | tf_op jit(solution)/shard_map/ppermute | solution.py:386
  28.1 2.3 %collective-permute-start = (f32[8,32]{1,0:T(8,128)S(1)}, f32[8,32]{1,0:T(8,128)S(1)}, u32[]{:S(2)}, u32[]{:S(2)}) collective-permute-start(f32[8,32]{1,0:T(8,128)S(1)} %pad.4.refs_0_), channel_id=1, source_target_pairs={{0,1},{1,0},{2,3},{3,2},{4,5},{5,4},{6,7},{7,6},{8,9},{9,8},{10,11... | collective-permute-start | bytes 3080 | tf_op jit(solution)/shard_map/ppermute | solution.py:405
  30.4 1.6 %collective-permute-start.4 = (f32[8,32]{1,0:T(8,128)S(1)}, f32[8,32]{1,0:T(8,128)S(1)}, u32[]{:S(2)}, u32[]{:S(2)}) collective-permute-start(f32[8,32]{1,0:T(8,128)S(1)} %collective-permute-done.2.refs_3_), channel_id=1, source_target_pairs={{0,1},{1,0},{2,3},{3,2},{4,5},{5,4},{6,7},{7,6},{8,9},{9,8},{10,11... | collective-permute-start | bytes 3080 | tf_op jit(solution)/shard_map/ppermute | solution.py:405
  32.0 1.5 %collective-permute-start.6 = (f32[8,32]{1,0:T(8,128)S(1)}, f32[8,32]{1,0:T(8,128)S(1)}, u32[]{:S(2)}, u32[]{:S(2)}) collective-permute-start(f32[8,32]{1,0:T(8,128)S(1)} %collective-permute-done.1.refs_2_), channel_id=1, source_target_pairs={{0,1},{1,0},{2,3},{3,2},{4,5},{5,4},{6,7},{7,6},{8,9},{9,8},{10,11... | collective-permute-start | bytes 3080 | tf_op jit(solution)/shard_map/ppermute | solution.py:405
  35.9 1.9 %constant_dynamic-update-slice_fusion.2 = f32[12,40,640]{2,1,0:T(8,128)} fusion(f32[4,40,640]{2,1,0:T(8,128)} %param.13), kind=kLoop, calls=%fused_computation.2 | loop fusion | bytes 819200
  37.8 1.8 %constant_dynamic-update-slice_fusion.1 = f32[12,40,640]{2,1,0:T(8,128)} fusion(f32[12,40,640]{2,1,0:T(8,128)} %constant_dynamic-update-slice_fusion.2, f32[4,40,640]{2,1,0:T(8,128)} %param.14), kind=kLoop, calls=%fused_computation.1 | loop fusion | bytes 819200
  40.7 1.0 collective-permute-start.12
  41.6 1.4 %collective-permute-start.11 = (f32[12,40,640]{2,1,0:T(8,128)}, f32[12,40,640]{2,1,0:T(8,128)}, u32[]{:S(2)}, u32[]{:S(2)}) collective-permute-start(f32[12,40,640]{2,1,0:T(8,128)} %constant_dynamic-update-slice_fusion.refs_0_), channel_id=1, source_target_pairs={{2,0},{3,1},{4,2},{5,3},{6,4},{7,5},{0,6},{1,7},{10,8},{11,9},{12,... | collective-permute-start | bytes 3686408 | tf_op jit(solution)/shard_map/ppermute | solution.py:386
  43.1 0.9 collective-permute-start.14
  44.0 52.5 %collective-permute-done.13.refs_3_ = f32[12,40,640]{2,1,0:T(8,128)} collective-permute-done((f32[12,40,640]{2,1,0:T(8,128)}, f32[12,40,640]{2,1,0:T(8,128)}, u32[]{:S(2)}, u32[]{:S(2)}) %collective-permute-start.13) | collective-permute-done | bytes 1228832 | tf_op jit(solution)/shard_map/ppermute | solution.py:386
  96.5 1.2 collective-permute-start.17
  98.3 4.3 %all-to-all-done.parts_ref = s16[32,416,128]{2,1,0:T(8,128)(2,1)S(1)} async-done(((s16[32,416,128]{2,1,0:T(8,128)(2,1)}), s16[32,416,128]{2,1,0:T(8,128)(2,1)S(1)}, u32[]{:S(2)}, u32[]{:S(2)}) %all-to-all-start) | async-done | bytes 3407904 | tf_op jit(solution)/shard_map/all_to_all | solution.py:418
  102.6 2.6 %collect.1.refs_0_ = s16[1216,128]{1,0:T(8,128)(2,1)S(1)} custom-call(s16[32,416,128]{2,1,0:T(8,128)(2,1)S(1)} %all-to-all-done.parts_ref), custom_call_target="tpu_custom_call" | custom-call | flops 3407872 | bytes 3407872 | tf_op jit(solution)/shard_map/collect/pallas_call | solution.py:175
  105.3 1.7 %collective-permute-start.8 = (s16[1216,128]{1,0:T(8,128)(2,1)S(1)}, s16[1216,128]{1,0:T(8,128)(2,1)S(1)}, u32[]{:S(2)}, u32[]{:S(2)}) collective-permute-start(s16[1216,128]{1,0:T(8,128)(2,1)S(1)} %collect.1.refs_0_), channel_id=1, source_target_pairs={{4,0},{5,1},{6,2},{7,3},{0,4},{1,5},{2,6},{3,7},{12,8},{13,9},{14,... | collective-permute-start | bytes 933896 | tf_op jit(solution)/shard_map/ppermute | solution.py:386
  107.0 1.9 %collective-permute-start.7 = (s16[1216,128]{1,0:T(8,128)(2,1)S(1)}, s16[1216,128]{1,0:T(8,128)(2,1)S(1)}, u32[]{:S(2)}, u32[]{:S(2)}) collective-permute-start(s16[1216,128]{1,0:T(8,128)(2,1)S(1)} %collect.1.refs_0_), channel_id=1, source_target_pairs={{2,0},{3,1},{4,2},{5,3},{6,4},{7,5},{0,6},{1,7},{10,8},{11,9},{12,... | collective-permute-start | bytes 933896 | tf_op jit(solution)/shard_map/ppermute | solution.py:386
  108.9 1.3 collective-permute-start.20
  110.2 3.9 %hold.1.refs_5_ = f32[8,12,40,640]{3,2,1,0:T(8,128)S(1)} custom-call(f32[12,40,640]{2,1,0:T(8,128)} %constant_dynamic-update-slice_fusion.refs_0_, f32[12,40,640]{2,1,0:T(8,128)} %collective-permute-done.11.refs_1_, f32[12,40,640]{2,1,0:T(8,128)} %collective-permute-done.12.refs_2_, f32[12,40,640]{2,1,0:T(8,128)} %collective-permute-done.13.refs_3_, ...), custom_call_target="tpu_custom_call" | custom-call | tf_op jit(solution)/shard_map/hold/pallas_call | solution.py:203
  114.1 1.9 %collective-permute-done.18.refs_2_ = s16[1216,128]{1,0:T(8,128)(2,1)S(1)} collective-permute-done((s16[1216,128]{1,0:T(8,128)(2,1)S(1)}, s16[1216,128]{1,0:T(8,128)(2,1)S(1)}, u32[]{:S(2)}, u32[]{:S(2)}) %collective-permute-start.18) | collective-permute-done | bytes 311328 | tf_op jit(solution)/shard_map/ppermute | solution.py:386
  116.0 6.9 %collective-permute-start.19 = (s16[1216,128]{1,0:T(8,128)(2,1)S(1)}, s16[1216,128]{1,0:T(8,128)(2,1)S(1)}, u32[]{:S(2)}, u32[]{:S(2)}) collective-permute-start(s16[1216,128]{1,0:T(8,128)(2,1)S(1)} %collective-permute-done.18.refs_2_), channel_id=1, source_target_pairs={{0,1},{1,0},{2,3},{3,2},{4,5},{5,4},{6,7},{7,6},{8,9},{9,8},{10,11... | collective-permute-start | bytes 933896 | tf_op jit(solution)/shard_map/ppermute | solution.py:424
  123.6 1.7 %begin.1.refs_6_ = f32[32,40,640]{2,1,0:T(8,128)S(1)} custom-call(bf16[512,144]{1,0:T(8,128)(2,1)S(1)} %copy-done.3, s16[1216,128]{1,0:T(8,128)(2,1)S(1)} %collect.1.refs_0_, s16[1216,128]{1,0:T(8,128)(2,1)S(1)} %collective-permute-done.20.refs_1_, s16[1216,128]{1,0:T(8,128)(2,1)S(1)} %collective-permute-done.18.refs_2_), custom_call_target="tpu_custom_call" | custom-call | tf_op jit(solution)/shard_map/begin/pallas_call | solution.py:249
  125.3 6.2 %update.1 = (f32[4,40,640]{2,1,0:T(8,128)}, f32[4,40,640]{2,1,0:T(8,128)}, f32[4,40,640]{2,1,0:T(8,128)}, bf16[6,40,640]{2,1,0:T(8,128)(2,1)}) custom-call(bf16[512,240]{1,0:T(8,128)(2,1)S(1)} %copy-done.1, bf16[96,256]{1,0:T(8,128)(2,1)S(1)} %get-tuple-element.31.merge_ref, s16[1216,128]{1,0:T(8,128)(2,1)S(1)} %collective-permute-done.7.refs_0_, ...), custom_call_target="tpu_custom_call" | custom-call | tf_op jit(solution)/shard_map/update/pallas_call | solution.py:307
  (43 shorter events, 4.9 us)
Async XLA Ops:
  10.0 12.9 %copy-start.5 = (f32[1,6,32]{2,0,1:T(1,128)S(1)}, f32[1,6,32]{2,0,1:T(1,128)}, u32[]{:S(2)}) copy-start(f32[1,6,32]{2,0,1:T(1,128)} %param.12) | copy-start | bytes 2308
  10.0 92.5 %all-to-all-start = ((s16[32,416,128]{2,1,0:T(8,128)(2,1)}), s16[32,416,128]{2,1,0:T(8,128)(2,1)S(1)}, u32[]{:S(2)}, u32[]{:S(2)}) async-start(s16[32,416,128]{2,1,0:T(8,128)(2,1)} %products.1), calls=%async_computation | async-start | bytes 6815744 | tf_op jit(solution)/shard_map/all_to_all | solution.py:418
  23.0 7.4 %collective-permute-start.3 = (f32[8,32]{1,0:T(8,128)S(1)}, f32[8,32]{1,0:T(8,128)S(1)}, u32[]{:S(2)}, u32[]{:S(2)}) collective-permute-start(f32[8,32]{1,0:T(8,128)S(1)} %pad.4.refs_0_), channel_id=1, source_target_pairs={{4,0},{5,1},{6,2},{7,3},{0,4},{1,5},{2,6},{3,7},{12,8},{13,9},{14,... | collective-permute-start | bytes 3080 | tf_op jit(solution)/shard_map/ppermute | solution.py:386
  26.7 3.7 %collective-permute-start.2 = (f32[8,32]{1,0:T(8,128)S(1)}, f32[8,32]{1,0:T(8,128)S(1)}, u32[]{:S(2)}, u32[]{:S(2)}) collective-permute-start(f32[8,32]{1,0:T(8,128)S(1)} %pad.4.refs_0_), channel_id=1, source_target_pairs={{2,0},{3,1},{4,2},{5,3},{6,4},{7,5},{0,6},{1,7},{10,8},{11,9},{12,... | collective-permute-start | bytes 3080 | tf_op jit(solution)/shard_map/ppermute | solution.py:386
  26.7 5.3 %collective-permute-start.1 = (f32[8,32]{1,0:T(8,128)S(1)}, f32[8,32]{1,0:T(8,128)S(1)}, u32[]{:S(2)}, u32[]{:S(2)}) collective-permute-start(f32[8,32]{1,0:T(8,128)S(1)} %pad.4.refs_0_), channel_id=1, source_target_pairs={{6,0},{7,1},{0,2},{1,3},{2,4},{3,5},{4,6},{5,7},{14,8},{15,9},{8,1... | collective-permute-start | bytes 3080 | tf_op jit(solution)/shard_map/ppermute | solution.py:386
  28.1 5.3 %collective-permute-start = (f32[8,32]{1,0:T(8,128)S(1)}, f32[8,32]{1,0:T(8,128)S(1)}, u32[]{:S(2)}, u32[]{:S(2)}) collective-permute-start(f32[8,32]{1,0:T(8,128)S(1)} %pad.4.refs_0_), channel_id=1, source_target_pairs={{0,1},{1,0},{2,3},{3,2},{4,5},{5,4},{6,7},{7,6},{8,9},{9,8},{10,11... | collective-permute-start | bytes 3080 | tf_op jit(solution)/shard_map/ppermute | solution.py:405
  30.4 3.0 %collective-permute-start.5 = (f32[8,32]{1,0:T(8,128)S(1)}, f32[8,32]{1,0:T(8,128)S(1)}, u32[]{:S(2)}, u32[]{:S(2)}) collective-permute-start(f32[8,32]{1,0:T(8,128)S(1)} %collective-permute-done.3.refs_4_), channel_id=1, source_target_pairs={{0,1},{1,0},{2,3},{3,2},{4,5},{5,4},{6,7},{7,6},{8,9},{9,8},{10,11... | collective-permute-start | bytes 3080 | tf_op jit(solution)/shard_map/ppermute | solution.py:405
  30.4 3.0 %collective-permute-start.4 = (f32[8,32]{1,0:T(8,128)S(1)}, f32[8,32]{1,0:T(8,128)S(1)}, u32[]{:S(2)}, u32[]{:S(2)}) collective-permute-start(f32[8,32]{1,0:T(8,128)S(1)} %collective-permute-done.2.refs_3_), channel_id=1, source_target_pairs={{0,1},{1,0},{2,3},{3,2},{4,5},{5,4},{6,7},{7,6},{8,9},{9,8},{10,11... | collective-permute-start | bytes 3080 | tf_op jit(solution)/shard_map/ppermute | solution.py:405
  32.0 2.3 %collective-permute-start.6 = (f32[8,32]{1,0:T(8,128)S(1)}, f32[8,32]{1,0:T(8,128)S(1)}, u32[]{:S(2)}, u32[]{:S(2)}) collective-permute-start(f32[8,32]{1,0:T(8,128)S(1)} %collective-permute-done.1.refs_2_), channel_id=1, source_target_pairs={{0,1},{1,0},{2,3},{3,2},{4,5},{5,4},{6,7},{7,6},{8,9},{9,8},{10,11... | collective-permute-start | bytes 3080 | tf_op jit(solution)/shard_map/ppermute | solution.py:405
  40.4 56.1 %collective-permute-start.13 = (f32[12,40,640]{2,1,0:T(8,128)}, f32[12,40,640]{2,1,0:T(8,128)}, u32[]{:S(2)}, u32[]{:S(2)}) collective-permute-start(f32[12,40,640]{2,1,0:T(8,128)} %constant_dynamic-update-slice_fusion.refs_0_), channel_id=1, source_target_pairs={{6,0},{7,1},{0,2},{1,3},{2,4},{3,5},{4,6},{5,7},{14,8},{15,9},{8,1... | collective-permute-start | bytes 3686408 | tf_op jit(solution)/shard_map/ppermute | solution.py:386
  40.7 57.0 %collective-permute-start.12 = (f32[12,40,640]{2,1,0:T(8,128)}, f32[12,40,640]{2,1,0:T(8,128)}, u32[]{:S(2)}, u32[]{:S(2)}) collective-permute-start(f32[12,40,640]{2,1,0:T(8,128)} %constant_dynamic-update-slice_fusion.refs_0_), channel_id=1, source_target_pairs={{4,0},{5,1},{6,2},{7,3},{0,4},{1,5},{2,6},{3,7},{12,8},{13,9},{14,... | collective-permute-start | bytes 3686408 | tf_op jit(solution)/shard_map/ppermute | solution.py:386
  41.6 56.1 %collective-permute-start.11 = (f32[12,40,640]{2,1,0:T(8,128)}, f32[12,40,640]{2,1,0:T(8,128)}, u32[]{:S(2)}, u32[]{:S(2)}) collective-permute-start(f32[12,40,640]{2,1,0:T(8,128)} %constant_dynamic-update-slice_fusion.refs_0_), channel_id=1, source_target_pairs={{2,0},{3,1},{4,2},{5,3},{6,4},{7,5},{0,6},{1,7},{10,8},{11,9},{12,... | collective-permute-start | bytes 3686408 | tf_op jit(solution)/shard_map/ppermute | solution.py:386
  43.1 62.2 %collective-permute-start.14 = (f32[12,40,640]{2,1,0:T(8,128)}, f32[12,40,640]{2,1,0:T(8,128)}, u32[]{:S(2)}, u32[]{:S(2)}) collective-permute-start(f32[12,40,640]{2,1,0:T(8,128)} %constant_dynamic-update-slice_fusion.refs_0_), channel_id=1, source_target_pairs={{0,1},{1,0},{2,3},{3,2},{4,5},{5,4},{6,7},{7,6},{8,9},{9,8},{10,11... | collective-permute-start | bytes 3686408 | tf_op jit(solution)/shard_map/ppermute | solution.py:405
  96.5 10.5 %collective-permute-start.17 = (f32[12,40,640]{2,1,0:T(8,128)}, f32[12,40,640]{2,1,0:T(8,128)}, u32[]{:S(2)}, u32[]{:S(2)}) collective-permute-start(f32[12,40,640]{2,1,0:T(8,128)} %collective-permute-done.13.refs_3_), channel_id=1, source_target_pairs={{0,1},{1,0},{2,3},{3,2},{4,5},{5,4},{6,7},{7,6},{8,9},{9,8},{10,11... | collective-permute-start | bytes 3686408 | tf_op jit(solution)/shard_map/ppermute | solution.py:405
  97.7 11.2 %collective-permute-start.16 = (f32[12,40,640]{2,1,0:T(8,128)}, f32[12,40,640]{2,1,0:T(8,128)}, u32[]{:S(2)}, u32[]{:S(2)}) collective-permute-start(f32[12,40,640]{2,1,0:T(8,128)} %collective-permute-done.12.refs_2_), channel_id=1, source_target_pairs={{0,1},{1,0},{2,3},{3,2},{4,5},{5,4},{6,7},{7,6},{8,9},{9,8},{10,11... | collective-permute-start | bytes 3686408 | tf_op jit(solution)/shard_map/ppermute | solution.py:405
  97.7 12.5 %collective-permute-start.15 = (f32[12,40,640]{2,1,0:T(8,128)}, f32[12,40,640]{2,1,0:T(8,128)}, u32[]{:S(2)}, u32[]{:S(2)}) collective-permute-start(f32[12,40,640]{2,1,0:T(8,128)} %collective-permute-done.11.refs_1_), channel_id=1, source_target_pairs={{0,1},{1,0},{2,3},{3,2},{4,5},{5,4},{6,7},{7,6},{8,9},{9,8},{10,11... | collective-permute-start | bytes 3686408 | tf_op jit(solution)/shard_map/ppermute | solution.py:405
  105.2 18.4 %copy-start.3 = (bf16[512,144]{1,0:T(8,128)(2,1)S(1)}, bf16[512,144]{1,0:T(8,128)(2,1)}, u32[]{:S(2)}) copy-start(bf16[512,144]{1,0:T(8,128)(2,1)} %copy-done.2) | copy-start | bytes 442372
  105.2 10.8 %collective-permute-start.18 = (s16[1216,128]{1,0:T(8,128)(2,1)S(1)}, s16[1216,128]{1,0:T(8,128)(2,1)S(1)}, u32[]{:S(2)}, u32[]{:S(2)}) collective-permute-start(s16[1216,128]{1,0:T(8,128)(2,1)S(1)} %collect.1.refs_0_), channel_id=1, source_target_pairs={{6,0},{7,1},{0,2},{1,3},{2,4},{3,5},{4,6},{5,7},{14,8},{15,9},{8,1... | collective-permute-start | bytes 933896 | tf_op jit(solution)/shard_map/ppermute | solution.py:386
  105.3 17.6 %collective-permute-start.8 = (s16[1216,128]{1,0:T(8,128)(2,1)S(1)}, s16[1216,128]{1,0:T(8,128)(2,1)S(1)}, u32[]{:S(2)}, u32[]{:S(2)}) collective-permute-start(s16[1216,128]{1,0:T(8,128)(2,1)S(1)} %collect.1.refs_0_), channel_id=1, source_target_pairs={{4,0},{5,1},{6,2},{7,3},{0,4},{1,5},{2,6},{3,7},{12,8},{13,9},{14,... | collective-permute-start | bytes 933896 | tf_op jit(solution)/shard_map/ppermute | solution.py:386
  107.0 15.9 %collective-permute-start.7 = (s16[1216,128]{1,0:T(8,128)(2,1)S(1)}, s16[1216,128]{1,0:T(8,128)(2,1)S(1)}, u32[]{:S(2)}, u32[]{:S(2)}) collective-permute-start(s16[1216,128]{1,0:T(8,128)(2,1)S(1)} %collect.1.refs_0_), channel_id=1, source_target_pairs={{2,0},{3,1},{4,2},{5,3},{6,4},{7,5},{0,6},{1,7},{10,8},{11,9},{12,... | collective-permute-start | bytes 933896 | tf_op jit(solution)/shard_map/ppermute | solution.py:386
  108.9 14.7 %collective-permute-start.20 = (s16[1216,128]{1,0:T(8,128)(2,1)S(1)}, s16[1216,128]{1,0:T(8,128)(2,1)S(1)}, u32[]{:S(2)}, u32[]{:S(2)}) collective-permute-start(s16[1216,128]{1,0:T(8,128)(2,1)S(1)} %collect.1.refs_0_), channel_id=1, source_target_pairs={{0,1},{1,0},{2,3},{3,2},{4,5},{5,4},{6,7},{7,6},{8,9},{9,8},{10,11... | collective-permute-start | bytes 933896 | tf_op jit(solution)/shard_map/ppermute | solution.py:422
  116.0 9.3 %collective-permute-start.19 = (s16[1216,128]{1,0:T(8,128)(2,1)S(1)}, s16[1216,128]{1,0:T(8,128)(2,1)S(1)}, u32[]{:S(2)}, u32[]{:S(2)}) collective-permute-start(s16[1216,128]{1,0:T(8,128)(2,1)S(1)} %collective-permute-done.18.refs_2_), channel_id=1, source_target_pairs={{0,1},{1,0},{2,3},{3,2},{4,5},{5,4},{6,7},{7,6},{8,9},{9,8},{10,11... | collective-permute-start | bytes 933896 | tf_op jit(solution)/shard_map/ppermute | solution.py:424
  122.9 2.3 %collective-permute-start.10 = (s16[1216,128]{1,0:T(8,128)(2,1)S(1)}, s16[1216,128]{1,0:T(8,128)(2,1)S(1)}, u32[]{:S(2)}, u32[]{:S(2)}) collective-permute-start(s16[1216,128]{1,0:T(8,128)(2,1)S(1)} %collective-permute-done.8.refs_1_), channel_id=1, source_target_pairs={{0,1},{1,0},{2,3},{3,2},{4,5},{5,4},{6,7},{7,6},{8,9},{9,8},{10,11... | collective-permute-start | bytes 933896 | tf_op jit(solution)/shard_map/ppermute | solution.py:427
  122.9 2.3 %collective-permute-start.9 = (s16[1216,128]{1,0:T(8,128)(2,1)S(1)}, s16[1216,128]{1,0:T(8,128)(2,1)S(1)}, u32[]{:S(2)}, u32[]{:S(2)}) collective-permute-start(s16[1216,128]{1,0:T(8,128)(2,1)S(1)} %collective-permute-done.7.refs_0_), channel_id=1, source_target_pairs={{0,1},{1,0},{2,3},{3,2},{4,5},{5,4},{6,7},{7,6},{8,9},{9,8},{10,11... | collective-permute-start | bytes 933896 | tf_op jit(solution)/shard_map/ppermute | solution.py:427
  (4 other events, 22.6 us)
